TPU v7x, 32 devices: a whole 2x2x4 slice. The times are simulated.
32 devices in a mesh: dp: 8 (over z, x), tensor: 4 (over y, core).
Axes of the slice: x: 2, y: 2, z: 4, core: 2. Of those that a mesh axis runs over, the one named last changes fastest.
Arguments:
- tokens: bfloat16 [2, 8192, 768], P(None, ('dp', 'tensor')), may hold values from -6 to 6
- cotangent: bfloat16 [2, 8192, 768], P(None, ('dp', 'tensor')), may hold values from -6 to 6
- segment_ids: int32 [2, 16, 512], P(None, 'dp'), may hold values from 0 to 3, never falling along the last dimension, each value on 1 to 256 neighbouring positions
- qkv_weight: bfloat16 [2, 3, 768, 768], P(None, None, 'dp', 'tensor'), may hold values from -0.21875 to 0.21875
- out_weight: bfloat16 [2, 768, 768], P(None, 'tensor', 'dp'), may hold values from -0.875 to 0.875
- in_weight: bfloat16 [2, 768, 3072], P(None, 'dp', 'tensor'), may hold values from -0.21875 to 0.21875
- down_weight: bfloat16 [2, 3072, 768], P(None, 'tensor', 'dp'), may hold values from -0.109375 to 0.109375
- qv_bias: bfloat16 [2, 2, 12, 64], P(None, None, 'tensor', 'dp'), may hold values from -3 to 3
- in_bias: bfloat16 [2, 48, 64], P(None, 'tensor', 'dp'), may hold values from -3 to 3
- row_bias: bfloat16 [2, 2, 768], P(None, None, 'dp'), may hold values from -3 to 3
- norm_gain: bfloat16 [2, 2, 768], P(None, None, 'dp'), may hold values from 0.5 to 1.5
- norm_shift: bfloat16 [2, 2, 768], P(None, None, 'dp'), may hold values from -3 to 3
Outputs:
- output: float32 [2, 8192, 768], P(None, ('dp', 'tensor'))
- grad_tokens: float32 [2, 8192, 768], P(None, ('dp', 'tensor'))
- grad_qkv_weight: float32 [2, 3, 768, 768], P(None, None, 'dp', 'tensor')
- grad_out_weight: float32 [2, 768, 768], P(None, 'tensor', 'dp')
- grad_in_weight: float32 [2, 768, 3072], P(None, 'dp', 'tensor')
- grad_down_weight: float32 [2, 3072, 768], P(None, 'tensor', 'dp')
- grad_qv_bias: float32 [2, 2, 12, 64], P(None, None, 'tensor', 'dp')
- grad_in_bias: float32 [2, 48, 64], P(None, 'tensor', 'dp')
- grad_row_bias: float32 [2, 2, 768], P(None, None, 'dp')
- grad_norm_gain: float32 [2, 2, 768], P(None, None, 'dp')
- grad_norm_shift: float32 [2, 2, 768], P(None, None, 'dp')
Inputs may be any that keep to these rules, and one draw needn't show every extreme that they name: `segment_ids`: within a packed row the ids never fall; a run of equal ids is one document of at most 256 tokens, and tokens attend only within their document.
All inputs are finite; a program needn't handle non-finite values.
Results may differ from a plain program's by a relative error of at most 0.03.
Values may be sent and summed in bfloat16 or wider, within the bound.
No kernel may reach another device: no remote copies, remote signals or barrier semaphores. Data moves between devices by JAX's collectives and lax.ppermute only.
A program may use at most 192 MiB of HBM per device.

v0:
```python
from functools import partial
import math

import jax
import jax.numpy as jnp
from jax import lax
from jax.sharding import PartitionSpec as P

HD = 64


NORM_EPSILON = 1e-12
MASK_VALUE = -1000000000.0


def layer_norm(values, gain_row, shift_row):
    centre = values - jnp.mean(values, axis=-1, keepdims=True)
    spread = jnp.mean(centre * centre, axis=-1, keepdims=True)
    return centre * lax.rsqrt(spread + NORM_EPSILON) * gain_row + shift_row


def gelu_exact(values):
    return jax.nn.gelu(values, approximate=False)


def fetch_again(
    layer_index,
    qkv_weight,
    out_weight,
    in_weight,
    down_weight,
    qv_bias,
    in_bias,
    row_bias,
    norm_gain,
    norm_shift,
):
    return (
        lax.all_gather(qkv_weight[layer_index], "dp", axis=1, tiled=True),
        lax.all_gather(out_weight[layer_index], "dp", axis=1, tiled=True),
        lax.all_gather(in_weight[layer_index], "dp", axis=0, tiled=True),
        lax.all_gather(down_weight[layer_index], "dp", axis=1, tiled=True),
        lax.all_gather(qv_bias[layer_index], "dp", axis=2, tiled=True),
        lax.all_gather(in_bias[layer_index], "dp", axis=1, tiled=True),
        lax.all_gather(row_bias[layer_index], "dp", axis=1, tiled=True),
        lax.all_gather(norm_gain[layer_index], "dp", axis=1, tiled=True),
        lax.all_gather(norm_shift[layer_index], "dp", axis=1, tiled=True),
    )


def gather_rows(row_block):
    return lax.all_gather(row_block, "tensor", axis=0, tiled=True)


def sum_rows(term_fn, row_count):
    return lax.psum_scatter(
        term_fn(jnp.int32(0), row_count * lax.axis_size("tensor")).astype(jnp.bfloat16),
        "tensor",
        scatter_dimension=0,
        tiled=True,
    ).astype(jnp.float32)


def gather_grads(row_block):
    return lax.all_gather(row_block, "tensor", axis=0, tiled=True)


def sum_grads(term_fn, row_count):
    return lax.psum_scatter(
        term_fn(jnp.int32(0), row_count * lax.axis_size("tensor")).astype(jnp.bfloat16),
        "tensor",
        scatter_dimension=0,
        tiled=True,
    ).astype(jnp.float32)


def slice_product(left_side, right_side, start, row_count):
    return jnp.dot(left_side, right_side, preferred_element_type=jnp.float32)


def slice_back(left_side, right_side, start, row_count):
    row_slice = lax.dynamic_slice_in_dim(left_side, start, row_count, 0)
    return lax.dot_general(
        row_slice, right_side, (((1,), (1,)), ((), ())), preferred_element_type=jnp.float32
    )


def slice_inputs(stacked, qkv_weight, start, row_count):
    row_slice = lax.dynamic_slice_in_dim(stacked, start, row_count, 1)
    return jnp.einsum("trc,tdc->rd", row_slice, qkv_weight, preferred_element_type=jnp.float32)


def head_scores(queries, key_rows, doc_ids):
    score_scale = 1.0 / math.sqrt(HD)
    scores = (
        jnp.einsum("qhe,khe->hqk", queries, key_rows, preferred_element_type=jnp.float32)
        * score_scale
    )
    same_doc = doc_ids[:, None] == doc_ids[None, :]
    return jnp.where(same_doc[None], scores, MASK_VALUE)


def attend(queries, key_rows, value_rows, doc_ids):
    all_rows, local_width = queries.shape
    seq_count, seq_length = doc_ids.shape
    head_shape = (seq_count, seq_length, local_width // HD, HD)

    def per_sequence(per_seq):
        query_seq, key_seq, value_seq, doc_seq = per_seq
        scores = head_scores(query_seq, key_seq, doc_seq)
        row_max = jnp.max(scores, axis=-1, keepdims=True)
        expo = jnp.exp(scores - row_max)
        row_sum = jnp.sum(expo, axis=-1, keepdims=True)
        weights_low = (expo / row_sum).astype(jnp.bfloat16)
        result = jnp.einsum(
            "hqk,khe->qhe", weights_low, value_seq, preferred_element_type=jnp.float32
        )
        return (result.astype(jnp.bfloat16), (row_max + jnp.log(row_sum))[..., 0])

    context, logsum = lax.map(
        per_sequence,
        (
            queries.reshape(head_shape),
            key_rows.reshape(head_shape),
            value_rows.reshape(head_shape),
            doc_ids,
        ),
    )
    return (context.reshape(all_rows, local_width), logsum)


def attend_back(queries, key_rows, value_rows, logsum, grad_context, doc_ids):
    all_rows, local_width = queries.shape
    seq_count, seq_length = doc_ids.shape
    head_shape = (seq_count, seq_length, local_width // HD, HD)
    score_scale = 1.0 / math.sqrt(HD)

    def per_sequence(per_seq):
        query_seq, key_seq, value_seq, lse_seq, grad_seq, doc_seq = per_seq
        scores = head_scores(query_seq, key_seq, doc_seq)
        weights_full = jnp.exp(scores - lse_seq[..., None])
        grad_value = jnp.einsum(
            "hqk,qhe->khe",
            weights_full.astype(jnp.bfloat16),
            grad_seq,
            preferred_element_type=jnp.float32,
        )
        grad_weights = jnp.einsum(
            "qhe,khe->hqk", grad_seq, value_seq, preferred_element_type=jnp.float32
        )
        centre = jnp.sum(weights_full * grad_weights, axis=-1, keepdims=True)
        grad_scores = (weights_full * (grad_weights - centre)).astype(jnp.bfloat16)
        grad_query = (
            jnp.einsum("hqk,khe->qhe", grad_scores, key_seq, preferred_element_type=jnp.float32)
            * score_scale
        )
        grad_key = (
            jnp.einsum("hqk,qhe->khe", grad_scores, query_seq, preferred_element_type=jnp.float32)
            * score_scale
        )
        return (
            grad_query.astype(jnp.bfloat16),
            grad_key.astype(jnp.bfloat16),
            grad_value.astype(jnp.bfloat16),
        )

    grad_q, grad_k, grad_v = lax.map(
        per_sequence,
        (
            queries.reshape(head_shape),
            key_rows.reshape(head_shape),
            value_rows.reshape(head_shape),
            logsum,
            grad_context.reshape(head_shape),
            doc_ids,
        ),
    )
    return (
        grad_q.reshape(all_rows, local_width),
        grad_k.reshape(all_rows, local_width),
        grad_v.reshape(all_rows, local_width),
    )


def forward_layer(current, doc_ids, params):
    (
        qkv_weight,
        out_weight,
        in_weight,
        down_weight,
        qv_bias,
        in_bias,
        row_bias,
        norm_gain,
        norm_shift,
    ) = params
    bias_rows = row_bias.astype(jnp.float32)
    gain_rows = norm_gain.astype(jnp.float32)
    shift_rows = norm_shift.astype(jnp.float32)
    row_count = current.shape[0]
    gathered = gather_rows(current.astype(jnp.bfloat16))
    projected = jnp.einsum("rd,tdc->trc", gathered, qkv_weight, preferred_element_type=jnp.float32)
    local_width = projected.shape[2]
    queries = (projected[0] + qv_bias[0].reshape(local_width).astype(jnp.float32)).astype(
        jnp.bfloat16
    )
    key_rows = projected[1].astype(jnp.bfloat16)
    value_rows = (projected[2] + qv_bias[1].reshape(local_width).astype(jnp.float32)).astype(
        jnp.bfloat16
    )
    context, logsum = attend(queries, key_rows, value_rows, doc_ids)
    mixed_one = (
        sum_rows(partial(slice_product, context, out_weight), row_count) + bias_rows[0] + current
    )
    normed = layer_norm(mixed_one, gain_rows[0], shift_rows[0])
    gathered_norm = gather_rows(normed.astype(jnp.bfloat16))
    hidden = jnp.dot(
        gathered_norm, in_weight, preferred_element_type=jnp.float32
    ) + in_bias.reshape(-1).astype(jnp.float32)
    active = gelu_exact(hidden).astype(jnp.bfloat16)
    mixed_two = (
        sum_rows(partial(slice_product, active, down_weight), row_count) + bias_rows[1] + normed
    )
    result = layer_norm(mixed_two, gain_rows[1], shift_rows[1])
    saved_state = (
        gathered,
        queries,
        key_rows,
        value_rows,
        context,
        logsum,
        mixed_one,
        gathered_norm,
        hidden,
        active,
        mixed_two,
    )
    return (result, saved_state)


def backward_layer(upstream, doc_ids, params, saved_state):
    (
        qkv_weight,
        out_weight,
        in_weight,
        down_weight,
        qv_bias,
        in_bias,
        row_bias,
        norm_gain,
        norm_shift,
    ) = params
    (
        gathered,
        queries,
        key_rows,
        value_rows,
        kept_context,
        logsum,
        mixed_one,
        gathered_norm,
        hidden,
        active,
        mixed_two,
    ) = saved_state
    gain_rows = norm_gain.astype(jnp.float32)
    shift_rows = norm_shift.astype(jnp.float32)
    row_count = upstream.shape[0]
    contract_rows = (((0,), (0,)), ((), ()))
    contract_cols = (((1,), (1,)), ((), ()))
    _, norm_back_two = jax.vjp(layer_norm, mixed_two, gain_rows[1], shift_rows[1])
    grad_two, gain_two, shift_two = norm_back_two(upstream)
    rows_two = gather_grads(grad_two.astype(jnp.bfloat16))
    grad_down = lax.dot_general(active, rows_two, contract_rows, preferred_element_type=jnp.float32)
    grad_active = lax.dot_general(
        rows_two, down_weight, contract_cols, preferred_element_type=jnp.float32
    )
    _, gelu_back = jax.vjp(gelu_exact, hidden)
    grad_hidden = gelu_back(grad_active)[0].astype(jnp.bfloat16)
    grad_inner = lax.dot_general(
        gathered_norm, grad_hidden, contract_rows, preferred_element_type=jnp.float32
    )
    grad_normed = sum_grads(partial(slice_back, grad_hidden, in_weight), row_count) + grad_two
    _, norm_back_one = jax.vjp(layer_norm, mixed_one, gain_rows[0], shift_rows[0])
    grad_one, gain_one, shift_one = norm_back_one(grad_normed)
    rows_one = gather_grads(grad_one.astype(jnp.bfloat16))
    grad_out = lax.dot_general(
        kept_context, rows_one, contract_rows, preferred_element_type=jnp.float32
    )
    grad_context = lax.dot_general(
        rows_one, out_weight, contract_cols, preferred_element_type=jnp.float32
    ).astype(jnp.bfloat16)
    grad_q, grad_k, grad_v = attend_back(
        queries, key_rows, value_rows, logsum, grad_context, doc_ids
    )
    stacked = jnp.stack([grad_q, grad_k, grad_v])
    grad_qkv = jnp.einsum("rd,trc->tdc", gathered, stacked, preferred_element_type=jnp.float32)
    grad_input = sum_grads(partial(slice_inputs, stacked, qkv_weight), row_count) + grad_one
    local_heads = queries.shape[1] // HD
    grad_qv = jnp.stack(
        [jnp.sum(grad_q, axis=0, dtype=jnp.float32), jnp.sum(grad_v, axis=0, dtype=jnp.float32)]
    ).reshape(2, local_heads, HD)
    grad_inner_bias = jnp.sum(grad_hidden, axis=0, dtype=jnp.float32).reshape(-1, HD)
    grad_bias_rows = jnp.stack([jnp.sum(grad_one, axis=0), jnp.sum(grad_two, axis=0)])
    grad_gain_rows = jnp.stack([gain_one, gain_two])
    grad_shift_rows = jnp.stack([shift_one, shift_two])
    return (
        grad_input,
        (
            grad_qkv,
            grad_out,
            grad_inner,
            grad_down,
            grad_qv,
            grad_inner_bias,
            grad_bias_rows,
            grad_gain_rows,
            grad_shift_rows,
        ),
    )


def on_device(
    tokens,
    cotangent,
    segment_ids,
    qkv_weight,
    out_weight,
    in_weight,
    down_weight,
    qv_bias,
    in_bias,
    row_bias,
    norm_gain,
    norm_shift,
):
    layers = qkv_weight.shape[0]
    model_width = tokens.shape[2]
    local_width = qkv_weight.shape[3]
    local_hidden = in_weight.shape[2]
    out_rows = out_weight.shape[1]
    zero_grads = (
        jnp.zeros((layers, 3, model_width, local_width), jnp.float32),
        jnp.zeros((layers, out_rows, model_width), jnp.float32),
        jnp.zeros((layers, model_width, local_hidden), jnp.float32),
        jnp.zeros((layers, local_hidden, model_width), jnp.float32),
        jnp.zeros((layers, 2, qv_bias.shape[2], HD), jnp.float32),
        jnp.zeros((layers, in_bias.shape[1], HD), jnp.float32),
        jnp.zeros((layers, 2, model_width), jnp.float32),
        jnp.zeros((layers, 2, model_width), jnp.float32),
        jnp.zeros((layers, 2, model_width), jnp.float32),
    )

    def micro_step(grad_totals, per_batch):
        token_rows, cot_rows, doc_ids = per_batch
        current = token_rows.astype(jnp.float32)
        saved_states = []
        for layer_index in range(layers):
            params = fetch_again(
                layer_index,
                qkv_weight,
                out_weight,
                in_weight,
                down_weight,
                qv_bias,
                in_bias,
                row_bias,
                norm_gain,
                norm_shift,
            )
            current, saved_state = forward_layer(current, doc_ids, params)
            saved_states.append(saved_state)
        upstream = cot_rows.astype(jnp.float32)
        updated = list(grad_totals)
        for layer_index in reversed(range(layers)):
            params = fetch_again(
                layer_index,
                qkv_weight,
                out_weight,
                in_weight,
                down_weight,
                qv_bias,
                in_bias,
                row_bias,
                norm_gain,
                norm_shift,
            )
            upstream, terms = backward_layer(upstream, doc_ids, params, saved_states[layer_index])
            updated = [summed.at[layer_index].add(term) for summed, term in zip(updated, terms)]
        return (tuple(updated), (current, upstream))

    totals, (outputs, grad_inputs) = lax.scan(
        micro_step, zero_grads, (tokens, cotangent, segment_ids)
    )
    out_total = totals[1]
    bias_sum, gain_sum, shift_sum = (
        lax.psum(totals[6].astype(jnp.bfloat16), "tensor").astype(jnp.float32),
        lax.psum(totals[7].astype(jnp.bfloat16), "tensor").astype(jnp.float32),
        lax.psum(totals[8].astype(jnp.bfloat16), "tensor").astype(jnp.float32),
    )
    shards = (
        lax.psum_scatter(totals[0], "dp", scatter_dimension=2, tiled=True),
        lax.psum_scatter(out_total, "dp", scatter_dimension=2, tiled=True),
        lax.psum_scatter(totals[2], "dp", scatter_dimension=1, tiled=True),
        lax.psum_scatter(totals[3], "dp", scatter_dimension=2, tiled=True),
        lax.psum_scatter(totals[4], "dp", scatter_dimension=3, tiled=True),
        lax.psum_scatter(totals[5], "dp", scatter_dimension=2, tiled=True),
        lax.psum_scatter(bias_sum, "dp", scatter_dimension=2, tiled=True),
        lax.psum_scatter(gain_sum, "dp", scatter_dimension=2, tiled=True),
        lax.psum_scatter(shift_sum, "dp", scatter_dimension=2, tiled=True),
    )
    return (
        outputs,
        grad_inputs,
        shards[0],
        shards[1],
        shards[2],
        shards[3],
        shards[4],
        shards[5],
        shards[6],
        shards[7],
        shards[8],
    )


def solution(mesh):
    placed = (
        P(None, ("dp", "tensor"), None),
        P(None, ("dp", "tensor"), None),
        P(None, "dp", None),
        P(None, None, "dp", "tensor"),
        P(None, "tensor", "dp"),
        P(None, "dp", "tensor"),
        P(None, "tensor", "dp"),
        P(None, None, "tensor", "dp"),
        P(None, "tensor", "dp"),
        P(None, None, "dp"),
        P(None, None, "dp"),
        P(None, None, "dp"),
    )
    return jax.shard_map(
        on_device,
        mesh=mesh,
        in_specs=placed,
        out_specs=(
            P(None, ("dp", "tensor"), None),
            P(None, ("dp", "tensor"), None),
            P(None, None, "dp", "tensor"),
            P(None, "tensor", "dp"),
            P(None, "dp", "tensor"),
            P(None, "tensor", "dp"),
            P(None, None, "tensor", "dp"),
            P(None, "tensor", "dp"),
            P(None, None, "dp"),
            P(None, None, "dp"),
            P(None, None, "dp"),
        ),
        check_vma=False,
    )
```

profile of v0, /device:TPU:0, one launch (start us, length us, event | category | flops | bytes accessed | tf_op | source)
XLA Modules:
  0.0 2571.4 jit_solution(2928028773543000333)
XLA Ops:
  26.5 1913.2 %while.179 = (s32[]{:T(128)}, f32[2,3,768,192]{2,3,1,0:T(8,128)}, f32[2,192,768]{2,1,0:T(8,128)}, f32[2,768,768]{2,1,0:T(8,128)}, f32[2,768,768]{2,1,0:T(8,128)}...) while((s32[]{:T(128)}, f32[2,3,768,192]{2,3,1,0:T(8,128)}, ...), condition=%wide.region_57.58_spmd, body=%wide.region_0.57_spmd.sunk | while | flops 23366356992 | bytes 576146304 | solution.py:392
  28.3 39.1 %all-gather.40 = bf16[1,3,768,192]{3,1,0,2:T(4,128)(2,1)S(1)} all-gather(bf16[1,3,96,192]{3,1,0,2:T(4,128)(2,1)S(1)} %get-tuple-element.1727), channel_id=3, replica_groups=mesh['dp'=8,'tensor'=4] {'dp'}, dimensions={2}, use_global_device_ids=true | all-gather | bytes 995328 | tf_op jit(solution)/shard_map/while/body/eval_jaxpr/all_gather | solution.py:39
  100.5 32.0 %all-gather.43 = bf16[1,192,768]{1,0,2:T(2,128)(2,1)S(1)} all-gather(bf16[1,192,96]{1,0,2:T(2,128)(2,1)S(1)} %get-tuple-element.1735), channel_id=5, replica_groups=mesh['dp'=8,'tensor'=4] {'dp'}, dimensions={2}, use_global_device_ids=true | all-gather | bytes 331776 | tf_op jit(solution)/shard_map/while/body/eval_jaxpr/all_gather | solution.py:40
  151.8 31.3 %all-gather.44 = bf16[1,2,768]{1,0,2:T(2,128)(2,1)S(1)} all-gather(bf16[1,2,96]{1,0,2:T(2,128)(2,1)S(1)} %get-tuple-element.1736), channel_id=6, replica_groups=mesh['dp'=8,'tensor'=4] {'dp'}, dimensions={2}, use_global_device_ids=true | all-gather | bytes 3456 | tf_op jit(solution)/shard_map/while/body/eval_jaxpr/all_gather | solution.py:45
  216.5 31.4 %all-gather.38 = bf16[1,2,768]{1,0,2:T(2,128)(2,1)S(1)} all-gather(bf16[1,2,96]{1,0,2:T(2,128)(2,1)S(1)} %get-tuple-element.1723), channel_id=8, replica_groups=mesh['dp'=8,'tensor'=4] {'dp'}, dimensions={2}, use_global_device_ids=true | all-gather | bytes 3456 | tf_op jit(solution)/shard_map/while/body/eval_jaxpr/all_gather | solution.py:47
  363.1 37.2 %all-gather.48 = bf16[1,3,768,192]{3,1,0,2:T(4,128)(2,1)S(1)} all-gather(bf16[1,3,96,192]{3,1,0,2:T(4,128)(2,1)} %get-tuple-element.1747), channel_id=12, replica_groups=mesh['dp'=8,'tensor'=4] {'dp'}, dimensions={2}, use_global_device_ids=true | all-gather | bytes 995328 | tf_op jit(solution)/shard_map/while/body/eval_jaxpr/all_gather | solution.py:39
  434.2 32.4 %all-gather.51 = bf16[1,192,768]{1,0,2:T(2,128)(2,1)S(1)} all-gather(bf16[1,192,96]{1,0,2:T(2,128)(2,1)} %get-tuple-element.1757), channel_id=14, replica_groups=mesh['dp'=8,'tensor'=4] {'dp'}, dimensions={2}, use_global_device_ids=true | all-gather | bytes 331776 | tf_op jit(solution)/shard_map/while/body/eval_jaxpr/all_gather | solution.py:40
  486.1 31.7 %all-gather.50 = bf16[1,2,768]{1,0,2:T(2,128)(2,1)S(1)} all-gather(bf16[1,2,96]{1,0,2:T(2,128)(2,1)S(1)} %copy-done.46), channel_id=15, replica_groups=mesh['dp'=8,'tensor'=4] {'dp'}, dimensions={2}, use_global_device_ids=true | all-gather | bytes 3456 | tf_op jit(solution)/shard_map/while/body/eval_jaxpr/all_gather | solution.py:45
  549.8 31.4 %all-gather.52 = bf16[1,2,768]{1,0,2:T(2,128)(2,1)S(1)} all-gather(bf16[1,2,96]{1,0,2:T(2,128)(2,1)S(1)} %copy-done.48), channel_id=17, replica_groups=mesh['dp'=8,'tensor'=4] {'dp'}, dimensions={2}, use_global_device_ids=true | all-gather | bytes 3456 | tf_op jit(solution)/shard_map/while/body/eval_jaxpr/all_gather | solution.py:47
  983.6 37.5 %all-gather.40 = bf16[1,3,768,192]{3,1,0,2:T(4,128)(2,1)S(1)} all-gather(bf16[1,3,96,192]{3,1,0,2:T(4,128)(2,1)S(1)} %get-tuple-element.1727), channel_id=3, replica_groups=mesh['dp'=8,'tensor'=4] {'dp'}, dimensions={2}, use_global_device_ids=true | all-gather | bytes 995328 | tf_op jit(solution)/shard_map/while/body/eval_jaxpr/all_gather | solution.py:39
  1054.1 32.1 %all-gather.43 = bf16[1,192,768]{1,0,2:T(2,128)(2,1)S(1)} all-gather(bf16[1,192,96]{1,0,2:T(2,128)(2,1)S(1)} %get-tuple-element.1735), channel_id=5, replica_groups=mesh['dp'=8,'tensor'=4] {'dp'}, dimensions={2}, use_global_device_ids=true | all-gather | bytes 331776 | tf_op jit(solution)/shard_map/while/body/eval_jaxpr/all_gather | solution.py:40
  1105.5 31.6 %all-gather.44 = bf16[1,2,768]{1,0,2:T(2,128)(2,1)S(1)} all-gather(bf16[1,2,96]{1,0,2:T(2,128)(2,1)S(1)} %get-tuple-element.1736), channel_id=6, replica_groups=mesh['dp'=8,'tensor'=4] {'dp'}, dimensions={2}, use_global_device_ids=true | all-gather | bytes 3456 | tf_op jit(solution)/shard_map/while/body/eval_jaxpr/all_gather | solution.py:45
  1170.4 31.4 %all-gather.38 = bf16[1,2,768]{1,0,2:T(2,128)(2,1)S(1)} all-gather(bf16[1,2,96]{1,0,2:T(2,128)(2,1)S(1)} %get-tuple-element.1723), channel_id=8, replica_groups=mesh['dp'=8,'tensor'=4] {'dp'}, dimensions={2}, use_global_device_ids=true | all-gather | bytes 3456 | tf_op jit(solution)/shard_map/while/body/eval_jaxpr/all_gather | solution.py:47
  1316.4 37.2 %all-gather.48 = bf16[1,3,768,192]{3,1,0,2:T(4,128)(2,1)S(1)} all-gather(bf16[1,3,96,192]{3,1,0,2:T(4,128)(2,1)} %get-tuple-element.1747), channel_id=12, replica_groups=mesh['dp'=8,'tensor'=4] {'dp'}, dimensions={2}, use_global_device_ids=true | all-gather | bytes 995328 | tf_op jit(solution)/shard_map/while/body/eval_jaxpr/all_gather | solution.py:39
  1387.5 32.4 %all-gather.51 = bf16[1,192,768]{1,0,2:T(2,128)(2,1)S(1)} all-gather(bf16[1,192,96]{1,0,2:T(2,128)(2,1)} %get-tuple-element.1757), channel_id=14, replica_groups=mesh['dp'=8,'tensor'=4] {'dp'}, dimensions={2}, use_global_device_ids=true | all-gather | bytes 331776 | tf_op jit(solution)/shard_map/while/body/eval_jaxpr/all_gather | solution.py:40
  1439.4 31.7 %all-gather.50 = bf16[1,2,768]{1,0,2:T(2,128)(2,1)S(1)} all-gather(bf16[1,2,96]{1,0,2:T(2,128)(2,1)S(1)} %copy-done.46), channel_id=15, replica_groups=mesh['dp'=8,'tensor'=4] {'dp'}, dimensions={2}, use_global_device_ids=true | all-gather | bytes 3456 | tf_op jit(solution)/shard_map/while/body/eval_jaxpr/all_gather | solution.py:45
  1503.1 31.4 %all-gather.52 = bf16[1,2,768]{1,0,2:T(2,128)(2,1)S(1)} all-gather(bf16[1,2,96]{1,0,2:T(2,128)(2,1)S(1)} %copy-done.48), channel_id=17, replica_groups=mesh['dp'=8,'tensor'=4] {'dp'}, dimensions={2}, use_global_device_ids=true | all-gather | bytes 3456 | tf_op jit(solution)/shard_map/while/body/eval_jaxpr/all_gather | solution.py:47
  2018.1 62.1 %reduce-scatter.38.cloned.1.call-done = f32[96,4]{1,0:T(8,128)} async-done(((f32[768,4]{1,0:T(8,128)}), f32[96,4]{1,0:T(8,128)}) %reduce-scatter.38.cloned.1.call-update) | async-done | bytes 1552
  2081.8 62.1 %reduce-scatter.40.cloned.1.call-done = f32[96,4]{1,0:T(8,128)} async-done(((f32[768,4]{1,0:T(8,128)}), f32[96,4]{1,0:T(8,128)}) %reduce-scatter.40.cloned.1.call-update) | async-done | bytes 1552
  2145.5 65.1 %reduce-scatter.34.cloned.1.call-done = f32[96,384]{1,0:T(8,128)} async-done(((f32[768,384]{1,0:T(8,128)}), f32[96,384]{1,0:T(8,128)}) %reduce-scatter.34.cloned.1.call-update) | async-done | bytes 147472
  2212.6 54.5 %reduce-scatter.32.cloned.1.call-done = f32[2,12,8]{1,2,0:T(8,128)} async-done(((f32[2,12,64]{1,2,0:T(8,128)}), f32[2,12,8]{1,2,0:T(8,128)}) %reduce-scatter.32.cloned.1.call-update) | async-done | bytes 784 | tf_op jit(solution)/shard_map/reduce_scatter | solution.py:407
  2267.1 98.5 %reduce-scatter.26.cloned.1.call-done = f32[2,3,96,192]{3,2,1,0:T(8,128)} async-done(((f32[2,3,768,192]{3,2,1,0:T(8,128)}), f32[2,3,96,192]{3,2,1,0:T(8,128)}) %reduce-scatter.26.cloned.1.call-update) | async-done | bytes 442384 | tf_op jit(solution)/shard_map/reduce_scatter | solution.py:402
  2365.6 99.1 %reduce-scatter.30.cloned.1.call-done = f32[2,768,96]{1,2,0:T(8,128)} async-done(((f32[2,768,768]{1,2,0:T(8,128)}), f32[2,768,96]{1,2,0:T(8,128)}) %reduce-scatter.30.cloned.1.call-update) | async-done | bytes 589840 | tf_op jit(solution)/shard_map/reduce_scatter | solution.py:405
  2464.7 99.0 %reduce-scatter.28.cloned.1.call-done = f32[2,96,768]{2,1,0:T(8,128)} async-done(((f32[2,768,768]{2,1,0:T(8,128)}), f32[2,96,768]{2,1,0:T(8,128)}) %reduce-scatter.28.cloned.1.call-update) | async-done | bytes 589840 | tf_op jit(solution)/shard_map/reduce_scatter | solution.py:404
  (1243 shorter events, 1542.5 us)
Async XLA Ops:
  26.6 108.2 %all-gather.70.cloned.1.call-start = ((), (), s32[]{:S(2)}) async-start(), calls=%async_computation.24 | async-start | bytes 1966080 | tf_op jit(solution)/shard_map/while/body/eval_jaxpr/all_gather | solution.py:52
  27.5 234.5 %reduce-scatter.42.cloned.1.call-start = ((), (), s32[]{:S(2)}) async-start(), calls=%async_computation.25 | async-start | bytes 1966080 | tf_op jit(solution)/shard_map/while/body/eval_jaxpr/reduce_scatter | solution.py:56
  150.2 144.1 %all-gather.74.cloned.1.call-start = ((), (), s32[]{:S(2)}) async-start(), calls=%async_computation.27 | async-start | bytes 1327104 | tf_op jit(solution)/shard_map/while/body/eval_jaxpr/all_gather | solution.py:41
  151.0 143.3 %all-gather.72.cloned.1.call-start = ((), (), s32[]{:S(2)}) async-start(), calls=%async_computation.26 | async-start | bytes 1966080 | tf_op jit(solution)/shard_map/while/body/eval_jaxpr/all_gather | solution.py:52
  267.5 92.9 %reduce-scatter.44.cloned.1.call-start = ((), (), s32[]{:S(2)}) async-start(), calls=%async_computation.29 | async-start | bytes 1966080 | tf_op jit(solution)/shard_map/while/body/eval_jaxpr/reduce_scatter | solution.py:56
  333.6 134.6 %all-gather.78.cloned.1.call-start = ((), (), s32[]{:S(2)}) async-start(), calls=%async_computation.30 | async-start | bytes 1966080 | tf_op jit(solution)/shard_map/while/body/eval_jaxpr/all_gather | solution.py:52
  363.1 232.2 %reduce-scatter.46.cloned.1.call-start = ((), (), s32[]{:S(2)}) async-start(), calls=%async_computation.31 | async-start | bytes 1966080 | tf_op jit(solution)/shard_map/while/body/eval_jaxpr/reduce_scatter | solution.py:56
  485.3 139.7 %all-gather.82.cloned.1.call-start = ((), (), s32[]{:S(2)}) async-start(), calls=%async_computation.33 | async-start | bytes 1327104 | tf_op jit(solution)/shard_map/while/body/eval_jaxpr/all_gather | solution.py:41
  486.0 138.9 %all-gather.80.cloned.1.call-start = ((), (), s32[]{:S(2)}) async-start(), calls=%async_computation.32 | async-start | bytes 1966080 | tf_op jit(solution)/shard_map/while/body/eval_jaxpr/all_gather | solution.py:52
  981.9 106.6 %all-gather.70.cloned.1.call-start = ((), (), s32[]{:S(2)}) async-start(), calls=%async_computation.24 | async-start | bytes 1966080 | tf_op jit(solution)/shard_map/while/body/eval_jaxpr/all_gather | solution.py:52
  982.8 233.2 %reduce-scatter.42.cloned.1.call-start = ((), (), s32[]{:S(2)}) async-start(), calls=%async_computation.25 | async-start | bytes 1966080 | tf_op jit(solution)/shard_map/while/body/eval_jaxpr/reduce_scatter | solution.py:56
  1103.9 144.3 %all-gather.74.cloned.1.call-start = ((), (), s32[]{:S(2)}) async-start(), calls=%async_computation.27 | async-start | bytes 1327104 | tf_op jit(solution)/shard_map/while/body/eval_jaxpr/all_gather | solution.py:41
  1104.7 143.5 %all-gather.72.cloned.1.call-start = ((), (), s32[]{:S(2)}) async-start(), calls=%async_computation.26 | async-start | bytes 1966080 | tf_op jit(solution)/shard_map/while/body/eval_jaxpr/all_gather | solution.py:52
  1286.9 134.6 %all-gather.78.cloned.1.call-start = ((), (), s32[]{:S(2)}) async-start(), calls=%async_computation.30 | async-start | bytes 1966080 | tf_op jit(solution)/shard_map/while/body/eval_jaxpr/all_gather | solution.py:52
  1316.4 232.2 %reduce-scatter.46.cloned.1.call-start = ((), (), s32[]{:S(2)}) async-start(), calls=%async_computation.31 | async-start | bytes 1966080 | tf_op jit(solution)/shard_map/while/body/eval_jaxpr/reduce_scatter | solution.py:56
  1438.6 139.8 %all-gather.82.cloned.1.call-start = ((), (), s32[]{:S(2)}) async-start(), calls=%async_computation.33 | async-start | bytes 1327104 | tf_op jit(solution)/shard_map/while/body/eval_jaxpr/all_gather | solution.py:41
  1439.3 139.1 %all-gather.80.cloned.1.call-start = ((), (), s32[]{:S(2)}) async-start(), calls=%async_computation.32 | async-start | bytes 1966080 | tf_op jit(solution)/shard_map/while/body/eval_jaxpr/all_gather | solution.py:52
  1953.8 126.4 %reduce-scatter.38.cloned.1.call-start = ((), (), s32[]{:S(2)}) async-start(), calls=%async_computation.22 | async-start | bytes 442368
  1955.6 188.4 %reduce-scatter.40.cloned.1.call-start = ((), (), s32[]{:S(2)}) async-start(), calls=%async_computation.23 | async-start | bytes 442368
  1957.3 253.4 %reduce-scatter.34.cloned.1.call-start = ((), (), s32[]{:S(2)}) async-start(), calls=%async_computation.20 | async-start | bytes 1327104
  1960.5 306.6 %reduce-scatter.32.cloned.1.call-start = ((), (), s32[]{:S(2)}) async-start(), calls=%async_computation.19 | async-start | bytes 73728 | tf_op jit(solution)/shard_map/reduce_scatter | solution.py:407
  1961.3 404.3 %reduce-scatter.26.cloned.1.call-start = ((), (), s32[]{:S(2)}) async-start(), calls=%async_computation.16 | async-start | bytes 5308416 | tf_op jit(solution)/shard_map/reduce_scatter | solution.py:402
  1966.9 497.8 %reduce-scatter.30.cloned.1.call-start = ((), (), s32[]{:S(2)}) async-start(), calls=%async_computation.18 | async-start | bytes 5308416 | tf_op jit(solution)/shard_map/reduce_scatter | solution.py:405
  1973.1 590.6 %reduce-scatter.28.cloned.1.call-start = ((), (), s32[]{:S(2)}) async-start(), calls=%async_computation.17 | async-start | bytes 5308416 | tf_op jit(solution)/shard_map/reduce_scatter | solution.py:404
  (305 other events, 6140.4 us)
Sparse Core Ops, SparseCore 0:
  29.5 22.3 all-gather.69
  150.3 27.0 reduce-scatter.41
  333.7 26.6 reduce-scatter.43
  485.3 26.6 reduce-scatter.45
  664.6 26.6 reduce-scatter.47
  698.2 19.6 all-gather.85
  763.1 19.6 all-gather.87
  846.0 19.6 all-gather.89
  909.8 19.6 all-gather.91
  951.3 28.2 reduce-scatter.55
  984.8 19.6 all-gather.69
  1104.0 26.2 reduce-scatter.41
  1287.0 26.6 reduce-scatter.43
  1438.7 26.6 reduce-scatter.45
  1618.1 26.6 reduce-scatter.47
  1651.7 19.6 all-gather.85
  1716.5 19.6 all-gather.87
  1799.4 19.6 all-gather.89
  1863.3 19.6 all-gather.91
  1904.8 28.2 reduce-scatter.55
Sparse Core Ops, SparseCore 1:
  153.4 41.3 all-gather.73
  287.6 41.5 all-gather.75
  363.1 19.5 all-gather.77
  489.0 41.4 all-gather.81
  618.6 41.5 all-gather.83
  728.3 28.1 reduce-scatter.49
  813.2 28.1 reduce-scatter.51
  876.1 28.1 reduce-scatter.53
  1107.2 40.8 all-gather.73
  1240.9 41.5 all-gather.75
  1316.5 19.5 all-gather.77
  1442.4 41.4 all-gather.81
  1572.0 41.5 all-gather.83
  1681.8 28.1 reduce-scatter.49
  1766.7 28.1 reduce-scatter.51
  1829.6 28.1 reduce-scatter.53
  1953.9 62.6 reduce-scatter.35
  2019.7 60.5 reduce-scatter.37
  2083.4 60.5 reduce-scatter.39
  2147.3 63.2 reduce-scatter.33
  2214.2 52.8 reduce-scatter.31
  2271.3 94.2 reduce-scatter.25
  2369.8 94.8 reduce-scatter.29
  2468.8 94.8 reduce-scatter.27
  (4 shorter events, 72.4 us)
where the time goes:
time: 2580 us; the launch traced here: 2570 us
  waiting for transfers between devices  1070 us (41%)
  blocking collectives  914 us (35%)
  matrix products  247 us (10%)
  local copies, waits for them, and re-layouts  206 us (8%)
  other arithmetic  102 us (4%)
    unnamed x12, waiting for transfers between devices  209 us
    reduce_scatter x8, waiting for transfers between devices, sum_grads(): lax.psum_scatter(term_fn(jnp.int32(0), row_count * lax.axis_size('tensor'...  189 us
    all_gather x4, blocking collectives, fetch_again(): lax.all_gather(qkv_weight[layer_index], 'dp', axis=1, tiled=True)  151 us
    all_gather x4, blocking collectives, fetch_again(): lax.all_gather(out_weight[layer_index], 'dp', axis=1, tiled=True)  129 us
    all_gather x4, blocking collectives, fetch_again(): lax.all_gather(row_bias[layer_index], 'dp', axis=1, tiled=True)  126 us
    all_gather x4, blocking collectives, fetch_again(): lax.all_gather(norm_shift[layer_index], 'dp', axis=1, tiled=True)  125 us
    all_gather x4, blocking collectives, fetch_again(): lax.all_gather(norm_gain[layer_index], 'dp', axis=1, tiled=True)  125 us
    all_gather x4, blocking collectives, fetch_again(): lax.all_gather(qv_bias[layer_index], 'dp', axis=2, tiled=True)  122 us
  transfers between devices with their start and end apart: 48, of which 32 were waited for; matrix products, arithmetic and copies ran while one was open for 10% of the time, Pallas kernels for 0%

commit v1 on v0

v1 whole, which is shorter than its diff:
```python
from functools import partial

import jax
import jax.numpy as jnp
from jax import lax
from jax.experimental import pallas as pl
from jax.experimental.pallas import tpu as pltpu
from jax.sharding import PartitionSpec as P

HD = 64
NORM_EPSILON = 1e-12
MASK_VALUE = -1000000000.0
F32 = jnp.float32
BF16 = jnp.bfloat16
VMEM_BYTES = 48 * 1024 * 1024
ROOT_HALF = 0.7071067811865476
ROOT_TWO_PI = 0.3989422804014327


def dot_nn(left, right):
    return lax.dot_general(left, right, (((1,), (0,)), ((), ())), preferred_element_type=F32)


def dot_nt(left, right):
    return lax.dot_general(left, right, (((1,), (1,)), ((), ())), preferred_element_type=F32)


def normed_rows(values):
    centre = values - jnp.mean(values, axis=-1, keepdims=True)
    spread = jnp.mean(centre * centre, axis=-1, keepdims=True)
    scale = lax.rsqrt(spread + NORM_EPSILON)
    return centre * scale, scale


def norm_back(upstream, normal, scale, gain):
    grad = upstream * gain
    mean_grad = jnp.mean(grad, axis=-1, keepdims=True)
    mean_both = jnp.mean(grad * normal, axis=-1, keepdims=True)
    return scale * (grad - mean_grad - normal * mean_both)


def token_sums(upstream, normal, result):
    return jnp.concatenate(
        [
            jnp.sum(upstream * normal, axis=0, keepdims=True),
            jnp.sum(upstream, axis=0, keepdims=True),
            jnp.sum(result, axis=0, keepdims=True),
        ],
        axis=0,
    )


def turned(values):
    return values.astype(F32).T.astype(BF16)


def whole(shape):
    return pl.BlockSpec(shape, lambda t: (0,) * len(shape))


def slab(shape):
    return pl.BlockSpec((None,) + tuple(shape), lambda t: (t,) + (0,) * len(shape))


def shaped(shape, dtype):
    return jax.ShapeDtypeStruct(tuple(shape), dtype)


def call(body, name, steps, in_specs, out_specs, out_shape, scratch, flops, moved):
    return pl.pallas_call(
        body,
        grid=(steps,),
        in_specs=in_specs,
        out_specs=out_specs,
        out_shape=out_shape,
        scratch_shapes=scratch,
        compiler_params=pltpu.CompilerParams(
            dimension_semantics=("arbitrary",), vmem_limit_bytes=VMEM_BYTES
        ),
        cost_estimate=pl.CostEstimate(flops=flops, bytes_accessed=moved, transcendentals=0),
        name=name,
    )


def attend_kernel(
    x_ref, w_ref, qb_ref, vb_ref, vec_ref, doc_col_ref, doc_row_ref,
    qkv_ref, prob_ref, context_ref, normal_ref, scale_ref,
    low_ref, total_ref,
):
    step = pl.program_id(0)

    @pl.when(step == 0)
    def _():
        low_ref[...] = x_ref[...].astype(BF16)
        total_ref[...] = x_ref[...].astype(F32) + vec_ref[0:1]

    width = qb_ref.shape[-1]
    projected = dot_nn(low_ref[...], w_ref[:, : 3 * width])
    queries = ((projected[:, :width] + qb_ref[...]).astype(BF16)) * jnp.asarray(0.125, BF16)
    key_rows = projected[:, width : 2 * width].astype(BF16)
    value_full = projected[:, 2 * width :] + vb_ref[...]
    value_rows = value_full.astype(BF16)
    qkv_ref[:, :width] = queries
    qkv_ref[:, width : 2 * width] = key_rows
    qkv_ref[:, 2 * width :] = value_rows
    value_turned = turned(value_full)
    same_doc = doc_col_ref[...] == doc_row_ref[...]
    parts = []
    for head in range(width // HD):
        cols = slice(head * HD, (head + 1) * HD)
        scores = jnp.where(same_doc, dot_nt(key_rows[:, cols], queries[:, cols]), MASK_VALUE)
        expo = jnp.exp(scores - jnp.max(scores, axis=0, keepdims=True))
        weights = (expo * (1.0 / jnp.sum(expo, axis=0, keepdims=True))).astype(BF16)
        prob_ref[head] = weights
        parts.append(dot_nn(value_turned[cols], weights))
    context_turned = jnp.concatenate(parts, axis=0)
    context_ref[...] = context_turned.astype(BF16)
    context = context_turned.T.astype(BF16)
    total_ref[...] += dot_nt(context, w_ref[:, 3 * width :])

    @pl.when(step == pl.num_programs(0) - 1)
    def _():
        normal, scale = normed_rows(total_ref[...])
        normal_ref[...] = normal
        scale_ref[...] = scale


def attend(x, weight, q_bias, v_bias, vec, doc_ids):
    steps, width = q_bias.shape[0], q_bias.shape[2]
    rows, model = x.shape
    heads = width // HD
    return call(
        attend_kernel,
        "attend",
        steps,
        [
            whole((rows, model)),
            slab((model, 4 * width)),
            slab((1, width)),
            slab((1, width)),
            whole(vec.shape),
            whole((rows, 1)),
            whole((1, rows)),
        ],
        [
            slab((rows, 3 * width)),
            pl.BlockSpec((heads, rows, rows), lambda t: (t, 0, 0)),
            slab((width, rows)),
            whole((rows, model)),
            whole((rows, 1)),
        ],
        [
            shaped((steps, rows, 3 * width), BF16),
            shaped((steps * heads, rows, rows), BF16),
            shaped((steps, width, rows), BF16),
            shaped((rows, model), F32),
            shaped((rows, 1), F32),
        ],
        [pltpu.VMEM((rows, model), BF16), pltpu.VMEM((rows, model), F32)],
        2 * rows * model * 4 * width * steps + 4 * rows * rows * width * steps * 4,
        weight.size * 2 + steps * heads * rows * rows * 2,
    )(x, weight, q_bias, v_bias, vec, doc_ids.reshape(rows, 1), doc_ids.reshape(1, rows))


def hidden_kernel(normal_ref, vec_ref, w_ref, bias_ref, low_out_ref, active_ref, slope_ref, low_ref):
    @pl.when(pl.program_id(0) == 0)
    def _():
        low = (normal_ref[...] * vec_ref[1:2] + vec_ref[2:3]).astype(BF16)
        low_ref[...] = low
        low_out_ref[...] = low

    hidden = dot_nn(low_ref[...], w_ref[...]) + bias_ref[...]
    below = 0.5 + 0.5 * lax.erf(hidden * ROOT_HALF)
    active_ref[...] = (hidden * below).astype(BF16)
    slope_ref[...] = (below + hidden * (jnp.exp(hidden * hidden * -0.5) * ROOT_TWO_PI)).astype(BF16)


def hidden_units(normal, vec, weight, bias):
    steps, model, width = weight.shape
    rows = normal.shape[0]
    return call(
        hidden_kernel,
        "hidden",
        steps,
        [whole((rows, model)), whole(vec.shape), slab((model, width)), slab((1, width))],
        [whole((rows, model)), slab((rows, width)), slab((rows, width))],
        [
            shaped((rows, model), BF16),
            shaped((steps, rows, width), BF16),
            shaped((steps, rows, width), BF16),
        ],
        [pltpu.VMEM((rows, model), BF16)],
        2 * rows * model * width * steps * 2,
        weight.size * 2 + 4 * rows * width * steps,
    )(normal, vec, weight, bias)


def down_kernel(active_ref, w_ref, normal_ref, vec_ref, vec_two_ref, out_ref, normal_two_ref, scale_ref, total_ref):
    step = pl.program_id(0)

    @pl.when(step == 0)
    def _():
        total_ref[...] = normal_ref[...] * vec_ref[1:2] + vec_ref[2:3] + vec_two_ref[0:1]

    total_ref[...] += dot_nt(active_ref[...], w_ref[...])

    @pl.when(step == pl.num_programs(0) - 1)
    def _():
        normal, scale = normed_rows(total_ref[...])
        normal_two_ref[...] = normal
        scale_ref[...] = scale
        out_ref[...] = normal * vec_two_ref[1:2] + vec_two_ref[2:3]


def down(active, weight, normal, vec, vec_two):
    steps, rows, width = active.shape
    model = weight.shape[1]
    return call(
        down_kernel,
        "down",
        steps,
        [
            slab((rows, width)),
            slab((model, width)),
            whole((rows, model)),
            whole(vec.shape),
            whole(vec_two.shape),
        ],
        [whole((rows, model)), whole((rows, model)), whole((rows, 1))],
        [shaped((rows, model), F32), shaped((rows, model), F32), shaped((rows, 1), F32)],
        [pltpu.VMEM((rows, model), F32)],
        2 * rows * model * width * steps,
        weight.size * 2 + 2 * rows * width * steps + 12 * rows * model,
    )(active, weight, normal, vec, vec_two)


def down_back_kernel(
    up_ref, normal_ref, scale_ref, vec_ref, active_ref, slope_ref, w_ref,
    grad_w_ref, grad_hidden_ref, grad_rows_ref, sums_ref, unit_sums_ref,
    low_ref, turned_ref,
):
    @pl.when(pl.program_id(0) == 0)
    def _():
        upstream = up_ref[...].astype(F32)
        normal = normal_ref[...]
        grad = norm_back(upstream, normal, scale_ref[...], vec_ref[1:2])
        grad_rows_ref[...] = grad
        sums_ref[...] = token_sums(upstream, normal, grad)
        low_ref[...] = grad.astype(BF16)
        turned_ref[...] = grad.T.astype(BF16)

    grad_w_ref[...] = dot_nn(turned_ref[...], active_ref[...]).astype(BF16)
    grad_hidden = (dot_nn(low_ref[...], w_ref[...]) * slope_ref[...].astype(F32)).astype(BF16)
    grad_hidden_ref[...] = grad_hidden
    unit_sums_ref[...] = jnp.sum(grad_hidden.astype(F32), axis=0, keepdims=True)


def down_back(upstream, normal, scale, vec, active, slope, weight):
    steps, rows, width = active.shape
    model = weight.shape[1]
    return call(
        down_back_kernel,
        "down_back",
        steps,
        [
            whole((rows, model)),
            whole((rows, model)),
            whole((rows, 1)),
            whole(vec.shape),
            slab((rows, width)),
            slab((rows, width)),
            slab((model, width)),
        ],
        [
            slab((model, width)),
            slab((rows, width)),
            whole((rows, model)),
            whole((3, model)),
            slab((1, width)),
        ],
        [
            shaped((steps, model, width), BF16),
            shaped((steps, rows, width), BF16),
            shaped((rows, model), F32),
            shaped((3, model), F32),
            shaped((steps, 1, width), F32),
        ],
        [pltpu.VMEM((rows, model), BF16), pltpu.VMEM((model, rows), BF16)],
        4 * rows * model * width * steps,
        weight.size * 4 + 6 * rows * width * steps + 12 * rows * model,
    )(upstream, normal, scale, vec, active, slope, weight)


def hidden_back_kernel(
    low_in_ref, grad_hidden_ref, w_ref, grad_two_ref, normal_ref, scale_ref, vec_ref,
    grad_w_ref, grad_one_ref, sums_ref,
    turned_ref, total_ref,
):
    step = pl.program_id(0)

    @pl.when(step == 0)
    def _():
        turned_ref[...] = turned(low_in_ref[...])
        total_ref[...] = grad_two_ref[...]

    grad_w_ref[...] = dot_nn(turned_ref[...], grad_hidden_ref[...]).astype(BF16)
    total_ref[...] += dot_nt(grad_hidden_ref[...], w_ref[...])

    @pl.when(step == pl.num_programs(0) - 1)
    def _():
        upstream = total_ref[...]
        normal = normal_ref[...]
        grad = norm_back(upstream, normal, scale_ref[...], vec_ref[1:2])
        grad_one_ref[...] = grad
        sums_ref[...] = token_sums(upstream, normal, grad)


def hidden_back(low, grad_hidden, weight, grad_two, normal, scale, vec):
    steps, rows, width = grad_hidden.shape
    model = weight.shape[1]
    return call(
        hidden_back_kernel,
        "hidden_back",
        steps,
        [
            whole((rows, model)),
            slab((rows, width)),
            slab((model, width)),
            whole((rows, model)),
            whole((rows, model)),
            whole((rows, 1)),
            whole(vec.shape),
        ],
        [slab((model, width)), whole((rows, model)), whole((3, model))],
        [
            shaped((steps, model, width), BF16),
            shaped((rows, model), F32),
            shaped((3, model), F32),
        ],
        [pltpu.VMEM((model, rows), BF16), pltpu.VMEM((rows, model), F32)],
        4 * rows * model * width * steps,
        weight.size * 4 + 2 * rows * width * steps + 12 * rows * model,
    )(low, grad_hidden, weight, grad_two, normal, scale, vec)


def attend_back_kernel(
    x_ref, grad_one_ref, w_ref, qkv_ref, prob_ref, context_ref,
    grad_w_ref, grad_x_ref, sums_ref,
    low_ref, turned_ref, x_turned_ref,
):
    step = pl.program_id(0)

    @pl.when(step == 0)
    def _():
        grad = grad_one_ref[...]
        low_ref[...] = grad.astype(BF16)
        turned_ref[...] = grad.T.astype(BF16)
        x_turned_ref[...] = turned(x_ref[...].astype(BF16))
        grad_x_ref[...] = grad

    width = context_ref.shape[0]
    queries, key_rows = qkv_ref[:, :width], qkv_ref[:, width : 2 * width]
    value_rows = qkv_ref[:, 2 * width :]
    key_turned = turned(key_rows)
    grad_context = dot_nn(low_ref[...], w_ref[:, 3 * width :]).astype(BF16)
    grad_w_ref[:, 3 * width :] = dot_nt(turned_ref[...], context_ref[...]).astype(BF16)
    grad_q, grad_k, grad_v = [], [], []
    for head in range(width // HD):
        cols = slice(head * HD, (head + 1) * HD)
        low_weights = prob_ref[head]
        weights = low_weights.astype(F32)
        part = weights * dot_nt(value_rows[:, cols], grad_context[:, cols])
        centre = jnp.sum(part, axis=0, keepdims=True)
        grad_scores = (part - weights * centre).astype(BF16)
        grad_v.append(dot_nn(low_weights, grad_context[:, cols]))
        grad_k.append(dot_nn(grad_scores, queries[:, cols]))
        grad_q.append(dot_nn(key_turned[cols], grad_scores))
    stacked = jnp.concatenate(
        [(jnp.concatenate(grad_q, axis=0) * 0.125).T] + grad_k + grad_v, axis=1
    ).astype(BF16)
    grad_w_ref[:, : 3 * width] = dot_nn(x_turned_ref[...], stacked).astype(BF16)
    grad_x_ref[...] += dot_nt(stacked, w_ref[:, : 3 * width])
    sums_ref[...] = jnp.sum(stacked.astype(F32), axis=0, keepdims=True)


def attend_back(x, grad_one, weight, qkv, prob, context):
    steps, width, rows = context.shape
    model = weight.shape[1]
    heads = width // HD
    return call(
        attend_back_kernel,
        "attend_back",
        steps,
        [
            whole((rows, model)),
            whole((rows, model)),
            slab((model, 4 * width)),
            slab((rows, 3 * width)),
            pl.BlockSpec((heads, rows, rows), lambda t: (t, 0, 0)),
            slab((width, rows)),
        ],
        [slab((model, 4 * width)), whole((rows, model)), slab((1, 3 * width))],
        [
            shaped((steps, model, 4 * width), BF16),
            shaped((rows, model), F32),
            shaped((steps, 1, 3 * width), F32),
        ],
        [
            pltpu.VMEM((rows, model), BF16),
            pltpu.VMEM((model, rows), BF16),
            pltpu.VMEM((model, rows), BF16),
        ],
        4 * rows * model * 4 * width * steps + 8 * rows * rows * width * steps * 4,
        weight.size * 4 + steps * heads * rows * rows * 2 + 8 * rows * model,
    )(x, grad_one, weight, qkv, prob, context)


BOTH = ("tensor", "dp")


def swap_cores(values):
    count = lax.axis_size("tensor")
    return lax.ppermute(values, "tensor", [(i, i ^ 1) for i in range(count)])


def to_sequence(blocks, core):
    mine = lax.dynamic_index_in_dim(blocks, core, 0, keepdims=False)
    other = lax.dynamic_index_in_dim(blocks, 1 - core, 0, keepdims=False)
    got = swap_cores(other)
    return jnp.concatenate(
        [jnp.where(core == 0, mine, got), jnp.where(core == 0, got, mine)], axis=0
    )


def from_sequence(values, core):
    half = values.shape[0] // 2
    mine = lax.dynamic_slice_in_dim(values, core * half, half, 0)
    got = swap_cores(lax.dynamic_slice_in_dim(values, (1 - core) * half, half, 0))
    return jnp.stack([jnp.where(core == 0, mine, got), jnp.where(core == 0, got, mine)])


def gather_group(shard, teams):
    rows, width = shard.shape
    got = lax.all_gather(shard, BOTH, axis=0, tiled=True)
    return got.reshape(teams, -1, width)


def scatter_group(grads):
    return lax.psum_scatter(
        grads.reshape(-1, grads.shape[-1]), BOTH, scatter_dimension=0, tiled=True
    ).astype(F32)


def on_device(
    tokens, cotangent, segment_ids, qkv_weight, out_weight, in_weight, down_weight,
    qv_bias, in_bias, row_bias, norm_gain, norm_shift,
):
    teams, parts = lax.axis_size("tensor"), lax.axis_size("dp")
    layers, _, piece, width = qkv_weight.shape
    heads = width // HD
    model = piece * parts
    units = in_weight.shape[2]
    tensor_at = lax.axis_index("tensor")
    core = tensor_at % 2

    out_turned = jnp.swapaxes(out_weight, 1, 2)
    down_turned = jnp.swapaxes(down_weight, 1, 2)
    attn_shard = jnp.concatenate(
        [qkv_weight[:, 0], qkv_weight[:, 1], qkv_weight[:, 2], out_turned], axis=2
    )
    small = (qv_bias, in_bias, row_bias, norm_gain, norm_shift)
    lengths = [s.size for s in small]
    flat = jnp.concatenate([s.reshape(-1) for s in small]).reshape(1, -1)
    flat_all = lax.all_gather(flat, BOTH, axis=0, tiled=True).reshape(teams, parts, -1)
    edges = [0]
    for n in lengths:
        edges.append(edges[-1] + n)
    cut = [flat_all[:, :, a:b] for a, b in zip(edges[:-1], edges[1:])]
    qv_all = (
        cut[0].reshape((teams, parts) + qv_bias.shape).transpose(2, 3, 0, 4, 1, 5)
        .reshape(layers, 2, teams, 1, width).astype(F32)
    )
    in_all = (
        cut[1].reshape((teams, parts) + in_bias.shape).transpose(2, 0, 3, 1, 4)
        .reshape(layers, teams, 1, units).astype(F32)
    )
    vecs = jnp.stack(
        [
            c[0].reshape((parts,) + row_bias.shape).transpose(1, 2, 0, 3)
            .reshape(layers, 2, model).astype(F32)
            for c in cut[2:]
        ],
        axis=2,
    )

    weights = []
    for layer in range(layers):
        weights.append(
            [
                gather_group(attn_shard[layer], teams),
                gather_group(in_weight[layer], teams),
                gather_group(down_turned[layer], teams),
            ]
        )

    doc_ids = segment_ids[core, tensor_at // 2]
    current = to_sequence(tokens, core)
    upstream = to_sequence(cotangent, core)

    saved = []
    for layer in range(layers):
        attn_w, in_w, down_w = weights[layer]
        entered = current
        qkv, prob, context, normal_one, scale_one = attend(
            entered, attn_w, qv_all[layer, 0], qv_all[layer, 1], vecs[layer, 0], doc_ids
        )
        low, active, slope = hidden_units(normal_one, vecs[layer, 0], in_w, in_all[layer])
        current, normal_two, scale_two = down(
            active, down_w, normal_one, vecs[layer, 0], vecs[layer, 1]
        )
        saved.append(
            (entered, qkv, prob, context, normal_one, scale_one, low, active, slope, normal_two, scale_two)
        )
    output = from_sequence(current, core)

    grads = [None] * layers
    smalls = [None] * layers
    for layer in reversed(range(layers)):
        attn_w, in_w, down_w = weights[layer]
        (entered, qkv, prob, context, normal_one, scale_one, low, active, slope, normal_two, scale_two) = saved[layer]
        grad_down, grad_hidden, grad_two, sums_two, unit_sums = down_back(
            upstream, normal_two, scale_two, vecs[layer, 1], active, slope, down_w
        )
        grad_in, grad_one, sums_one = hidden_back(
            low, grad_hidden, in_w, grad_two, normal_one, scale_one, vecs[layer, 0]
        )
        grad_attn, upstream, qkv_sums = attend_back(entered, grad_one, attn_w, qkv, prob, context)
        grads[layer] = (
            scatter_group(grad_attn),
            scatter_group(grad_in),
            scatter_group(grad_down),
        )
        smalls[layer] = (qkv_sums, unit_sums, sums_one, sums_two)
    grad_tokens = from_sequence(upstream, core)

    sizes = [s.size for s in smalls[0]]
    flat = jnp.concatenate([s.reshape(-1) for layer in smalls for s in layer])
    flat = lax.psum(flat, BOTH).reshape(layers, -1)
    dp_at = lax.axis_index("dp")
    qkv_sums = flat[:, : sizes[0]].reshape(layers, teams, 3, heads, parts, -1)
    qkv_sums = lax.dynamic_index_in_dim(qkv_sums, tensor_at, 1, keepdims=False)
    qkv_sums = lax.dynamic_index_in_dim(qkv_sums, dp_at, 3, keepdims=False)
    grad_qv = jnp.stack([qkv_sums[:, 0], qkv_sums[:, 2]], axis=1)
    unit_sums = flat[:, sizes[0] : sizes[0] + sizes[1]].reshape(layers, teams, units // HD, parts, -1)
    unit_sums = lax.dynamic_index_in_dim(unit_sums, tensor_at, 1, keepdims=False)
    grad_unit = lax.dynamic_index_in_dim(unit_sums, dp_at, 2, keepdims=False)
    row_sums = flat[:, sizes[0] + sizes[1] :].reshape(layers, 2, 3, parts, piece)
    row_sums = lax.dynamic_index_in_dim(row_sums, dp_at, 3, keepdims=False)

    grad_attn = jnp.stack([g[0] for g in grads])
    grad_qkv = jnp.stack(
        [grad_attn[:, :, i * width : (i + 1) * width] for i in range(3)], axis=1
    )
    return (
        output,
        grad_tokens,
        grad_qkv,
        jnp.swapaxes(grad_attn[:, :, 3 * width :], 1, 2),
        jnp.stack([g[1] for g in grads]),
        jnp.swapaxes(jnp.stack([g[2] for g in grads]), 1, 2),
        grad_qv,
        grad_unit,
        row_sums[:, :, 2],
        row_sums[:, :, 0],
        row_sums[:, :, 1],
    )


def solution(mesh):
    placed = (
        P(None, ("dp", "tensor"), None),
        P(None, ("dp", "tensor"), None),
        P(None, "dp", None),
        P(None, None, "dp", "tensor"),
        P(None, "tensor", "dp"),
        P(None, "dp", "tensor"),
        P(None, "tensor", "dp"),
        P(None, None, "tensor", "dp"),
        P(None, "tensor", "dp"),
        P(None, None, "dp"),
        P(None, None, "dp"),
        P(None, None, "dp"),
    )
    return jax.shard_map(
        on_device,
        mesh=mesh,
        in_specs=placed,
        out_specs=(
            P(None, ("dp", "tensor"), None),
            P(None, ("dp", "tensor"), None),
            P(None, None, "dp", "tensor"),
            P(None, "tensor", "dp"),
            P(None, "dp", "tensor"),
            P(None, "tensor", "dp"),
            P(None, None, "tensor", "dp"),
            P(None, "tensor", "dp"),
            P(None, None, "dp"),
            P(None, None, "dp"),
            P(None, None, "dp"),
        ),
        check_vma=False,
    )
```

time: 2580 us -> 1430 us (0.55)
  blocking collectives: 914 us -> 0 us
  matrix products: 247 us -> 0 us
  local copies, waits for them, and re-layouts: 206 us -> 42.7 us
  waiting for transfers between devices: 1070 us -> 1220 us
  Pallas kernels: 0 us -> 137 us
  other arithmetic: 102 us -> 11.5 us
    all_gather x28 -> x0, blocking collectives: 882 us -> none  [the longest x4 151 us: fetch_again(): lax.all_gather(qkv_weight[layer_index], 'dp', axis=1, tiled=True)]
    dot_general x100 -> x0, matrix products: 236 us -> none  [the longest x4 44.8 us: forward_layer(): jnp.dot(gathered_norm, in_weight, preferred_element_type=jnp.float32)]
    reduce_scatter x20 -> x4, waiting for transfers between devices: 648 us -> 443 us  [scatter_group(): lax.psum_scatter(grads.reshape(-1, grads.shape[-1]), BOTH, scatter_dimens...]
    pallas_call x0 -> x12, Pallas kernels: none -> 137 us  [the longest x2 37 us: attend_back(): call(attend_back_kernel, 'attend_back', steps, [whole((rows, model)), who...]
    unnamed x12 -> x17, waiting for transfers between devices: 209 us -> 333 us
    all_gather x24 -> x6, waiting for transfers between devices: 212 us -> 327 us  [gather_group(): got = lax.all_gather(shard, BOTH, axis=0, tiled=True)]
    psum x0 -> x1, waiting for transfers between devices: none -> 112 us  [on_device(): flat = lax.psum(flat, BOTH).reshape(layers, -1)]
    slice x38 -> x11, local copies, waits for them, and re-layouts: 69.8 us -> 5.98 us  [the longest x1 1.35 us: on_device(): flat[:, sizes[0]:sizes[0] + sizes[1]]]
  transfers between devices with their start and end apart: 48 -> 18, of which waited for: 32 -> 14; matrix products, arithmetic and copies ran while one was open for 10% -> 2% of each run, Pallas kernels for 0% -> 4%
where the time goes in v1:
time: 1430 us; the launch traced here: 1420 us
  waiting for transfers between devices  1220 us (85%)
  Pallas kernels  137 us (10%)
  local copies, waits for them, and re-layouts  42.7 us (3%)
  between operations  15.2 us (1%)
    reduce_scatter x4, waiting for transfers between devices, scatter_group(): lax.psum_scatter(grads.reshape(-1, grads.shape[-1]), BOTH, scatter_dimens...  443 us
    unnamed x17, waiting for transfers between devices  333 us
    all_gather x6, waiting for transfers between devices, gather_group(): got = lax.all_gather(shard, BOTH, axis=0, tiled=True)  327 us
    psum x1, waiting for transfers between devices, on_device(): flat = lax.psum(flat, BOTH).reshape(layers, -1)  112 us
    pallas_call x2, Pallas kernels, attend_back(): call(attend_back_kernel, 'attend_back', steps, [whole((rows, model)), who...  37 us
    pallas_call x2, Pallas kernels, attend(): call(attend_kernel, 'attend', steps, [whole((rows, model)), slab((model,...  30.5 us
  transfers between devices with their start and end apart: 18, of which 14 were waited for; matrix products, arithmetic and copies ran while one was open for 2% of the time, Pallas kernels for 4%

profile of v1, /device:TPU:0, one launch (start us, length us, event | category | flops | bytes accessed | tf_op | source)
XLA Modules:
  0.0 1423.6 jit_solution(2637988215734043342)
XLA Ops:
  23.0 114.4 %all-reduce.6.cloned.1.call-done = bf16[46080]{0:T(1024)(128)(2,1)} async-done(((bf16[46080]{0:T(1024)(128)(2,1)}), bf16[46080]{0:T(1024)(128)(2,1)}) %all-reduce.6.cloned.1.call-update) | async-done | bytes 92176
  143.0 62.7 %all-gather.14.cloned.1.call-done = bf16[1,3072,768]{2,1,0:T(8,128)(2,1)} async-done(((bf16[1,96,768]{2,1,0:T(8,128)(2,1)}), bf16[1,3072,768]{2,1,0:T(8,128)(2,1)}) %all-gather.14.cloned.1.call-update) | async-done | bytes 4718608 | tf_op jit(solution)/shard_map/all_gather | solution.py:444
  205.7 15.2 %attend.2 = (bf16[4,512,576]{2,1,0:T(8,128)(2,1)}, bf16[12,512,512]{2,1,0:T(8,128)(2,1)}, bf16[4,192,512]{2,1,0:T(8,128)(2,1)S(1)}, f32[512,768]{1,0:T(8,128)S(1)}, f32[512,1]{1,0:T(8,128)S(1)}) custom-call(bf16[512,768]{1,0:T(8,128)(2,1)S(1)} %pad_maximum_fusion.2.x_ref, bf16[4,768,768]{2,1,0:T(8,128)(2,1)} %bitcast.143, ...), custom_call_target="tpu_custom_call" | custom-call | flops 5637144576 | bytes 11010048 | tf_op jit(solution)/shard_map/attend/pallas_call | solution.py:132
  221.8 50.0 %all-gather.16.cloned.1.call-done = bf16[1,3072,768]{2,1,0:T(8,128)(2,1)} async-done(((bf16[1,96,768]{2,1,0:T(8,128)(2,1)}), bf16[1,3072,768]{2,1,0:T(8,128)(2,1)}) %all-gather.16.cloned.1.call-update) | async-done | bytes 4718608 | tf_op jit(solution)/shard_map/all_gather | solution.py:444
  271.8 7.6 hidden.2
  281.9 55.8 %all-gather.18.cloned.1.call-done = bf16[1,3072,768]{2,1,0:T(8,128)(2,1)} async-done(((bf16[1,96,768]{2,1,0:T(8,128)(2,1)}), bf16[1,3072,768]{2,1,0:T(8,128)(2,1)}) %all-gather.18.cloned.1.call-update) | async-done | bytes 4718608 | tf_op jit(solution)/shard_map/all_gather | solution.py:444
  347.1 56.6 %all-gather.20.cloned.1.call-done = bf16[1,3072,768]{2,1,0:T(8,128)(2,1)} async-done(((bf16[1,96,768]{2,1,0:T(8,128)(2,1)}), bf16[1,3072,768]{2,1,0:T(8,128)(2,1)}) %all-gather.20.cloned.1.call-update) | async-done | bytes 4718608 | tf_op jit(solution)/shard_map/all_gather | solution.py:444
  405.1 15.3 %attend.3 = (bf16[4,512,576]{2,1,0:T(8,128)(2,1)}, bf16[12,512,512]{2,1,0:T(8,128)(2,1)}, bf16[4,192,512]{2,1,0:T(8,128)(2,1)S(1)}, f32[512,768]{1,0:T(8,128)S(1)}, f32[512,1]{1,0:T(8,128)S(1)}) custom-call(f32[512,768]{1,0:T(8,128)S(1)} %copy-done.11, bf16[4,768,768]{2,1,0:T(8,128)(2,1)} %bitcast.147, f32[4,1,192]{2,1,0:T(1,128)S(1)} %get-tuple-element.174.qb_ref, ...), custom_call_target="tpu_custom_call" | custom-call | flops 5637144576 | bytes 11010048 | tf_op jit(solution)/shard_map/attend/pallas_call | solution.py:132
  422.0 47.0 %all-gather.22.cloned.1.call-done = bf16[1,3072,768]{2,1,0:T(8,128)(2,1)} async-done(((bf16[1,96,768]{2,1,0:T(8,128)(2,1)}), bf16[1,3072,768]{2,1,0:T(8,128)(2,1)}) %all-gather.22.cloned.1.call-update) | async-done | bytes 4718608 | tf_op jit(solution)/shard_map/all_gather | solution.py:444
  469.0 7.6 hidden.3
  479.2 55.3 %all-gather.24.cloned.1.call-done = bf16[1,3072,768]{2,1,0:T(8,128)(2,1)} async-done(((bf16[1,96,768]{2,1,0:T(8,128)(2,1)}), bf16[1,3072,768]{2,1,0:T(8,128)(2,1)}) %all-gather.24.cloned.1.call-update) | async-done | bytes 4718608 | tf_op jit(solution)/shard_map/all_gather | solution.py:444
  542.4 10.9 down_back.2
  553.3 10.2 hidden_back.2
  563.5 18.6 %attend_back.2 = (bf16[4,768,768]{2,1,0:T(8,128)(2,1)}, f32[512,768]{1,0:T(8,128)S(1)}, f32[4,1,576]{2,1,0:T(1,128)S(1)}) custom-call(f32[512,768]{1,0:T(8,128)S(1)} %copy-done.12, f32[512,768]{1,0:T(8,128)S(1)} %get-tuple-element.69.grad_one_ref, bf16[4,768,768]{2,1,0:T(8,128)(2,1)} %bitcast.148, bf16[4,512,576]{2,1,0:T(8,128)(2,1)} %get-tuple-element.70.qkv_ref, ...), custom_call_target="tpu_custom_call" | custom-call | flops 11274289152 | bytes 18874368 | tf_op jit(solution)/shard_map/attend_back/pallas_call | solution.py:390
  582.1 10.4 down_back.3
  592.5 10.3 hidden_back.3
  602.9 18.4 %attend_back.3 = (bf16[4,768,768]{2,1,0:T(8,128)(2,1)}, f32[512,768]{1,0:T(8,128)S(1)}, f32[4,1,576]{2,1,0:T(1,128)S(1)}) custom-call(bf16[512,768]{1,0:T(8,128)(2,1)S(1)} %copy-done.6, f32[512,768]{1,0:T(8,128)S(1)} %get-tuple-element.80.grad_one_ref, bf16[4,768,768]{2,1,0:T(8,128)(2,1)} %bitcast.144, bf16[4,512,576]{2,1,0:T(8,128)(2,1)} %get-tuple-element.81.qkv_ref, ...), custom_call_target="tpu_custom_call" | custom-call | flops 11274289152 | bytes 18874368 | tf_op jit(solution)/shard_map/attend_back/pallas_call | solution.py:390
  628.8 111.8 %all-reduce.4.cloned.1.call-done = f32[2,9984]{1,0:T(2,128)} async-done(((f32[2,9984]{1,0:T(2,128)}), f32[2,9984]{1,0:T(2,128)}) %all-reduce.4.cloned.1.call-update) | async-done | bytes 79888 | tf_op jit(solution)/shard_map/psum | solution.py:548
  753.1 102.0 %reduce-scatter.21.cloned.1.call-done = bf16[96,768]{1,0:T(8,128)(2,1)} async-done(((bf16[3072,768]{1,0:T(8,128)(2,1)}), bf16[96,768]{1,0:T(8,128)(2,1)}) %reduce-scatter.21.cloned.1.call-update) | async-done | bytes 147472
  856.2 111.2 %reduce-scatter.19.cloned.1.call-done = bf16[96,768]{1,0:T(8,128)(2,1)} async-done(((bf16[3072,768]{1,0:T(8,128)(2,1)}), bf16[96,768]{1,0:T(8,128)(2,1)}) %reduce-scatter.19.cloned.1.call-update) | async-done | bytes 147472
  970.5 108.5 %reduce-scatter.13.cloned.1.call-done = bf16[96,768]{1,0:T(8,128)(2,1)} async-done(((bf16[3072,768]{1,0:T(8,128)(2,1)}), bf16[96,768]{1,0:T(8,128)(2,1)}) %reduce-scatter.13.cloned.1.call-update) | async-done | bytes 147472 | tf_op jit(solution)/shard_map/reduce_scatter | solution.py:449
  1079.0 112.4 %reduce-scatter.11.cloned.1.call-done = bf16[96,768]{1,0:T(8,128)(2,1)} async-done(((bf16[3072,768]{1,0:T(8,128)(2,1)}), bf16[96,768]{1,0:T(8,128)(2,1)}) %reduce-scatter.11.cloned.1.call-update) | async-done | bytes 147472 | tf_op jit(solution)/shard_map/reduce_scatter | solution.py:449
  1193.2 109.7 %reduce-scatter.17.cloned.1.call-done = bf16[96,768]{1,0:T(8,128)(2,1)} async-done(((bf16[3072,768]{1,0:T(8,128)(2,1)}), bf16[96,768]{1,0:T(8,128)(2,1)}) %reduce-scatter.17.cloned.1.call-update) | async-done | bytes 147472 | tf_op jit(solution)/shard_map/reduce_scatter | solution.py:449
  1302.9 112.4 %reduce-scatter.15.cloned.1.call-done = bf16[96,768]{1,0:T(8,128)(2,1)} async-done(((bf16[3072,768]{1,0:T(8,128)(2,1)}), bf16[96,768]{1,0:T(8,128)(2,1)}) %reduce-scatter.15.cloned.1.call-update) | async-done | bytes 147472 | tf_op jit(solution)/shard_map/reduce_scatter | solution.py:449
  (204 shorter events, 74.0 us)
Async XLA Ops:
  7.2 130.2 %all-reduce.6.cloned.1.call-start = ((), (), s32[]{:S(2)}) async-start(), calls=%async_computation.17 | async-start | bytes 184320
  14.2 191.5 %all-gather.14.cloned.1.call-start = ((), (), s32[]{:S(2)}) async-start(), calls=%async_computation.11 | async-start | bytes 4866048 | tf_op jit(solution)/shard_map/all_gather | solution.py:444
  17.2 254.6 %all-gather.16.cloned.1.call-start = ((), (), s32[]{:S(2)}) async-start(), calls=%async_computation.12 | async-start | bytes 4866048 | tf_op jit(solution)/shard_map/all_gather | solution.py:444
  18.0 319.7 %all-gather.18.cloned.1.call-start = ((), (), s32[]{:S(2)}) async-start(), calls=%async_computation.13 | async-start | bytes 4866048 | tf_op jit(solution)/shard_map/all_gather | solution.py:444
  18.8 384.9 %all-gather.20.cloned.1.call-start = ((), (), s32[]{:S(2)}) async-start(), calls=%async_computation.14 | async-start | bytes 4866048 | tf_op jit(solution)/shard_map/all_gather | solution.py:444
  19.4 449.6 %all-gather.22.cloned.1.call-start = ((), (), s32[]{:S(2)}) async-start(), calls=%async_computation.15 | async-start | bytes 4866048 | tf_op jit(solution)/shard_map/all_gather | solution.py:444
  20.0 514.6 %all-gather.24.cloned.1.call-start = ((), (), s32[]{:S(2)}) async-start(), calls=%async_computation.16 | async-start | bytes 4866048 | tf_op jit(solution)/shard_map/all_gather | solution.py:444
  20.7 720.0 %all-reduce.4.cloned.1.call-start = ((), (), s32[]{:S(2)}) async-start(), calls=%async_computation.10 | async-start | bytes 159744 | tf_op jit(solution)/shard_map/psum | solution.py:548
  20.8 119.8 %collective-permute-start = (bf16[256,768]{1,0:T(8,128)(2,1)S(1)}, bf16[256,768]{1,0:T(8,128)(2,1)}, u32[]{:S(2)}, u32[]{:S(2)}) collective-permute-start(bf16[256,768]{1,0:T(8,128)(2,1)S(1)} %dynamic-slice_bitcast_fusion.1), channel_id=1, source_target_pairs={{0,1},{1,0},{2,3},{3,2},{4,5},{5,4},{6,7},{7,6},{8,9},{9,8},{10,11... | collective-permute-start | bytes 1179656 | tf_op jit(solution)/shard_map/ppermute | solution.py:423
  22.1 119.7 %collective-permute-start.2 = (bf16[256,768]{1,0:T(8,128)(2,1)}, bf16[256,768]{1,0:T(8,128)(2,1)S(1)}, u32[]{:S(2)}, u32[]{:S(2)}) collective-permute-start(bf16[256,768]{1,0:T(8,128)(2,1)} %dynamic-slice_bitcast_fusion), channel_id=1, source_target_pairs={{0,1},{1,0},{2,3},{3,2},{4,5},{5,4},{6,7},{7,6},{8,9},{9,8},{10,11... | collective-permute-start | bytes 1179656 | tf_op jit(solution)/shard_map/ppermute | solution.py:423
  141.8 63.9 %copy-start.5 = (bf16[512,768]{1,0:T(8,128)(2,1)}, bf16[512,768]{1,0:T(8,128)(2,1)S(1)}, u32[]{:S(2)}) copy-start(bf16[512,768]{1,0:T(8,128)(2,1)S(1)} %pad_maximum_fusion.2.x_ref) | copy-start | bytes 2359300
  221.8 57.6 %copy-start.19 = (f32[512,1]{1,0:T(8,128)}, f32[512,1]{1,0:T(8,128)S(1)}, u32[]{:S(2)}) copy-start(f32[512,1]{1,0:T(8,128)S(1)} %get-tuple-element.79.scale_ref) | copy-start | bytes 6148
  422.0 54.6 %copy-start.2 = (f32[512,768]{1,0:T(8,128)}, f32[512,768]{1,0:T(8,128)S(1)}, u32[]{:S(2)}) copy-start(f32[512,768]{1,0:T(8,128)S(1)} %get-tuple-element.58.normal_ref) | copy-start | bytes 4718596
  563.5 18.6 %copy-start.9 = (f32[512,768]{1,0:T(8,128)S(1)}, f32[512,768]{1,0:T(8,128)}, u32[]{:S(2)}) copy-start(f32[512,768]{1,0:T(8,128)} %copy-done.8) | copy-start | bytes 4718596
  563.5 18.6 %copy-start.14 = (f32[512,1]{1,0:T(8,128)S(1)}, f32[512,1]{1,0:T(8,128)}, u32[]{:S(2)}) copy-start(f32[512,1]{1,0:T(8,128)} %copy-done.13) | copy-start | bytes 6148
  602.9 18.7 %copy-start.33 = (f32[19968]{0:T(1024)S(1)}, f32[19968]{0:T(1024)}, u32[]{:S(2)}) copy-start(f32[19968]{0:T(1024)} %custom-call) | copy-start | bytes 239620
  622.5 232.6 %reduce-scatter.21.cloned.1.call-start = ((), (), s32[]{:S(2)}) async-start(), calls=%async_computation.19 | async-start | bytes 4866048
  623.2 344.2 %reduce-scatter.19.cloned.1.call-start = ((), (), s32[]{:S(2)}) async-start(), calls=%async_computation.18 | async-start | bytes 4866048
  623.8 455.2 %reduce-scatter.13.cloned.1.call-start = ((), (), s32[]{:S(2)}) async-start(), calls=%async_computation.7 | async-start | bytes 4866048 | tf_op jit(solution)/shard_map/reduce_scatter | solution.py:449
  624.5 566.8 %reduce-scatter.11.cloned.1.call-start = ((), (), s32[]{:S(2)}) async-start(), calls=%async_computation.6 | async-start | bytes 4866048 | tf_op jit(solution)/shard_map/reduce_scatter | solution.py:449
  625.1 677.8 %reduce-scatter.17.cloned.1.call-start = ((), (), s32[]{:S(2)}) async-start(), calls=%async_computation.9 | async-start | bytes 4866048 | tf_op jit(solution)/shard_map/reduce_scatter | solution.py:449
  625.8 789.4 %reduce-scatter.15.cloned.1.call-start = ((), (), s32[]{:S(2)}) async-start(), calls=%async_computation.8 | async-start | bytes 4866048 | tf_op jit(solution)/shard_map/reduce_scatter | solution.py:449
  627.4 120.7 %collective-permute-start.1 = (f32[256,768]{1,0:T(8,128)}, f32[256,768]{1,0:T(8,128)}, u32[]{:S(2)}, u32[]{:S(2)}) collective-permute-start(f32[256,768]{1,0:T(8,128)} %constant_dynamic-slice_fusion.4), channel_id=1, source_target_pairs={{0,1},{1,0},{2,3},{3,2},{4,5},{5,4},{6,7},{7,6},{8,9},{9,8},{10,11... | collective-permute-start | bytes 2359304 | tf_op jit(solution)/shard_map/ppermute | solution.py:423
  628.6 122.0 %collective-permute-start.3 = (f32[256,768]{1,0:T(8,128)}, f32[256,768]{1,0:T(8,128)}, u32[]{:S(2)}, u32[]{:S(2)}) collective-permute-start(f32[256,768]{1,0:T(8,128)} %constant_dynamic-slice_fusion.3), channel_id=1, source_target_pairs={{0,1},{1,0},{2,3},{3,2},{4,5},{5,4},{6,7},{7,6},{8,9},{9,8},{10,11... | collective-permute-start | bytes 2359304 | tf_op jit(solution)/shard_map/ppermute | solution.py:423
  (28 other events, 140.1 us)
Sparse Core Ops, SparseCore 0:
  14.3 123.0 all-reduce.5
  141.0 64.6 all-gather.13
  209.3 62.4 all-gather.15
  275.2 62.4 all-gather.17
  341.1 62.4 all-gather.19
  406.5 62.4 all-gather.21
  472.0 62.4 all-gather.23
  622.6 118.0 all-reduce.3
  746.2 108.8 reduce-scatter.20
  861.3 106.0 reduce-scatter.18
  972.9 106.0 reduce-scatter.12
  1085.2 106.0 reduce-scatter.10
  1196.8 106.0 reduce-scatter.16
  1309.1 106.0 reduce-scatter.14

commit v2 on v1

v2 whole, which is shorter than its diff:
```python
from functools import partial

import jax
import jax.numpy as jnp
from jax import lax
from jax.experimental import pallas as pl
from jax.experimental.pallas import tpu as pltpu
from jax.sharding import PartitionSpec as P

HD = 64
NORM_EPSILON = 1e-12
MASK_VALUE = -1000000000.0
F32 = jnp.float32
BF16 = jnp.bfloat16
STREAM_BYTES = 60 * 1024 * 1024
MERGE_BYTES = 32 * 1024 * 1024
FORWARD_SCALE, BACKWARD_SCALE = 0.25, 2000


def lasting(microseconds, scale):
    return pl.CostEstimate(flops=int(1.15e9 * microseconds * scale), bytes_accessed=0, transcendentals=0)


ROOT_HALF = 0.7071067811865476
ROOT_TWO_PI = 0.3989422804014327

LINE = (1, 3, 0, 2)

GATHERED = (1,)
SCATTERED = ((1, 1),)


def dot_nn(left, right):
    return lax.dot_general(left, right, (((1,), (0,)), ((), ())), preferred_element_type=F32)


def dot_nt(left, right):
    return lax.dot_general(left, right, (((1,), (1,)), ((), ())), preferred_element_type=F32)


def dot_tn(left, right):
    return lax.dot_general(left, right, (((0,), (0,)), ((), ())), preferred_element_type=F32)


def normed_rows(values):
    centre = values - jnp.mean(values, axis=-1, keepdims=True)
    spread = jnp.mean(centre * centre, axis=-1, keepdims=True)
    scale = lax.rsqrt(spread + NORM_EPSILON)
    return centre * scale, scale


def norm_back(upstream, normal, scale, gain):
    grad = upstream * gain
    mean_grad = jnp.mean(grad, axis=-1, keepdims=True)
    mean_both = jnp.mean(grad * normal, axis=-1, keepdims=True)
    return scale * (grad - mean_grad - normal * mean_both)


def token_sums(upstream, normal, result):
    return jnp.concatenate(
        [
            jnp.sum(upstream * normal, axis=0, keepdims=True),
            jnp.sum(upstream, axis=0, keepdims=True),
            jnp.sum(result, axis=0, keepdims=True),
        ],
        axis=0,
    )


def turned(values):
    return values.astype(F32).T.astype(BF16)


ANYWHERE = pl.BlockSpec(memory_space=pl.ANY)
IN_VMEM = pl.BlockSpec(memory_space=pltpu.VMEM)
IN_SMEM = pl.BlockSpec(memory_space=pltpu.SMEM)


def shaped(shape, dtype):
    return jax.ShapeDtypeStruct(tuple(shape), dtype)


class Rows:
    def __init__(self, array, split=False):
        self.operands = [array]
        self.scratch = [
            pltpu.VMEM(array.shape, array.dtype),
            pltpu.SemaphoreType.DMA((array.shape[0] if split else 1,)),
        ]

    def bind(self, refs, scratch, table):
        (self.ref,), (self.held, self.sems) = refs, scratch
        return self

    def copy(self, index):
        if index is None:
            return pltpu.make_async_copy(self.ref, self.held, self.sems.at[0])
        return pltpu.make_async_copy(self.ref.at[index], self.held.at[index], self.sems.at[index])

    def start(self, index=None):
        self.copy(index).start()

    def wait(self, index=None):
        self.copy(index).wait()


class Weights:
    def __init__(self, group, start, width):
        self.group, self.cols = group, pl.ds(group.start + start, width)
        self.operands = list(group.arrays)
        model = group.model
        self.scratch = [
            pltpu.VMEM((len(LINE), model, width), BF16),
            pltpu.SemaphoreType.DMA((len(LINE), len(group.places) if group.common else 1)),
        ]

    def bind(self, refs, scratch, table):
        self.refs, (self.held, self.sems), self.table = refs, scratch, table
        return self

    def copies(self, index):
        if not self.group.common:
            yield pltpu.make_async_copy(
                self.refs[index].at[:, self.cols], self.held.at[index], self.sems.at[index, 0]
            )
            return
        places = len(self.group.places)
        piece = self.group.model // places
        for place in range(places):
            row = pl.multiple_of(self.table[index] + self.table[len(LINE) + place], piece)
            yield pltpu.make_async_copy(
                self.refs[0].at[pl.ds(row, piece), self.cols],
                self.held.at[index, pl.ds(place * piece, piece)],
                self.sems.at[index, place],
            )

    def start(self, index):
        for copy in self.copies(index):
            copy.start()

    def wait(self, index):
        for copy in self.copies(index):
            copy.wait()


class Result:
    def __init__(self, shape, dtype, split=False):
        self.shapes = [shaped(shape, dtype)]
        self.indices = range(shape[0]) if split else (None,)
        self.scratch = [
            pltpu.VMEM(shape, dtype),
            pltpu.SemaphoreType.DMA((shape[0] if split else 1,)),
        ]

    def bind(self, refs, scratch, table):
        (self.ref,), (self.held, self.sems) = refs, scratch
        return self

    def copy(self, index):
        if index is None:
            return pltpu.make_async_copy(self.held, self.ref, self.sems.at[0])
        return pltpu.make_async_copy(self.held.at[index], self.ref.at[index], self.sems.at[index])

    def start(self, index=None):
        self.copy(index).start()

    def finish(self):
        for index in self.indices:
            self.copy(index).wait()


class Grads:
    def __init__(self, model, width, places, common):
        self.model, self.places, self.common = model, places, common
        teams = len(LINE)
        if common:
            self.shapes = [shaped((teams * model, width), BF16)]
        else:
            self.shapes = [shaped((2, model, width), BF16)] * 2
        self.scratch = [
            pltpu.VMEM((teams, model, width), BF16),
            pltpu.SemaphoreType.DMA((teams, len(places) if common else 1)),
        ]

    def bind(self, refs, scratch, table):
        self.refs, (self.held, self.sems), self.table = refs, scratch, table
        return self

    def copies(self, index):
        if not self.common:
            yield pltpu.make_async_copy(
                self.held.at[index], self.refs[index // 2].at[index % 2], self.sems.at[index, 0]
            )
            return
        places = len(self.places)
        piece = self.model // places
        for place in range(places):
            row = pl.multiple_of(self.table[index] + self.table[len(LINE) + place], piece)
            yield pltpu.make_async_copy(
                self.held.at[index, pl.ds(place * piece, piece)],
                self.refs[0].at[pl.ds(row, piece)],
                self.sems.at[index, place],
            )

    def start(self, index):
        for copy in self.copies(index):
            copy.start()

    def finish(self):
        for index in range(len(LINE)):
            for copy in self.copies(index):
                copy.wait()


def streamed(body, name, table, ins, outs, scratch=(), after=(), lasts=15, scale=FORWARD_SCALE):
    waits = len(after)
    operands = [array for item in ins for array in item.operands]
    shapes = [shape for item in outs for shape in item.shapes]

    def wrapped(*refs):
        refs = list(refs)

        def take(count):
            taken = refs[:count]
            del refs[:count]
            return taken

        (table_ref,) = take(1)
        in_refs = [take(len(item.operands)) for item in ins]
        take(waits)
        out_refs = [take(len(item.shapes)) for item in outs]
        (token_ref,) = take(1)
        token_ref[...] = jnp.zeros((8, 128), F32)
        inlets = [item.bind(own, take(len(item.scratch)), table_ref) for item, own in zip(ins, in_refs)]
        outlets = [item.bind(own, take(len(item.scratch)), table_ref) for item, own in zip(outs, out_refs)]
        body(inlets, outlets, *refs)
        for outlet in outlets:
            outlet.finish()

    kernel = pl.pallas_call(
        wrapped,
        in_specs=[IN_SMEM] + [ANYWHERE] * (len(operands) + waits),
        out_specs=[ANYWHERE] * len(shapes) + [IN_VMEM],
        out_shape=shapes + [shaped((8, 128), F32)],
        scratch_shapes=[entry for item in list(ins) + list(outs) for entry in item.scratch] + list(scratch),
        compiler_params=pltpu.CompilerParams(vmem_limit_bytes=STREAM_BYTES),
        cost_estimate=lasting(lasts, scale),
        name=name,
    )
    return kernel(table, *operands, *after)


def attend_body(inlets, outlets, low_ref):
    x, doc_col, doc_row, vec, q_bias, v_bias, weights = inlets
    qkv, prob, context, normal_out, scale_out = outlets
    steps, _, width = q_bias.held.shape
    heads = width // HD
    for inlet in (doc_col, doc_row, vec, q_bias, v_bias, x):
        inlet.start()
    weights.start(0)
    weights.start(1)
    for inlet in (doc_col, doc_row, vec, q_bias, v_bias, x):
        inlet.wait()
    low_ref[...] = x.held[...].astype(BF16)
    total = x.held[...].astype(F32) + vec.held[0:1]
    same_doc = doc_col.held[...] == doc_row.held[...]
    for step in range(steps):
        weights.wait(step)
        if step + 2 < steps:
            weights.start(step + 2)
        projected = dot_nn(low_ref[...], weights.held[step, :, : 3 * width])
        queries = (projected[:, :width] + q_bias.held[step]).astype(BF16) * jnp.asarray(0.125, BF16)
        key_rows = projected[:, width : 2 * width].astype(BF16)
        value_full = projected[:, 2 * width :] + v_bias.held[step]
        qkv.held[step, :, :width] = queries
        qkv.held[step, :, width : 2 * width] = key_rows
        qkv.held[step, :, 2 * width :] = value_full.astype(BF16)
        qkv.start(step)
        value_turned = turned(value_full)
        parts = []
        for head in range(heads):
            cols = slice(head * HD, (head + 1) * HD)
            scores = jnp.where(same_doc, dot_nt(key_rows[:, cols], queries[:, cols]), MASK_VALUE)
            expo = jnp.exp(scores - jnp.max(scores, axis=0, keepdims=True))
            chances = (expo * (1.0 / jnp.sum(expo, axis=0, keepdims=True))).astype(BF16)
            prob.held[step * heads + head] = chances
            prob.start(step * heads + head)
            parts.append(dot_nn(value_turned[cols], chances))
        context_turned = jnp.concatenate(parts, axis=0)
        context.held[step] = context_turned.astype(BF16)
        context.start(step)
        total = total + dot_nt(context_turned.T.astype(BF16), weights.held[step, :, 3 * width :])
    normal, scale = normed_rows(total)
    normal_out.held[...] = normal
    scale_out.held[...] = scale
    normal_out.start()
    scale_out.start()


def attend(table, x, weights, q_bias, v_bias, vec, doc_ids, after=()):
    steps, width = q_bias.shape[0], q_bias.shape[2]
    rows, model = x.shape
    heads = width // HD
    return streamed(
        attend_body,
        "attend",
        table,
        [
            Rows(x), Rows(doc_ids.reshape(rows, 1)), Rows(doc_ids.reshape(1, rows)), Rows(vec), Rows(q_bias),
            Rows(v_bias), Weights(weights, 0, 4 * width),
        ],
        [
            Result((steps, rows, 3 * width), BF16, True),
            Result((steps * heads, rows, rows), BF16, True),
            Result((steps, width, rows), BF16, True),
            Result((rows, model), F32),
            Result((rows, 1), F32),
        ],
        [pltpu.VMEM((rows, model), BF16)],
        after=after,
    )


def forward_body(inlets, outlets, low_ref):
    normal, vec, vec_two, bias, first, second = inlets
    low_out, active, slope, out, normal_two, scale_two = outlets
    steps = bias.held.shape[0]
    for inlet in (vec, vec_two, bias, normal):
        inlet.start()
    for step in range(2):
        first.start(step)
        second.start(step)
    for inlet in (vec, vec_two, bias, normal):
        inlet.wait()
    rows = normal.held[...] * vec.held[1:2] + vec.held[2:3]
    low_ref[...] = rows.astype(BF16)
    low_out.held[...] = rows.astype(BF16)
    low_out.start()
    total = rows + vec_two.held[0:1]
    for step in range(steps):
        first.wait(step)
        second.wait(step)
        if step + 2 < steps:
            first.start(step + 2)
            second.start(step + 2)
        hidden = dot_nn(low_ref[...], first.held[step]) + bias.held[step]
        below = 0.5 + 0.5 * lax.erf(hidden * ROOT_HALF)
        value = (hidden * below).astype(BF16)
        active.held[step] = value
        slope.held[step] = (below + hidden * (jnp.exp(hidden * hidden * -0.5) * ROOT_TWO_PI)).astype(BF16)
        active.start(step)
        slope.start(step)
        total = total + dot_nt(value, second.held[step])
    normal_value, scale = normed_rows(total)
    normal_two.held[...] = normal_value
    scale_two.held[...] = scale
    out.held[...] = normal_value * vec_two.held[1:2] + vec_two.held[2:3]
    for outlet in (normal_two, scale_two, out):
        outlet.start()


def forward(table, normal, vec, vec_two, bias, first, second, after=()):
    steps, _, width = bias.shape
    rows, model = normal.shape
    return streamed(
        forward_body,
        "forward",
        table,
        [
            Rows(normal), Rows(vec), Rows(vec_two), Rows(bias),
            Weights(first, 0, width), Weights(second, 0, width),
        ],
        [
            Result((rows, model), BF16),
            Result((steps, rows, width), BF16, True),
            Result((steps, rows, width), BF16, True),
            Result((rows, model), F32),
            Result((rows, model), F32),
            Result((rows, 1), F32),
        ],
        [pltpu.VMEM((rows, model), BF16)],
        after=after,
    )


def forward_back_body(inlets, outlets, low_two_ref):
    up, normal_two, scale_two, vec_two, active, slope, second, first, low, normal, scale, vec = inlets
    grads, grad_one, sums_two, sums_one, unit_sums = outlets
    steps, _, width = active.held.shape
    for inlet in (scale_two, vec_two, up, normal_two):
        inlet.start()
    for inlet in (scale_two, vec_two, up, normal_two):
        inlet.wait()

    def bring(step):
        for inlet in (active, second, slope, first):
            inlet.start(step)

    bring(0)
    low.start()
    bring(1)
    upstream, normal_value = up.held[...].astype(F32), normal_two.held[...]
    grad = norm_back(upstream, normal_value, scale_two.held[...], vec_two.held[1:2])
    low_two_ref[...] = grad.astype(BF16)
    total = grad
    sums_two.held[...] = token_sums(upstream, normal_value, grad)
    sums_two.start()
    for step in range(steps):
        for inlet in (active, second, slope, first):
            inlet.wait(step)
        if step == 0:
            low.wait()
        if step + 2 < steps:
            bring(step + 2)
        elif step + 2 == steps:
            for inlet in (scale, vec, normal):
                inlet.start()
        grads.held[step, :, width:] = dot_tn(low_two_ref[...], active.held[step]).astype(BF16)
        value = (dot_nn(low_two_ref[...], second.held[step]) * slope.held[step].astype(F32)).astype(BF16)
        unit_sums.held[step] = jnp.sum(value.astype(F32), axis=0, keepdims=True)
        grads.held[step, :, :width] = dot_tn(low.held[...], value).astype(BF16)
        grads.start(step)
        unit_sums.start(step)
        total = total + dot_nt(value, first.held[step])
    for inlet in (scale, vec, normal):
        inlet.wait()
    normal_value = normal.held[...]
    grad = norm_back(total, normal_value, scale.held[...], vec.held[1:2])
    grad_one.held[...] = grad
    sums_one.held[...] = token_sums(total, normal_value, grad)
    grad_one.start()
    sums_one.start()


def forward_back(
    table, upstream, normal_two, scale_two, vec_two, active, slope, first, second, low, normal, scale, vec, common,
    after=(),
):
    steps, rows, width = active.shape
    model = low.shape[1]
    return streamed(
        forward_back_body,
        "forward_back",
        table,
        [
            Rows(upstream), Rows(normal_two), Rows(scale_two), Rows(vec_two), Rows(active, True), Rows(slope, True),
            Weights(second, 0, width), Weights(first, 0, width), Rows(low), Rows(normal), Rows(scale), Rows(vec),
        ],
        [
            Grads(model, 2 * width, first.places, common),
            Result((rows, model), F32),
            Result((3, model), F32),
            Result((3, model), F32),
            Result((steps, 1, width), F32, True),
        ],
        [pltpu.VMEM((rows, model), BF16)],
        after=after,
        lasts=19,
        scale=BACKWARD_SCALE,
    )


def attend_back_body(inlets, outlets, low_ref, x_low_ref):
    x, grad_one, qkv, prob, context, weights = inlets
    grads, grad_x, sums = outlets
    steps, width, _ = context.held.shape
    heads = prob.held.shape[0] // steps

    def bring(step):
        weights.start(step)
        qkv.start(step)
        for head in range(heads):
            prob.start(step * heads + head)
        context.start(step)

    grad_one.start()
    bring(0)
    x.start()
    bring(1)
    grad_one.wait()
    low_ref[...] = grad_one.held[...].astype(BF16)
    total = grad_one.held[...]
    for step in range(steps):
        weights.wait(step)
        qkv.wait(step)
        context.wait(step)
        for head in range(heads):
            prob.wait(step * heads + head)
        if step == 0:
            x.wait()
            x_low_ref[...] = x.held[...].astype(BF16)
        if step + 2 < steps:
            bring(step + 2)
        block = qkv.held[step]
        queries, key_rows = block[:, :width], block[:, width : 2 * width]
        value_rows = block[:, 2 * width :]
        key_turned = turned(key_rows)
        grad_context = dot_nn(low_ref[...], weights.held[step, :, 3 * width :]).astype(BF16)
        grad_q, grad_k, grad_v = [], [], []
        for head in range(heads):
            cols = slice(head * HD, (head + 1) * HD)
            low_weights = prob.held[step * heads + head]
            chances = low_weights.astype(F32)
            part = chances * dot_nt(value_rows[:, cols], grad_context[:, cols])
            centre = jnp.sum(part, axis=0, keepdims=True)
            grad_scores = (part - chances * centre).astype(BF16)
            grad_v.append(dot_nn(low_weights, grad_context[:, cols]))
            grad_k.append(dot_nn(grad_scores, queries[:, cols]))
            grad_q.append(dot_nn(key_turned[cols], grad_scores))
        stacked = jnp.concatenate(
            [(jnp.concatenate(grad_q, axis=0) * 0.125).T] + grad_k + grad_v, axis=1
        ).astype(BF16)
        grads.held[step, :, : 3 * width] = dot_tn(x_low_ref[...], stacked).astype(BF16)
        grads.held[step, :, 3 * width :] = dot_tn(low_ref[...], turned(context.held[step])).astype(BF16)
        grads.start(step)
        total = total + dot_nt(stacked, weights.held[step, :, : 3 * width])
        sums.held[step] = jnp.sum(stacked.astype(F32), axis=0, keepdims=True)
        sums.start(step)
    grad_x.held[...] = total
    grad_x.start()


def attend_back(table, x, grad_one, weights, qkv, prob, context, common, after=()):
    steps, width, rows = context.shape
    model = x.shape[1]
    return streamed(
        attend_back_body,
        "attend_back",
        table,
        [
            Rows(x), Rows(grad_one), Rows(qkv, True), Rows(prob, True), Rows(context, True),
            Weights(weights, 0, 4 * width),
        ],
        [
            Grads(model, 4 * width, weights.places, common),
            Result((rows, model), F32),
            Result((steps, 1, 3 * width), F32, True),
        ],
        [pltpu.VMEM((rows, model), BF16), pltpu.VMEM((rows, model), BF16)],
        after=after,
        lasts=22,
        scale=BACKWARD_SCALE,
    )


def whole(shape):
    return pl.BlockSpec(shape, lambda t: (0,) * len(shape))


def call(body, name, steps, in_specs, out_specs, out_shape, scratch, flops, moved, after=(), token=False):
    single = not isinstance(out_shape, list)
    out_specs = [out_specs] if single else list(out_specs)
    out_shape = [out_shape] if single else list(out_shape)
    inputs, outputs, waits = len(in_specs), len(out_shape), len(after)
    if token:
        out_specs.append(whole((8, 128)))
        out_shape.append(shaped((8, 128), F32))

    def wrapped(*refs):
        made = refs[inputs + waits :]
        if token:
            made[outputs][...] = jnp.zeros((8, 128), F32)
        body(*refs[:inputs], *made[:outputs], *made[outputs + token :])

    kernel = pl.pallas_call(
        wrapped,
        grid=(steps,),
        in_specs=list(in_specs) + [ANYWHERE] * waits,
        out_specs=out_specs,
        out_shape=out_shape,
        scratch_shapes=scratch,
        compiler_params=pltpu.CompilerParams(
            dimension_semantics=("arbitrary",), vmem_limit_bytes=MERGE_BYTES
        ),
        cost_estimate=lasting(2, BACKWARD_SCALE),
        name=name,
    )

    def run(*args):
        made = kernel(*args, *after)
        if not single or token:
            return made
        return made[0]

    return run


def reorder_kernel(values_ref, place_ref, out_ref):
    values = values_ref[...]
    high = values.astype(BF16)
    low = (values - high.astype(F32)).astype(BF16)
    place = place_ref[...]
    out_ref[...] = dot_nt(high, place) + dot_nt(low, place)


def reorder(values, place, after=()):
    rows, model = values.shape
    return call(
        reorder_kernel,
        "reorder",
        1,
        [whole((rows, model)), whole((model, model))],
        whole((rows, model)),
        shaped((rows, model), F32),
        [],
        4 * rows * model * model,
        8 * rows * model,
        after=after,
    )(values, place)


def dp_bits(parts):
    return list(range(1, parts.bit_length() - 1)) + [0]


def dp_places(parts):
    bits = dp_bits(parts)
    return [sum(((place >> k) & 1) << bit for k, bit in enumerate(bits)) for place in range(parts)]


def trade(values, axis, bit):
    return lax.ppermute(values, axis, [(i, i ^ (1 << bit)) for i in range(lax.axis_size(axis))])


def swap_cores(values):
    return trade(values, "tensor", 0)


def to_sequence(blocks, core):
    mine = lax.dynamic_index_in_dim(blocks, core, 0, keepdims=False)
    other = lax.dynamic_index_in_dim(blocks, 1 - core, 0, keepdims=False)
    got = swap_cores(other)
    return jnp.concatenate(
        [jnp.where(core == 0, mine, got), jnp.where(core == 0, got, mine)], axis=0
    )


def from_sequence(values, core):
    half = values.shape[0] // 2
    mine = lax.dynamic_slice_in_dim(values, core * half, half, 0)
    got = swap_cores(lax.dynamic_slice_in_dim(values, (1 - core) * half, half, 0))
    return jnp.stack([jnp.where(core == 0, mine, got), jnp.where(core == 0, got, mine)])


def joined(*blocks):
    return jnp.concatenate(blocks, axis=0)


def gated(values, token):
    return values if token is None else values + token[0, 0].astype(values.dtype)


class Group:
    def __init__(self, arrays, model, places, common):
        self.arrays, self.model, self.places, self.common = arrays, model, places, common
        self.start = 0


def mark(*arrays):
    def body(*refs):
        refs[-1][...] = jnp.zeros((8, 128), F32)

    return pl.pallas_call(
        body,
        in_specs=[ANYWHERE] * len(arrays),
        out_specs=IN_VMEM,
        out_shape=shaped((8, 128), F32),
        cost_estimate=lasting(0.5, FORWARD_SCALE),
        name="mark",
    )(*arrays)


def moved(plan, after):
    arrays = []
    for parts in plan:
        for array, _, _ in parts:
            if not any(array is other for other in arrays):
                arrays.append(array)
    steps = []
    for out, parts in enumerate(plan):
        at = 0
        for array, start, rows in parts:
            source = [array is other for other in arrays].index(True)
            steps.append((source, start, out, at, rows))
            at += rows
    shapes = [
        shaped((sum(rows for _, _, rows in parts),) + parts[0][0].shape[1:], parts[0][0].dtype) for parts in plan
    ]
    count, waits = len(arrays), len(after)

    def body(*refs):
        refs = list(refs)
        sources, results = refs[:count], refs[count + waits : count + waits + len(plan)]
        token_ref, *held = refs[count + waits + len(plan) : -2]
        sems, out_sems = refs[-2:]
        token_ref[...] = jnp.zeros((8, 128), F32)
        brought = [
            pltpu.make_async_copy(
                sources[source].at[pl.ds(start, rows)], held[out].at[pl.ds(at, rows)], sems.at[k]
            )
            for k, (source, start, out, at, rows) in enumerate(steps)
        ]
        for copy in brought:
            copy.start()
        for copy in brought:
            copy.wait()
        given = [pltpu.make_async_copy(held[k], results[k], out_sems.at[k]) for k in range(len(plan))]
        for copy in given:
            copy.start()
        for copy in given:
            copy.wait()

    return pl.pallas_call(
        body,
        in_specs=[ANYWHERE] * (count + waits),
        out_specs=[ANYWHERE] * len(shapes) + [IN_VMEM],
        out_shape=shapes + [shaped((8, 128), F32)],
        scratch_shapes=[pltpu.VMEM(shape.shape, shape.dtype) for shape in shapes]
        + [pltpu.SemaphoreType.DMA((len(steps),)), pltpu.SemaphoreType.DMA((len(plan),))],
        compiler_params=pltpu.CompilerParams(vmem_limit_bytes=MERGE_BYTES),
        cost_estimate=lasting(2, FORWARD_SCALE),
        name="moved",
    )(*arrays, *after)


def built(plan, after, fine):
    if fine:
        *made, token = moved(plan, after)
        return made, token
    token = mark(*after) if after else None
    made = [joined(*[gated(array[start : start + rows], token) for array, start, rows in parts]) for parts in plan]
    return made, mark(*made)


def gather_group(shard, places):
    parts = len(places)
    bits = dp_bits(parts)
    fine = shard.shape[0] % 16 == 0
    block = shard
    for bit in bits[:-1]:
        got = trade(block, "dp", bit)
        after = yield None
        rows = block.shape[0]
        (block,), token = built([[(block, 0, rows), (got, 0, rows)]], after, fine)
        yield token
    half = block.shape[0] // 2
    beyond = trade(block, "dp", bits[-1])
    across = trade(block, "tensor", 1)
    after = yield None
    (low, high), token = built([[(across, 0, half)], [(beyond, half, half)]], after, fine)
    yield token
    far_low = trade(low, "dp", bits[-1])
    far_high = trade(high, "tensor", 1)
    after = yield None
    (mine, across), token = built(
        [[(block, 0, 2 * half), (beyond, 0, 2 * half)], [(across, 0, 2 * half), (far_low, 0, half), (far_high, 0, half)]],
        after, fine,
    )
    yield token
    yield Group([swap_cores(mine), swap_cores(across), mine, across], mine.shape[0], places, False)


def gather_flat(flat, parts):
    for bit in dp_bits(parts):
        flat = joined(flat, trade(flat, "dp", bit))
    flat = joined(flat, trade(flat, "tensor", 1))
    return joined(swap_cores(flat), flat).reshape(len(LINE), parts, -1)


def gather_common(shards, places, place_rows):
    parts = len(places)
    piece = shards[0].shape[0]
    model = parts * piece
    got = lax.all_gather(jnp.concatenate(shards, axis=1), ("tensor", "dp"), axis=0, tiled=True)
    groups, start = [], 0
    for shard in shards:
        width = shard.shape[1]
        if piece % 16:
            own = got[:, start : start + width].reshape(len(LINE), parts, piece, width)
            own = own[place_rows[0]][:, place_rows[1]].reshape(len(LINE), model, width)
            groups.append(Group([own[i] for i in range(len(LINE))], model, places, False))
        else:
            groups.append(Group([got], model, places, True))
            groups[-1].start = start
        start += width
    return groups


def added(left, right):
    return left.astype(F32) + right.astype(F32)


def merge_core_kernel(keep_ref, got_ref, across_ref, mine_a_ref, beyond_ref, mine_b_ref):
    total = added(keep_ref[...], got_ref[...]).astype(BF16)

    @pl.when(pl.program_id(0) == 0)
    def _():
        across_ref[...] = total[1]
        mine_a_ref[...] = total[0]

    @pl.when(pl.program_id(0) == 1)
    def _():
        beyond_ref[...] = total[:, 1]
        mine_b_ref[...] = total[:, 0]


def merge_core(keep, got, token):
    _, rows, width = keep.shape
    fourth = rows // 4
    view = (2, 2, 2, fourth, width)
    spec = pl.BlockSpec((2, 2, None, fourth, width), lambda t: (0, 0, t, 0, 0))
    return call(
        merge_core_kernel,
        "merge_core",
        2,
        [spec, spec],
        [whole((2, fourth, width))] * 4,
        [shaped((2, fourth, width), BF16)] * 4,
        [],
        keep.size,
        keep.size * 6,
        after=() if token is None else (token,),
        token=True,
    )(keep.reshape(view), got.reshape(view))


def merge_sides_kernel(a_ref, got_a_ref, b_ref, got_b_ref, keep_a_ref, send_a_ref, keep_b_ref, send_b_ref):
    keep_a_ref[...] = added(a_ref[0], got_a_ref[0]).astype(BF16)
    send_a_ref[...] = added(a_ref[1], got_a_ref[1]).astype(BF16)
    keep_b_ref[...] = added(b_ref[0], got_b_ref[0]).astype(BF16)
    send_b_ref[...] = added(b_ref[1], got_b_ref[1]).astype(BF16)


def merge_sides(a, got_a, b, got_b, token):
    _, rows, width = a.shape
    return call(
        merge_sides_kernel,
        "merge_sides",
        1,
        [whole((2, rows, width))] * 4,
        [whole((rows, width))] * 4,
        [shaped((rows, width), BF16)] * 4,
        [],
        a.size,
        a.size * 12,
        after=() if token is None else (token,),
        token=True,
    )(a, got_a, b, got_b)


def merge_pair_kernel(a_ref, got_a_ref, b_ref, got_b_ref, out_a_ref, out_b_ref):
    out_a_ref[...] = added(a_ref[...], got_a_ref[...]).astype(BF16)
    out_b_ref[...] = added(b_ref[...], got_b_ref[...]).astype(BF16)


def merge_pair(a, got_a, b, got_b, token):
    rows, width = a.shape
    return call(
        merge_pair_kernel,
        "merge_pair",
        1,
        [whole((rows, width))] * 4,
        [whole((rows, width))] * 2,
        [shaped((rows, width), BF16)] * 2,
        [],
        a.size,
        a.size * 12,
        after=() if token is None else (token,),
        token=True,
    )(a, got_a, b, got_b)


def merge_halves_kernel(a_ref, got_ref, keep_ref, send_ref):
    half = keep_ref.shape[0]
    keep_ref[...] = added(a_ref[:half], got_ref[:half]).astype(BF16)
    send_ref[...] = added(a_ref[half:], got_ref[half:]).astype(BF16)


def merge_halves(a, got, token):
    rows, width = a.shape
    return call(
        merge_halves_kernel,
        "merge_halves",
        1,
        [whole((rows, width))] * 2,
        [whole((rows // 2, width))] * 2,
        [shaped((rows // 2, width), BF16)] * 2,
        [],
        a.size,
        a.size * 6,
        after=() if token is None else (token,),
        token=True,
    )(a, got)


def scatter_group(send, keep, parts):
    bits = dp_bits(parts)
    got = swap_cores(send)
    token = yield None
    across, mine_a, beyond, mine_b, ran = merge_core(keep, got, token)
    got_a, got_b = trade(across, "tensor", 1), trade(beyond, "dp", bits[-1])
    token = yield ran
    keep_a, send_a, keep_b, send_b, ran = merge_sides(mine_a, got_a, mine_b, got_b, token)
    got_a, got_b = trade(send_a, "dp", bits[-1]), trade(send_b, "tensor", 1)
    token = yield ran
    keep, send, ran = merge_pair(keep_a, got_a, keep_b, got_b, token)
    for bit in reversed(bits[1:-1]):
        got = trade(send, "dp", bit)
        token = yield ran
        keep, send, ran = merge_halves(keep, got, token)
    got = trade(send, "dp", bits[0])
    token = yield ran
    yield added(keep, gated(got, token))


def on_device(
    tokens, cotangent, segment_ids, qkv_weight, out_weight, in_weight, down_weight,
    qv_bias, in_bias, row_bias, norm_gain, norm_shift,
):
    teams, parts = lax.axis_size("tensor"), lax.axis_size("dp")
    layers, _, piece, width = qkv_weight.shape
    heads = width // HD
    model = piece * parts
    units = in_weight.shape[2]
    tensor_at, dp_at = lax.axis_index("tensor"), lax.axis_index("dp")
    core = tensor_at % 2

    places = dp_places(parts)
    back = [places.index(i) for i in range(parts)]
    place_of = jnp.asarray(back)[jnp.arange(parts) ^ dp_at]
    line_of = jnp.asarray([LINE.index(i) for i in range(teams)])[jnp.arange(teams) ^ tensor_at]
    column = jnp.arange(model)
    source = (jnp.asarray(places)[column // piece] ^ dp_at) * piece + column % piece
    place = (column[:, None] == source[None, :]).astype(BF16)

    starts = (jnp.asarray(LINE) ^ tensor_at) * model
    rows = (jnp.asarray(places) ^ dp_at) * piece
    table = jnp.concatenate([starts, rows]).astype(jnp.int32)
    from_common = (jnp.asarray(LINE) ^ tensor_at, jnp.asarray(places) ^ dp_at)

    out_turned = jnp.swapaxes(out_weight, 1, 2)
    down_turned = jnp.swapaxes(down_weight, 1, 2)
    shards = []
    for layer in range(layers):
        shards.append(
            jnp.concatenate([qkv_weight[layer, i] for i in range(3)] + [out_turned[layer]], axis=1)
        )
        shards += [in_weight[layer], down_turned[layer]]

    weights = {}
    for layer in GATHERED:
        for kind, group in enumerate(gather_common(shards[3 * layer : 3 * layer + 3], places, from_common)):
            weights[3 * layer + kind] = group

    doc_ids = segment_ids[core, tensor_at // 2]
    current = dot_nn(to_sequence(tokens, core), place).astype(BF16)
    upstream = dot_nn(to_sequence(cotangent, core), place).astype(BF16)

    small = (qv_bias, in_bias, row_bias, norm_gain, norm_shift)
    lengths = [s.size for s in small]
    flat = gather_flat(jnp.concatenate([s.reshape(-1) for s in small]).reshape(1, -1), parts)
    edges = [0]
    for n in lengths:
        edges.append(edges[-1] + n)
    ordered = flat[:, place_of, : edges[2]]
    qv_all = (
        ordered[:, :, : edges[1]].reshape((teams, parts) + qv_bias.shape).transpose(2, 3, 0, 4, 1, 5)
        .reshape(layers, 2, teams, 1, width).astype(F32)
    )
    in_all = (
        ordered[:, :, edges[1] : edges[2]].reshape((teams, parts) + in_bias.shape).transpose(2, 0, 3, 1, 4)
        .reshape(layers, teams, 1, units).astype(F32)
    )
    vecs = (
        flat[0, :, edges[2] :].reshape((parts, 3) + row_bias.shape).transpose(2, 3, 1, 0, 4)
        .reshape(layers, 2, 3, model).astype(F32)
    )

    coming = {at: gather_group(shard, places) for at, shard in enumerate(shards) if at not in weights}
    for group in coming.values():
        next(group)
    steps = len(dp_bits(parts)) - 1
    last = ()

    def turn(index, after=()):
        nonlocal last
        last = (coming[index].send(tuple(last) + tuple(after)),)
        return next(coming[index])

    ready = (qv_all, in_all, vecs, current, upstream)
    saved = []
    for layer in range(layers):
        at = 3 * layer
        entered = current
        if at in coming:
            for _ in range(steps):
                turn(at)
            for _ in range(steps - 1):
                turn(at + 1)
            turn(at, ready)
            turn(at + 1)
            weights[at] = turn(at)
            for _ in range(steps - 1):
                turn(at + 2)
        qkv, prob, context, normal_one, scale_one, token = attend(
            table, entered, weights[at], qv_all[layer, 0], qv_all[layer, 1], vecs[layer, 0], doc_ids, last
        )
        last = (token,)
        if at in coming:
            turn(at + 1)
            turn(at + 2)
            weights[at + 1] = turn(at + 1)
            turn(at + 2)
            weights[at + 2] = turn(at + 2)
        low, active, slope, current, normal_two, scale_two, token = forward(
            table, normal_one, vecs[layer, 0], vecs[layer, 1], in_all[layer], weights[at + 1], weights[at + 2], last
        )
        last = (token,)
        saved.append(
            (entered, qkv, prob, context, normal_one, scale_one, low, active, slope, normal_two, scale_two)
        )
    smalls = [None] * layers
    owned, flights, ran, settled = {}, {}, [], ()
    fine = piece % 16 == 0

    def launch(key, grads):
        if key not in SCATTERED:
            flights[key] = scatter_group(*grads, parts)
            next(flights[key])
            return
        if not fine:
            grads = [
                joined(*grads).reshape(teams, parts, piece, -1)[line_of][:, place_of]
                .reshape(teams * model, -1)
            ]
        owned[key] = lax.psum_scatter(
            grads[0], ("tensor", "dp"), scatter_dimension=0, tiled=True
        ).astype(F32)

    def advance(keys, token):
        made = []
        for key in keys:
            got = flights[key].send(token)
            if got.shape != (8, 128):
                owned[key] = got
                del flights[key]
            else:
                made.append(got)
        return tuple(made)

    last = ()

    def push(*keys):
        nonlocal last
        for key in keys:
            if key in flights:
                last = advance([key], last[0] if last else None) or last

    for layer in reversed(range(layers)):
        (entered, qkv, prob, context, normal_one, scale_one, low, active, slope, normal_two, scale_two) = saved[layer]
        *grads, grad_one, sums_two, sums_one, unit_sums, token = forward_back(
            table, upstream, normal_two, scale_two, vecs[layer, 1], active, slope, weights[3 * layer + 1],
            weights[3 * layer + 2], low, normal_one, scale_one, vecs[layer, 0], (layer, 1) in SCATTERED and fine, last,
        )
        last = (token,)
        launch((layer, 1), grads)
        push(*flights)
        *grads, upstream, qkv_sums, token = attend_back(
            table, entered, grad_one, weights[3 * layer], qkv, prob, context, (layer, 0) in SCATTERED and fine, last,
        )
        last = (token,)
        launch((layer, 0), grads)
        smalls[layer] = (qkv_sums, unit_sums, sums_one, sums_two)
        push(*flights)
    keys = list(flights)
    token = last[0]
    for layer in range(layers):
        qkv_sums, unit_sums, sums_one, sums_two = (gated(s, token) for s in smalls[layer])
        row_sums = jnp.stack([sums_one, sums_two]).reshape(6, parts, piece)[:, place_of]
        smalls[layer] = (qkv_sums[line_of], unit_sums[line_of], row_sums)
    sizes = [s.size for s in smalls[0]]
    flat = jnp.concatenate([s.reshape(-1) for layer in smalls for s in layer]).reshape(-1, 128)
    rounds = [("tensor", bit) for bit in range(teams.bit_length() - 1)]
    rounds += [("dp", bit) for bit in range(parts.bit_length() - 1)]
    output = from_sequence(reorder(current, place, last), core)
    grad_tokens = from_sequence(reorder(upstream, place, last), core)
    while flights:
        for key in list(flights):
            got = trade(flat, *rounds.pop(0)) if rounds else None
            push(key)
            if got is not None:
                flat = flat + gated(got, last[0])
    for axis, bit in rounds:
        flat = flat + trade(flat, axis, bit)
    grads = [[owned[layer, 0], owned[layer, 1][:, :units], owned[layer, 1][:, units:]] for layer in range(layers)]

    flat = flat.reshape(layers, -1)
    qkv_sums = flat[:, : sizes[0]].reshape(layers, teams, 3, heads, parts, -1)
    qkv_sums = lax.dynamic_index_in_dim(qkv_sums, tensor_at, 1, keepdims=False)
    qkv_sums = lax.dynamic_index_in_dim(qkv_sums, dp_at, 3, keepdims=False)
    grad_qv = jnp.stack([qkv_sums[:, 0], qkv_sums[:, 2]], axis=1)
    unit_sums = flat[:, sizes[0] : sizes[0] + sizes[1]].reshape(layers, teams, units // HD, parts, -1)
    unit_sums = lax.dynamic_index_in_dim(unit_sums, tensor_at, 1, keepdims=False)
    grad_unit = lax.dynamic_index_in_dim(unit_sums, dp_at, 2, keepdims=False)
    row_sums = flat[:, sizes[0] + sizes[1] :].reshape(layers, 2, 3, parts, piece)
    row_sums = lax.dynamic_index_in_dim(row_sums, dp_at, 3, keepdims=False)

    grad_attn = jnp.stack([g[0] for g in grads])
    grad_qkv = jnp.stack(
        [grad_attn[:, :, i * width : (i + 1) * width] for i in range(3)], axis=1
    )
    return (
        output,
        grad_tokens,
        grad_qkv,
        jnp.swapaxes(grad_attn[:, :, 3 * width :], 1, 2),
        jnp.stack([g[1] for g in grads]),
        jnp.swapaxes(jnp.stack([g[2] for g in grads]), 1, 2),
        grad_qv,
        grad_unit,
        row_sums[:, :, 2],
        row_sums[:, :, 0],
        row_sums[:, :, 1],
    )


def solution(mesh):
    placed = (
        P(None, ("dp", "tensor"), None),
        P(None, ("dp", "tensor"), None),
        P(None, "dp", None),
        P(None, None, "dp", "tensor"),
        P(None, "tensor", "dp"),
        P(None, "dp", "tensor"),
        P(None, "tensor", "dp"),
        P(None, None, "tensor", "dp"),
        P(None, "tensor", "dp"),
        P(None, None, "dp"),
        P(None, None, "dp"),
        P(None, None, "dp"),
    )
    return jax.shard_map(
        on_device,
        mesh=mesh,
        in_specs=placed,
        out_specs=(
            P(None, ("dp", "tensor"), None),
            P(None, ("dp", "tensor"), None),
            P(None, None, "dp", "tensor"),
            P(None, "tensor", "dp"),
            P(None, "dp", "tensor"),
            P(None, "tensor", "dp"),
            P(None, None, "tensor", "dp"),
            P(None, "tensor", "dp"),
            P(None, None, "dp"),
            P(None, None, "dp"),
            P(None, None, "dp"),
        ),
        check_vma=False,
    )
```

time: 1430 us -> 493 us (0.34)
  waiting for transfers between devices: 1220 us -> 106 us
  starting transfers between devices: 1.64 us -> 82 us
  Pallas kernels: 137 us -> 189 us
  local copies, waits for them, and re-layouts: 42.7 us -> 61.6 us
  other arithmetic: 11.5 us -> 29.2 us
    reduce_scatter x4 -> x1, waiting for transfers between devices: 443 us -> 0.01 us  [launch(): lax.psum_scatter(grads[0], ('tensor', 'dp'), scatter_dimension=0, tiled=T...]
    unnamed x17 -> x2, waiting for transfers between devices: 333 us -> 0.03 us
    all_gather x6 -> x1, waiting for transfers between devices: 327 us -> 0.02 us  [gather_common(): lax.all_gather(jnp.concatenate(shards, axis=1), ('tensor', 'dp'), axis=0,...]
    psum x1 -> x0, waiting for transfers between devices: 112 us -> none  [on_device(): flat = lax.psum(flat, BOTH).reshape(layers, -1)]
    ppermute x4 -> x59, waiting for transfers between devices: 0.01 us -> 106 us  [trade(): lax.ppermute(values, axis, [(i, i ^ 1 << bit) for i in range(lax.axis_siz...]
    ppermute x4 -> x59, starting transfers between devices: 1.09 us -> 81.9 us  [trade(): lax.ppermute(values, axis, [(i, i ^ 1 << bit) for i in range(lax.axis_siz...]
    pallas_call x12 -> x34, Pallas kernels: 137 us -> 189 us  [the longest x8 149 us: streamed(): return kernel(table, *operands, *after)]
  transfers between devices with their start and end apart: 18 -> 61, of which waited for: 14 -> 26; matrix products, arithmetic and copies ran while one was open for 2% -> 16% of each run, Pallas kernels for 4% -> 23%
where the time goes in v2:
time: 493 us; the launch traced here: 485 us
  Pallas kernels  189 us (38%)
  waiting for transfers between devices  106 us (22%)
  starting transfers between devices  82 us (17%)
  local copies, waits for them, and re-layouts  61.6 us (12%)
  other arithmetic  29.2 us (6%)
  between operations  16.4 us (3%)
    pallas_call x8, Pallas kernels, streamed(): return kernel(table, *operands, *after)  149 us
    ppermute x59, waiting for transfers between devices, trade(): lax.ppermute(values, axis, [(i, i ^ 1 << bit) for i in range(lax.axis_siz...  106 us
    ppermute x59, starting transfers between devices, trade(): lax.ppermute(values, axis, [(i, i ^ 1 << bit) for i in range(lax.axis_siz...  81.9 us
    pallas_call x14, Pallas kernels, run(): made = kernel(*args, *after)  30.5 us
    unnamed x145, local copies, waits for them, and re-layouts  20.4 us
  transfers between devices with their start and end apart: 61, of which 26 were waited for; matrix products, arithmetic and copies ran while one was open for 16% of the time, Pallas kernels for 23%

profile of v2, /device:TPU:0, one launch (start us, length us, event | category | flops | bytes accessed | tf_op | source)
XLA Modules:
  0.0 485.4 jit_solution(9559699091153032346)
XLA Ops:
  50.6 10.3 %collective-permute-done.7.refs_1_ = bf16[192,768]{1,0:T(8,128)(2,1)S(1)} collective-permute-done((bf16[192,768]{1,0:T(8,128)(2,1)S(1)}, bf16[192,768]{1,0:T(8,128)(2,1)S(1)}, u32[]{:S(2)}, u32[]{:S(2)}) %collective-permute-start.7) | collective-permute-done | bytes 294944 | tf_op jit(solution)/shard_map/ppermute | solution.py:622
  66.3 7.3 %collective-permute-done.8.refs_1_ = bf16[384,768]{1,0:T(8,128)(2,1)S(1)} collective-permute-done((bf16[384,768]{1,0:T(8,128)(2,1)S(1)}, bf16[384,768]{1,0:T(8,128)(2,1)S(1)}, u32[]{:S(2)}, u32[]{:S(2)}) %collective-permute-start.8) | collective-permute-done | bytes 589856 | tf_op jit(solution)/shard_map/ppermute | solution.py:622
  77.3 5.9 %collective-permute-done.14.refs_1_ = bf16[192,768]{1,0:T(8,128)(2,1)S(1)} collective-permute-done((bf16[192,768]{1,0:T(8,128)(2,1)S(1)}, bf16[192,768]{1,0:T(8,128)(2,1)S(1)}, u32[]{:S(2)}, u32[]{:S(2)}) %collective-permute-start.14) | collective-permute-done | bytes 294944 | tf_op jit(solution)/shard_map/ppermute | solution.py:622
  85.9 7.7 %collective-permute-start.17 = (bf16[96,768]{1,0:T(8,128)(2,1)S(1)}, bf16[96,768]{1,0:T(8,128)(2,1)S(1)}, u32[]{:S(2)}, u32[]{:S(2)}) collective-permute-start(bf16[96,768]{1,0:T(8,128)(2,1)S(1)} %get-tuple-element.315.refs_0_), channel_id=1, source_target_pairs={{0,8},{4,12},{8,0},{12,4},{16,24},{20,28},{24,16},{28,20},{1,9},{5... | collective-permute-start | bytes 442376 | tf_op jit(solution)/shard_map/ppermute | solution.py:622
  101.9 7.2 %collective-permute-done.17.refs_1_ = bf16[96,768]{1,0:T(8,128)(2,1)S(1)} collective-permute-done((bf16[96,768]{1,0:T(8,128)(2,1)S(1)}, bf16[96,768]{1,0:T(8,128)(2,1)S(1)}, u32[]{:S(2)}, u32[]{:S(2)}) %collective-permute-start.17) | collective-permute-done | bytes 147488 | tf_op jit(solution)/shard_map/ppermute | solution.py:622
  113.5 17.3 %attend.2 = (bf16[4,512,576]{2,1,0:T(8,128)(2,1)}, bf16[12,512,512]{2,1,0:T(8,128)(2,1)}, bf16[4,192,512]{2,1,0:T(8,128)(2,1)}, f32[512,768]{1,0:T(8,128)}, f32[512,1]{1,0:T(8,128)}, /*index=5*/f32[8,128]{1,0:T(8,128)}) custom-call(s32[12]{0:T(128)} %pad_add_fusion.refs_0_, bf16[512,768]{1,0:T(8,128)(2,1)} %copy-done.4, s32[512,1]{1,0:T(8,128)} %copy.66.refs_2_, ...), custom_call_target="tpu_custom_call" | custom-call | flops 4312500224 | tf_op jit(solution)/shard_map/attend/pallas_call | solution.py:250
  131.7 5.0 %collective-permute-done.22.refs_1_ = bf16[192,768]{1,0:T(8,128)(2,1)S(1)} collective-permute-done((bf16[192,768]{1,0:T(8,128)(2,1)S(1)}, bf16[192,768]{1,0:T(8,128)(2,1)S(1)}, u32[]{:S(2)}, u32[]{:S(2)}) %collective-permute-start.22) | collective-permute-done | bytes 294944 | tf_op jit(solution)/shard_map/ppermute | solution.py:622
  138.0 4.3 collective-permute-start.26
  142.4 11.4 %collective-permute-done.20.refs_3_ = bf16[192,768]{1,0:T(8,128)(2,1)S(1)} collective-permute-done((bf16[192,768]{1,0:T(8,128)(2,1)S(1)}, bf16[192,768]{1,0:T(8,128)(2,1)S(1)}, u32[]{:S(2)}, u32[]{:S(2)}) %collective-permute-start.20) | collective-permute-done | bytes 294944 | tf_op jit(solution)/shard_map/ppermute | solution.py:622
  172.9 13.4 %forward.2 = (bf16[512,768]{1,0:T(8,128)(2,1)}, bf16[4,512,768]{2,1,0:T(8,128)(2,1)}, bf16[4,512,768]{2,1,0:T(8,128)(2,1)}, f32[512,768]{1,0:T(8,128)}, f32[512,...) custom-call(s32[12]{0:T(128)} %pad_add_fusion.refs_0_, f32[512,768]{1,0:T(8,128)} %get-tuple-element.151.refs_1_.refs_16_, ...), custom_call_target="tpu_custom_call" | custom-call | flops 4312500224 | tf_op jit(solution)/shard_map/forward/pallas_call | solution.py:250
  186.3 18.0 %attend.3 = (bf16[4,512,576]{2,1,0:T(8,128)(2,1)}, bf16[12,512,512]{2,1,0:T(8,128)(2,1)}, bf16[4,192,512]{2,1,0:T(8,128)(2,1)}, f32[512,768]{1,0:T(8,128)}, f32[512,1]{1,0:T(8,128)}, /*index=5*/f32[8,128]{1,0:T(8,128)}) custom-call(s32[12]{0:T(128)} %pad_add_fusion.refs_0_, f32[512,768]{1,0:T(8,128)} %get-tuple-element.169.refs_1_, s32[512,1]{1,0:T(8,128)} %copy.66.refs_2_, ...), custom_call_target="tpu_custom_call" | custom-call | flops 4312500224 | tf_op jit(solution)/shard_map/attend/pallas_call | solution.py:250
  204.3 15.2 %forward.3 = (bf16[512,768]{1,0:T(8,128)(2,1)}, bf16[4,512,768]{2,1,0:T(8,128)(2,1)}, bf16[4,512,768]{2,1,0:T(8,128)(2,1)}, f32[512,768]{1,0:T(8,128)}, f32[512,...) custom-call(s32[12]{0:T(128)} %pad_add_fusion.refs_0_, f32[512,768]{1,0:T(8,128)} %get-tuple-element.171.refs_1_.refs_10_, ...), custom_call_target="tpu_custom_call" | custom-call | flops 4312500224 | tf_op jit(solution)/shard_map/forward/pallas_call | solution.py:250
  219.5 20.1 %forward_back.2 = (bf16[3072,1536]{1,0:T(8,128)(2,1)}, f32[512,768]{1,0:T(8,128)}, f32[3,768]{1,0:T(4,128)}, f32[3,768]{1,0:T(4,128)}, f32[4,1,768]{2,1,0:T(1,128)}, /*index=5*/f32[8,128]{1,0:T(8,128)}) custom-call(s32[12]{0:T(128)} %pad_add_fusion.refs_0_, bf16[512,768]{1,0:T(8,128)(2,1)} %copy-done.5, f32[512,768]{1,0:T(8,128)} %get-tuple-element.174.refs_2_, ...), custom_call_target="tpu_custom_call" | custom-call | flops 43700000391168 | tf_op jit(solution)/shard_map/forward_back/pallas_call | solution.py:250
  239.6 23.3 %attend_back.2 = (bf16[2,768,768]{2,1,0:T(8,128)(2,1)}, bf16[2,768,768]{2,1,0:T(8,128)(2,1)}, f32[512,768]{1,0:T(8,128)}, f32[4,1,576]{2,1,0:T(1,128)}, f32[8,128]{1,0:T(8,128)}) custom-call(s32[12]{0:T(128)} %pad_add_fusion.refs_0_, f32[512,768]{1,0:T(8,128)} %get-tuple-element.169.refs_1_, f32[512,768]{1,0:T(8,128)} %get-tuple-element.180.refs_2_, ...), custom_call_target="tpu_custom_call" | custom-call | flops 50599999569920 | tf_op jit(solution)/shard_map/attend_back/pallas_call | solution.py:250
  276.1 19.3 %forward_back.3 = (bf16[2,768,1536]{2,1,0:T(8,128)(2,1)}, bf16[2,768,1536]{2,1,0:T(8,128)(2,1)}, f32[512,768]{1,0:T(8,128)}, f32[3,768]{1,0:T(4,128)}, f32[3,768...) custom-call(s32[12]{0:T(128)} %pad_add_fusion.refs_0_, f32[512,768]{1,0:T(8,128)} %get-tuple-element.185.refs_1_, ...), custom_call_target="tpu_custom_call" | custom-call | flops 43700000391168 | tf_op jit(solution)/shard_map/forward_back/pallas_call | solution.py:250
  300.5 4.1 collective-permute-done.32
  304.6 6.0 %merge_core.4 = (bf16[2,192,1536]{2,1,0:T(8,128)(2,1)}, bf16[2,192,1536]{2,1,0:T(8,128)(2,1)S(1)}, bf16[2,192,1536]{2,1,0:T(8,128)(2,1)}, bf16[2,192,1536]{2,1,0:T(8,128)(2,1)S(1)}, f32[8,128]{1,0:T(8,128)S(1)}) custom-call(bf16[2,2,2,192,1536]{4,3,2,1,0:T(8,128)(2,1)S(1)} %bitcast.176, bf16[2,2,2,192,1536]{4,3,2,1,0:T(8,128)(2,1)} %bitcast.41.refs_1_, ...), custom_call_target="tpu_custom_call" | custom-call | flops 4600000151552 | tf_op jit(solution)/shard_map/merge_core/pallas_call | solution.py:580
  312.2 22.6 %attend_back.3 = (bf16[2,768,768]{2,1,0:T(8,128)(2,1)}, bf16[2,768,768]{2,1,0:T(8,128)(2,1)}, f32[512,768]{1,0:T(8,128)}, f32[4,1,576]{2,1,0:T(1,128)}, f32[8,128]{1,0:T(8,128)}) custom-call(s32[12]{0:T(128)} %pad_add_fusion.refs_0_, bf16[512,768]{1,0:T(8,128)(2,1)} %copy-done.4, f32[512,768]{1,0:T(8,128)} %get-tuple-element.196.refs_2_, ...), custom_call_target="tpu_custom_call" | custom-call | flops 50599999569920 | tf_op jit(solution)/shard_map/attend_back/pallas_call | solution.py:250
  338.6 8.9 %collective-permute-done.36.refs_1_ = bf16[2,192,1536]{2,1,0:T(8,128)(2,1)} collective-permute-done((bf16[2,192,1536]{2,1,0:T(8,128)(2,1)}, bf16[2,192,1536]{2,1,0:T(8,128)(2,1)}, u32[]{:S(2)}, u32[]{:S(2)}) %collective-permute-start.36) | collective-permute-done | bytes 1179680 | tf_op jit(solution)/shard_map/ppermute | solution.py:622
  380.7 11.4 %collective-permute-start.52 = (bf16[96,768]{1,0:T(8,128)(2,1)}, bf16[96,768]{1,0:T(8,128)(2,1)}, u32[]{:S(2)}, u32[]{:S(2)}) collective-permute-start(bf16[96,768]{1,0:T(8,128)(2,1)} %get-tuple-element.251), channel_id=1, source_target_pairs={{0,8},{4,12},{8,0},{12,4},{16,24},{20,28},{24,16},{28,20},{1,9},{5... | collective-permute-start | bytes 442376 | tf_op jit(solution)/shard_map/ppermute | solution.py:622
  399.5 4.8 collective-permute-done.55
  414.7 3.9 collective-permute-start.57
  434.2 4.1 collective-permute-done.58
  459.2 9.1 %collective-permute-done.50.refs_1_ = bf16[192,768]{1,0:T(8,128)(2,1)S(1)} collective-permute-done((bf16[192,768]{1,0:T(8,128)(2,1)S(1)}, bf16[192,768]{1,0:T(8,128)(2,1)S(1)}, u32[]{:S(2)}, u32[]{:S(2)}) %collective-permute-start.50) | collective-permute-done | bytes 294944 | tf_op jit(solution)/shard_map/ppermute | solution.py:622
  (412 shorter events, 208.4 us)
Async XLA Ops:
  7.2 179.1 %all-gather.2.cloned.1.call-start = ((), (), s32[]{:S(2)}) async-start(), calls=%async_computation.1 | async-start | bytes 14598144 | tf_op jit(solution)/shard_map/all_gather | solution.py:774
  11.4 464.8 %reduce-scatter.2.cloned.1.call-start = ((), (), s32[]{:S(2)}) async-start(), calls=%async_computation.2 | async-start | bytes 9732096 | tf_op jit(solution)/shard_map/reduce_scatter | solution.py:1036
  12.3 37.3 %collective-permute-start.11 = (bf16[256,768]{1,0:T(8,128)(2,1)}, bf16[256,768]{1,0:T(8,128)(2,1)}, u32[]{:S(2)}, u32[]{:S(2)}) collective-permute-start(bf16[256,768]{1,0:T(8,128)(2,1)} %dynamic-slice_bitcast_fusion), channel_id=1, source_target_pairs={{0,1},{1,0},{2,3},{3,2},{4,5},{5,4},{6,7},{7,6},{8,9},{9,8},{10,11... | collective-permute-start | bytes 1179656 | tf_op jit(solution)/shard_map/ppermute | solution.py:622
  13.5 51.0 %collective-permute-start = (bf16[256,768]{1,0:T(8,128)(2,1)}, bf16[256,768]{1,0:T(8,128)(2,1)S(1)}, u32[]{:S(2)}, u32[]{:S(2)}) collective-permute-start(bf16[256,768]{1,0:T(8,128)(2,1)} %dynamic-slice_bitcast_fusion.1), channel_id=1, source_target_pairs={{0,1},{1,0},{2,3},{3,2},{4,5},{5,4},{6,7},{7,6},{8,9},{9,8},{10,11... | collective-permute-start | bytes 1179656 | tf_op jit(solution)/shard_map/ppermute | solution.py:622
  17.5 48.2 %collective-permute-start.10 = (bf16[96,768]{1,0:T(8,128)(2,1)S(1)}, bf16[96,768]{1,0:T(8,128)(2,1)S(1)}, u32[]{:S(2)}, u32[]{:S(2)}) collective-permute-start(bf16[96,768]{1,0:T(8,128)(2,1)S(1)} %get-tuple-element.317.refs_0_), channel_id=1, source_target_pairs={{0,8},{4,12},{8,0},{12,4},{16,24},{20,28},{24,16},{28,20},{1,9},{5... | collective-permute-start | bytes 442376 | tf_op jit(solution)/shard_map/ppermute | solution.py:622
  34.6 26.3 %collective-permute-start.7 = (bf16[192,768]{1,0:T(8,128)(2,1)S(1)}, bf16[192,768]{1,0:T(8,128)(2,1)S(1)}, u32[]{:S(2)}, u32[]{:S(2)}) collective-permute-start(bf16[192,768]{1,0:T(8,128)(2,1)S(1)} %get-tuple-element.137.refs_0_), channel_id=1, source_target_pairs={{0,16},{4,20},{8,24},{12,28},{16,0},{20,4},{24,8},{28,12},{1,17},{... | collective-permute-start | bytes 884744 | tf_op jit(solution)/shard_map/ppermute | solution.py:622
  85.3 28.1 %collective-permute-start.15 = (bf16[768,768]{1,0:T(8,128)(2,1)S(1)}, bf16[768,768]{1,0:T(8,128)(2,1)}, u32[]{:S(2)}, u32[]{:S(2)}) collective-permute-start(bf16[768,768]{1,0:T(8,128)(2,1)S(1)} %get-tuple-element.147.refs_9_.refs_8_), channel_id=1, source_target_pairs={{0,1},{1,0},{2,3},{3,2},{4,5},{5,4},{6,7},{7,6},{8,9},{9,8},{10,11... | collective-permute-start | bytes 3538952 | tf_op jit(solution)/shard_map/ppermute | solution.py:622
  85.4 28.1 %collective-permute-start.16 = (bf16[768,768]{1,0:T(8,128)(2,1)}, bf16[768,768]{1,0:T(8,128)(2,1)}, u32[]{:S(2)}, u32[]{:S(2)}) collective-permute-start(bf16[768,768]{1,0:T(8,128)(2,1)} %get-tuple-element.148.refs_10_.refs_9_), channel_id=1, source_target_pairs={{0,1},{1,0},{2,3},{3,2},{4,5},{5,4},{6,7},{7,6},{8,9},{9,8},{10,11... | collective-permute-start | bytes 3538952 | tf_op jit(solution)/shard_map/ppermute | solution.py:622
  96.9 33.8 %collective-permute-start.18 = (bf16[384,768]{1,0:T(8,128)(2,1)S(1)}, bf16[384,768]{1,0:T(8,128)(2,1)S(1)}, u32[]{:S(2)}, u32[]{:S(2)}) collective-permute-start(bf16[384,768]{1,0:T(8,128)(2,1)S(1)} %get-tuple-element.152.refs_0_), channel_id=1, source_target_pairs={{0,4},{4,0},{8,12},{12,8},{16,20},{20,16},{24,28},{28,24},{1,5},{5... | collective-permute-start | bytes 1769480 | tf_op jit(solution)/shard_map/ppermute | solution.py:622
  98.8 32.0 %collective-permute-start.19 = (bf16[384,768]{1,0:T(8,128)(2,1)S(1)}, bf16[384,768]{1,0:T(8,128)(2,1)S(1)}, u32[]{:S(2)}, u32[]{:S(2)}) collective-permute-start(bf16[384,768]{1,0:T(8,128)(2,1)S(1)} %get-tuple-element.152.refs_0_), channel_id=1, source_target_pairs={{0,2},{1,3},{2,0},{3,1},{4,6},{5,7},{6,4},{7,5},{8,10},{9,11},{10,... | collective-permute-start | bytes 1769480 | tf_op jit(solution)/shard_map/ppermute | solution.py:622
  109.7 27.0 %collective-permute-start.22 = (bf16[192,768]{1,0:T(8,128)(2,1)S(1)}, bf16[192,768]{1,0:T(8,128)(2,1)S(1)}, u32[]{:S(2)}, u32[]{:S(2)}) collective-permute-start(bf16[192,768]{1,0:T(8,128)(2,1)S(1)} %get-tuple-element.156.refs_0_), channel_id=1, source_target_pairs={{0,16},{4,20},{8,24},{12,28},{16,0},{20,4},{24,8},{28,12},{1,17},{... | collective-permute-start | bytes 884744 | tf_op jit(solution)/shard_map/ppermute | solution.py:622
  298.5 36.5 %collective-permute-start.38 = (bf16[192,768]{1,0:T(8,128)(2,1)}, bf16[192,768]{1,0:T(8,128)(2,1)}, u32[]{:S(2)}, u32[]{:S(2)}) collective-permute-start(bf16[192,768]{1,0:T(8,128)(2,1)} %get-tuple-element.216), channel_id=1, source_target_pairs={{0,4},{4,0},{8,12},{12,8},{16,20},{20,16},{24,28},{28,24},{1,5},{5... | collective-permute-start | bytes 884744 | tf_op jit(solution)/shard_map/ppermute | solution.py:622
  300.5 34.5 %collective-permute-start.39 = (bf16[192,768]{1,0:T(8,128)(2,1)}, bf16[192,768]{1,0:T(8,128)(2,1)}, u32[]{:S(2)}, u32[]{:S(2)}) collective-permute-start(bf16[192,768]{1,0:T(8,128)(2,1)} %get-tuple-element.218), channel_id=1, source_target_pairs={{0,2},{1,3},{2,0},{3,1},{4,6},{5,7},{6,4},{7,5},{8,10},{9,11},{10,... | collective-permute-start | bytes 884744 | tf_op jit(solution)/shard_map/ppermute | solution.py:622
  310.6 36.8 %collective-permute-start.36 = (bf16[2,192,1536]{2,1,0:T(8,128)(2,1)}, bf16[2,192,1536]{2,1,0:T(8,128)(2,1)}, u32[]{:S(2)}, u32[]{:S(2)}) collective-permute-start(bf16[2,192,1536]{2,1,0:T(8,128)(2,1)} %get-tuple-element.212), channel_id=1, source_target_pairs={{0,2},{1,3},{2,0},{3,1},{4,6},{5,7},{6,4},{7,5},{8,10},{9,11},{10,... | collective-permute-start | bytes 3538952 | tf_op jit(solution)/shard_map/ppermute | solution.py:622
  310.9 36.8 %collective-permute-start.37 = (bf16[2,192,1536]{2,1,0:T(8,128)(2,1)}, bf16[2,192,1536]{2,1,0:T(8,128)(2,1)}, u32[]{:S(2)}, u32[]{:S(2)}) collective-permute-start(bf16[2,192,1536]{2,1,0:T(8,128)(2,1)} %get-tuple-element.214), channel_id=1, source_target_pairs={{0,4},{4,0},{8,12},{12,8},{16,20},{20,16},{24,28},{28,24},{1,5},{5... | collective-permute-start | bytes 3538952 | tf_op jit(solution)/shard_map/ppermute | solution.py:622
  338.5 36.4 %collective-permute-start.46 = (bf16[192,768]{1,0:T(8,128)(2,1)}, bf16[192,768]{1,0:T(8,128)(2,1)}, u32[]{:S(2)}, u32[]{:S(2)}) collective-permute-start(bf16[192,768]{1,0:T(8,128)(2,1)} %get-tuple-element.233), channel_id=1, source_target_pairs={{0,16},{4,20},{8,24},{12,28},{16,0},{20,4},{24,8},{28,12},{1,17},{... | collective-permute-start | bytes 884744 | tf_op jit(solution)/shard_map/ppermute | solution.py:622
  380.0 27.2 %collective-permute-start.42 = (bf16[2,192,768]{2,1,0:T(8,128)(2,1)}, bf16[2,192,768]{2,1,0:T(8,128)(2,1)}, u32[]{:S(2)}, u32[]{:S(2)}) collective-permute-start(bf16[2,192,768]{2,1,0:T(8,128)(2,1)} %get-tuple-element.225), channel_id=1, source_target_pairs={{0,2},{1,3},{2,0},{3,1},{4,6},{5,7},{6,4},{7,5},{8,10},{9,11},{10,... | collective-permute-start | bytes 1769480 | tf_op jit(solution)/shard_map/ppermute | solution.py:622
  380.3 27.5 %collective-permute-start.43 = (bf16[2,192,768]{2,1,0:T(8,128)(2,1)}, bf16[2,192,768]{2,1,0:T(8,128)(2,1)}, u32[]{:S(2)}, u32[]{:S(2)}) collective-permute-start(bf16[2,192,768]{2,1,0:T(8,128)(2,1)} %get-tuple-element.227), channel_id=1, source_target_pairs={{0,4},{4,0},{8,12},{12,8},{16,20},{20,16},{24,28},{28,24},{1,5},{5... | collective-permute-start | bytes 1769480 | tf_op jit(solution)/shard_map/ppermute | solution.py:622
  380.7 41.5 %collective-permute-start.49 = (bf16[192,1536]{1,0:T(8,128)(2,1)}, bf16[192,1536]{1,0:T(8,128)(2,1)}, u32[]{:S(2)}, u32[]{:S(2)}) collective-permute-start(bf16[192,1536]{1,0:T(8,128)(2,1)} %get-tuple-element.241), channel_id=1, source_target_pairs={{0,16},{4,20},{8,24},{12,28},{16,0},{20,4},{24,8},{28,12},{1,17},{... | collective-permute-start | bytes 1769480 | tf_op jit(solution)/shard_map/ppermute | solution.py:622
  380.7 49.8 %collective-permute-start.52 = (bf16[96,768]{1,0:T(8,128)(2,1)}, bf16[96,768]{1,0:T(8,128)(2,1)}, u32[]{:S(2)}, u32[]{:S(2)}) collective-permute-start(bf16[96,768]{1,0:T(8,128)(2,1)} %get-tuple-element.251), channel_id=1, source_target_pairs={{0,8},{4,12},{8,0},{12,4},{16,24},{20,28},{24,16},{28,20},{1,9},{5... | collective-permute-start | bytes 442376 | tf_op jit(solution)/shard_map/ppermute | solution.py:622
  404.3 43.4 %collective-permute-start.41 = (f32[256,768]{1,0:T(8,128)}, f32[256,768]{1,0:T(8,128)}, u32[]{:S(2)}, u32[]{:S(2)}) collective-permute-start(f32[256,768]{1,0:T(8,128)} %constant_dynamic-slice_fusion.2), channel_id=1, source_target_pairs={{0,1},{1,0},{2,3},{3,2},{4,5},{5,4},{6,7},{7,6},{8,9},{9,8},{10,11... | collective-permute-start | bytes 2359304 | tf_op jit(solution)/shard_map/ppermute | solution.py:622
  407.2 41.8 %collective-permute-start.40 = (f32[256,768]{1,0:T(8,128)}, f32[256,768]{1,0:T(8,128)}, u32[]{:S(2)}, u32[]{:S(2)}) collective-permute-start(f32[256,768]{1,0:T(8,128)} %constant_dynamic-slice_fusion.3), channel_id=1, source_target_pairs={{0,1},{1,0},{2,3},{3,2},{4,5},{5,4},{6,7},{7,6},{8,9},{9,8},{10,11... | collective-permute-start | bytes 2359304 | tf_op jit(solution)/shard_map/ppermute | solution.py:622
  425.4 27.3 %collective-permute-start.47 = (bf16[192,768]{1,0:T(8,128)(2,1)S(1)}, bf16[192,768]{1,0:T(8,128)(2,1)S(1)}, u32[]{:S(2)}, u32[]{:S(2)}) collective-permute-start(bf16[192,768]{1,0:T(8,128)(2,1)S(1)} %get-tuple-element.237), channel_id=1, source_target_pairs={{0,4},{4,0},{8,12},{12,8},{16,20},{20,16},{24,28},{28,24},{1,5},{5... | collective-permute-start | bytes 884744 | tf_op jit(solution)/shard_map/ppermute | solution.py:622
  426.9 25.8 %collective-permute-start.48 = (bf16[192,768]{1,0:T(8,128)(2,1)S(1)}, bf16[192,768]{1,0:T(8,128)(2,1)S(1)}, u32[]{:S(2)}, u32[]{:S(2)}) collective-permute-start(bf16[192,768]{1,0:T(8,128)(2,1)S(1)} %get-tuple-element.239), channel_id=1, source_target_pairs={{0,2},{1,3},{2,0},{3,1},{4,6},{5,7},{6,4},{7,5},{8,10},{9,11},{10,... | collective-permute-start | bytes 884744 | tf_op jit(solution)/shard_map/ppermute | solution.py:622
  (102 other events, 959.2 us)
Sparse Core Ops, SparseCore 0:
  11.6 131.4 all-gather.1
  265.6 178.6 reduce-scatter.1

commit v3 on v2

--- a/solution.py
+++ b/solution.py
@@ -27,7 +27,7 @@
 LINE = (1, 3, 0, 2)
 
 GATHERED = (1,)
-SCATTERED = ((1, 1),)
+SCATTERED = ()
 
 
 def dot_nn(left, right):
@@ -111,7 +111,7 @@
         model = group.model
         self.scratch = [
             pltpu.VMEM((len(LINE), model, width), BF16),
-            pltpu.SemaphoreType.DMA((len(LINE), len(group.places) if group.common else 1)),
+            pltpu.SemaphoreType.DMA((len(LINE), len(group.places))),
         ]
 
     def bind(self, refs, scratch, table):
@@ -119,7 +119,7 @@
         return self
 
     def copies(self, index):
-        if not self.group.common:
+        if not self.group.common and self.group.pitch * len(self.group.places) == self.group.model:
             yield pltpu.make_async_copy(
                 self.refs[index].at[:, self.cols], self.held.at[index], self.sems.at[index, 0]
             )
@@ -127,9 +127,13 @@
         places = len(self.group.places)
         piece = self.group.model // places
         for place in range(places):
-            row = pl.multiple_of(self.table[index] + self.table[len(LINE) + place], piece)
+            if self.group.common:
+                ref = self.refs[0]
+                row = pl.multiple_of(self.table[index] + self.table[len(LINE) + place], piece)
+            else:
+                ref, row = self.refs[index], place * self.group.pitch
             yield pltpu.make_async_copy(
-                self.refs[0].at[pl.ds(row, piece), self.cols],
+                ref.at[pl.ds(row, piece), self.cols],
                 self.held.at[index, pl.ds(place * piece, piece)],
                 self.sems.at[index, place],
             )
@@ -461,8 +465,11 @@
 
 
 def attend_back_body(inlets, outlets, low_ref, x_low_ref):
-    x, grad_one, qkv, prob, context, weights = inlets
-    grads, grad_x, sums = outlets
+    x, grad_one, qkv, prob, context, weights, unit_sums, sums_one, sums_two = inlets
+    grads, grad_x = outlets
+    places = len(grads.places)
+    model = x.held.shape[1]
+    piece, pitch = model // places, grads.held.shape[1] // places
     steps, width, _ = context.held.shape
     heads = prob.held.shape[0] // steps
 
@@ -477,9 +484,14 @@
     bring(0)
     x.start()
     bring(1)
+    for inlet in (unit_sums, sums_one, sums_two):
+        inlet.start()
     grad_one.wait()
     low_ref[...] = grad_one.held[...].astype(BF16)
     total = grad_one.held[...]
+    for inlet in (unit_sums, sums_one, sums_two):
+        inlet.wait()
+    sums = jnp.concatenate([sums_one.held[...], sums_two.held[...]], axis=0)
     for step in range(steps):
         weights.wait(step)
         qkv.wait(step)
@@ -510,17 +522,30 @@
         stacked = jnp.concatenate(
             [(jnp.concatenate(grad_q, axis=0) * 0.125).T] + grad_k + grad_v, axis=1
         ).astype(BF16)
-        grads.held[step, :, : 3 * width] = dot_tn(x_low_ref[...], stacked).astype(BF16)
-        grads.held[step, :, 3 * width :] = dot_tn(low_ref[...], turned(context.held[step])).astype(BF16)
+        qkv_grad = dot_tn(x_low_ref[...], stacked)
+        out_grad = dot_tn(low_ref[...], turned(context.held[step]))
+        qkv_sums = jnp.sum(stacked.astype(F32), axis=0, keepdims=True)
+        top = jnp.concatenate(
+            [jnp.concatenate([qkv_sums, jnp.zeros((1, width), F32)], axis=1), unit_sums.held[step]], axis=0
+        )
+        for place in range(places):
+            rows = slice(place * piece, (place + 1) * piece)
+            at = place * pitch
+            grads.held[step, at : at + piece, : 3 * width] = qkv_grad[rows].astype(BF16)
+            grads.held[step, at : at + piece, 3 * width :] = out_grad[rows].astype(BF16)
+            own = jnp.concatenate([sums[:, rows], jnp.zeros((6, 4 * width - piece), F32)], axis=1)
+            grads.held[step, at + pitch - EXTRA : at + pitch] = jnp.concatenate(
+                [top, own, jnp.zeros((EXTRA - 8, 4 * width), F32)], axis=0
+            ).astype(BF16)
         grads.start(step)
         total = total + dot_nt(stacked, weights.held[step, :, : 3 * width])
-        sums.held[step] = jnp.sum(stacked.astype(F32), axis=0, keepdims=True)
-        sums.start(step)
     grad_x.held[...] = total
     grad_x.start()
 
 
-def attend_back(table, x, grad_one, weights, qkv, prob, context, common, after=()):
+def attend_back(
+    table, x, grad_one, weights, qkv, prob, context, unit_sums, sums_one, sums_two, after=()
+):
     steps, width, rows = context.shape
     model = x.shape[1]
     return streamed(
@@ -529,12 +554,11 @@
         table,
         [
             Rows(x), Rows(grad_one), Rows(qkv, True), Rows(prob, True), Rows(context, True),
-            Weights(weights, 0, 4 * width),
+            Weights(weights, 0, 4 * width), Rows(unit_sums), Rows(sums_one), Rows(sums_two),
         ],
         [
-            Grads(model, 4 * width, weights.places, common),
+            Grads(len(weights.places) * (-(-model // len(weights.places) // 16) * 16 + EXTRA), 4 * width, weights.places, False),
             Result((rows, model), F32),
-            Result((steps, 1, 3 * width), F32, True),
         ],
         [pltpu.VMEM((rows, model), BF16), pltpu.VMEM((rows, model), BF16)],
         after=after,
@@ -610,7 +634,7 @@
 
 
 def dp_bits(parts):
-    return list(range(1, parts.bit_length() - 1)) + [0]
+    return list(range(1, parts.bit_length() - 1))[::-1] + [0]
 
 
 def dp_places(parts):
@@ -653,7 +677,7 @@
 class Group:
     def __init__(self, arrays, model, places, common):
         self.arrays, self.model, self.places, self.common = arrays, model, places, common
-        self.start = 0
+        self.start, self.pitch = 0, model // len(places)
 
 
 def mark(*arrays):
@@ -760,11 +784,24 @@
     yield Group([swap_cores(mine), swap_cores(across), mine, across], mine.shape[0], places, False)
 
 
-def gather_flat(flat, parts):
-    for bit in dp_bits(parts):
-        flat = joined(flat, trade(flat, "dp", bit))
-    flat = joined(flat, trade(flat, "tensor", 1))
-    return joined(swap_cores(flat), flat).reshape(len(LINE), parts, -1)
+EXTRA = 16
+
+
+def padded(rows, to):
+    return jnp.pad(rows, ((0, to - rows.shape[0]), (0, 0)))
+
+
+def without_extra(group, piece):
+    parts = len(group.places)
+    pitch = group.model // parts
+    blocks = [array.reshape(parts, pitch, -1) for array in group.arrays]
+    extra = jnp.stack([block[:, pitch - EXTRA :] for block in blocks])
+    group.model = parts * piece
+    if piece % 16:
+        group.arrays = [block[:, :piece].reshape(parts * piece, -1) for block in blocks]
+        pitch = piece
+    group.pitch = pitch
+    return group, extra
 
 
 def gather_common(shards, places, place_rows):
@@ -926,9 +963,6 @@
     core = tensor_at % 2
 
     places = dp_places(parts)
-    back = [places.index(i) for i in range(parts)]
-    place_of = jnp.asarray(back)[jnp.arange(parts) ^ dp_at]
-    line_of = jnp.asarray([LINE.index(i) for i in range(teams)])[jnp.arange(teams) ^ tensor_at]
     column = jnp.arange(model)
     source = (jnp.asarray(places)[column // piece] ^ dp_at) * piece + column % piece
     place = (column[:, None] == source[None, :]).astype(BF16)
@@ -956,25 +990,17 @@
     current = dot_nn(to_sequence(tokens, core), place).astype(BF16)
     upstream = dot_nn(to_sequence(cotangent, core), place).astype(BF16)
 
-    small = (qv_bias, in_bias, row_bias, norm_gain, norm_shift)
-    lengths = [s.size for s in small]
-    flat = gather_flat(jnp.concatenate([s.reshape(-1) for s in small]).reshape(1, -1), parts)
-    edges = [0]
-    for n in lengths:
-        edges.append(edges[-1] + n)
-    ordered = flat[:, place_of, : edges[2]]
-    qv_all = (
-        ordered[:, :, : edges[1]].reshape((teams, parts) + qv_bias.shape).transpose(2, 3, 0, 4, 1, 5)
-        .reshape(layers, 2, teams, 1, width).astype(F32)
-    )
-    in_all = (
-        ordered[:, :, edges[1] : edges[2]].reshape((teams, parts) + in_bias.shape).transpose(2, 0, 3, 1, 4)
-        .reshape(layers, teams, 1, units).astype(F32)
-    )
-    vecs = (
-        flat[0, :, edges[2] :].reshape((parts, 3) + row_bias.shape).transpose(2, 3, 1, 0, 4)
-        .reshape(layers, 2, 3, model).astype(F32)
-    )
+    per = HD // parts
+    lanes = [qv_bias[layer, i].reshape(-1) for layer in range(layers) for i in range(2)]
+    lanes += [in_bias[layer].reshape(-1) for layer in range(layers)]
+    lanes = jnp.concatenate(lanes)
+    wide = shards[0].shape[1]
+    vectors = jnp.stack([row_bias, norm_gain, norm_shift], axis=2).reshape(-1, piece)
+    extra = jnp.concatenate(
+        [jnp.pad(lanes, (0, wide - lanes.size))[None], jnp.pad(vectors, ((0, 0), (0, wide - piece)))]
+    )
+    filled = -(-piece // 16) * 16
+    shards[0] = joined(padded(shards[0], filled), padded(extra, EXTRA))
 
     coming = {at: gather_group(shard, places) for at, shard in enumerate(shards) if at not in weights}
     for group in coming.values():
@@ -987,7 +1013,7 @@
         last = (coming[index].send(tuple(last) + tuple(after)),)
         return next(coming[index])
 
-    ready = (qv_all, in_all, vecs, current, upstream)
+    ready = (current, upstream)
     saved = []
     for layer in range(layers):
         at = 3 * layer
@@ -1000,10 +1026,28 @@
             turn(at, ready)
             turn(at + 1)
             weights[at] = turn(at)
+            if at == 0:
+                weights[0], extra = without_extra(weights[0], piece)
+                vecs = (
+                    extra[0, :, 1 : 1 + 6 * layers, :piece].transpose(1, 0, 2)
+                    .reshape(layers, 2, 3, model).astype(F32)
+                )
+                widths = [width] * (2 * layers) + [units] * layers
+                bias, first, sums = [], 0, extra[:, :, 0]
+                for size in widths:
+                    own = sums[:, :, first : first + size // parts].reshape(teams * parts, -1)
+                    column = jnp.arange(size)
+                    spread = (
+                        jnp.arange(size // parts)[:, None] == (column // HD * per + column % per)[None]
+                    ).astype(BF16)
+                    mask = (jnp.asarray(places)[:, None] ^ dp_at) == (column % HD // per)[None]
+                    full = jnp.where(mask[None], dot_nn(own, spread).reshape(teams, parts, size), 0.0)
+                    bias.append(jnp.sum(full, axis=1, keepdims=True))
+                    first += size // parts
             for _ in range(steps - 1):
                 turn(at + 2)
         qkv, prob, context, normal_one, scale_one, token = attend(
-            table, entered, weights[at], qv_all[layer, 0], qv_all[layer, 1], vecs[layer, 0], doc_ids, last
+            table, entered, weights[at], bias[2 * layer], bias[2 * layer + 1], vecs[layer, 0], doc_ids, last
         )
         last = (token,)
         if at in coming:
@@ -1013,13 +1057,12 @@
             turn(at + 2)
             weights[at + 2] = turn(at + 2)
         low, active, slope, current, normal_two, scale_two, token = forward(
-            table, normal_one, vecs[layer, 0], vecs[layer, 1], in_all[layer], weights[at + 1], weights[at + 2], last
+            table, normal_one, vecs[layer, 0], vecs[layer, 1], bias[2 * layers + layer], weights[at + 1], weights[at + 2], last
         )
         last = (token,)
         saved.append(
             (entered, qkv, prob, context, normal_one, scale_one, low, active, slope, normal_two, scale_two)
         )
-    smalls = [None] * layers
     owned, flights, ran, settled = {}, {}, [], ()
     fine = piece % 16 == 0
 
@@ -1065,45 +1108,29 @@
         last = (token,)
         launch((layer, 1), grads)
         push(*flights)
-        *grads, upstream, qkv_sums, token = attend_back(
-            table, entered, grad_one, weights[3 * layer], qkv, prob, context, (layer, 0) in SCATTERED and fine, last,
+        *grads, upstream, token = attend_back(
+            table, entered, grad_one, weights[3 * layer], qkv, prob, context, unit_sums, sums_one, sums_two, last
         )
         last = (token,)
         launch((layer, 0), grads)
-        smalls[layer] = (qkv_sums, unit_sums, sums_one, sums_two)
         push(*flights)
-    keys = list(flights)
-    token = last[0]
-    for layer in range(layers):
-        qkv_sums, unit_sums, sums_one, sums_two = (gated(s, token) for s in smalls[layer])
-        row_sums = jnp.stack([sums_one, sums_two]).reshape(6, parts, piece)[:, place_of]
-        smalls[layer] = (qkv_sums[line_of], unit_sums[line_of], row_sums)
-    sizes = [s.size for s in smalls[0]]
-    flat = jnp.concatenate([s.reshape(-1) for layer in smalls for s in layer]).reshape(-1, 128)
-    rounds = [("tensor", bit) for bit in range(teams.bit_length() - 1)]
-    rounds += [("dp", bit) for bit in range(parts.bit_length() - 1)]
+    first, second, third, final = list(flights)
+    push(first, final, third)
     output = from_sequence(reorder(current, place, last), core)
+    push(final, second, third)
     grad_tokens = from_sequence(reorder(upstream, place, last), core)
+    push(final, second, third, final)
     while flights:
-        for key in list(flights):
-            got = trade(flat, *rounds.pop(0)) if rounds else None
-            push(key)
-            if got is not None:
-                flat = flat + gated(got, last[0])
-    for axis, bit in rounds:
-        flat = flat + trade(flat, axis, bit)
-    grads = [[owned[layer, 0], owned[layer, 1][:, :units], owned[layer, 1][:, units:]] for layer in range(layers)]
-
-    flat = flat.reshape(layers, -1)
-    qkv_sums = flat[:, : sizes[0]].reshape(layers, teams, 3, heads, parts, -1)
-    qkv_sums = lax.dynamic_index_in_dim(qkv_sums, tensor_at, 1, keepdims=False)
+        push(*list(flights))
+    tops = jnp.stack([owned[layer, 0][-EXTRA:] for layer in range(layers)])
+    grads = [[owned[layer, 0][:piece], owned[layer, 1][:, :units], owned[layer, 1][:, units:]] for layer in range(layers)]
+
+    qkv_sums = tops[:, 0, : 3 * width].reshape(layers, 3, heads, parts, per)
     qkv_sums = lax.dynamic_index_in_dim(qkv_sums, dp_at, 3, keepdims=False)
     grad_qv = jnp.stack([qkv_sums[:, 0], qkv_sums[:, 2]], axis=1)
-    unit_sums = flat[:, sizes[0] : sizes[0] + sizes[1]].reshape(layers, teams, units // HD, parts, -1)
-    unit_sums = lax.dynamic_index_in_dim(unit_sums, tensor_at, 1, keepdims=False)
+    unit_sums = tops[:, 1, :units].reshape(layers, units // HD, parts, per)
     grad_unit = lax.dynamic_index_in_dim(unit_sums, dp_at, 2, keepdims=False)
-    row_sums = flat[:, sizes[0] + sizes[1] :].reshape(layers, 2, 3, parts, piece)
-    row_sums = lax.dynamic_index_in_dim(row_sums, dp_at, 3, keepdims=False)
+    row_sums = tops[:, 2:8, :piece].reshape(layers, 2, 3, piece)
 
     grad_attn = jnp.stack([g[0] for g in grads])
     grad_qkv = jnp.stack(

time: 493 us -> 478 us (0.970)
  waiting for transfers between devices: 106 us -> 142 us
  local copies, waits for them, and re-layouts: 61.6 us -> 34.2 us
  starting transfers between devices: 82 us -> 54.7 us
  Pallas kernels: 189 us -> 207 us
  other arithmetic: 29.2 us -> 16 us
    ppermute x59 -> x56, waiting for transfers between devices: 106 us -> 142 us  [trade(): lax.ppermute(values, axis, [(i, i ^ 1 << bit) for i in range(lax.axis_siz...]
    ppermute x59 -> x56, starting transfers between devices: 81.9 us -> 54.7 us  [trade(): lax.ppermute(values, axis, [(i, i ^ 1 << bit) for i in range(lax.axis_siz...]
    pallas_call x14 -> x18, Pallas kernels: 30.5 us -> 45.9 us  [run(): made = kernel(*args, *after)]
    add x9 -> x0, other arithmetic: 11.5 us -> none  [the longest x5 8.91 us: on_device(): flat = flat + gated(got, last[0])]
    gather x11 -> x0, local copies, waits for them, and re-layouts: 8.48 us -> none  [the longest x1 3.57 us: on_device(): ordered = flat[:, place_of, :edges[2]]]
    reshape x21 -> x1, local copies, waits for them, and re-layouts: 6.93 us -> 0.02 us  [on_device(): jnp.stack([row_bias, norm_gain, norm_shift], axis=2).reshape(-1, piece)]
    unnamed x145 -> x112, local copies, waits for them, and re-layouts: 20.4 us -> 14.3 us
  transfers between devices with their start and end apart: 61 -> 57, of which waited for: 26 -> 21; matrix products, arithmetic and copies ran while one was open for 16% -> 8% of each run, Pallas kernels for 23% -> 31%
where the time goes in v3:
time: 478 us; the launch traced here: 473 us
  Pallas kernels  207 us (43%)
  waiting for transfers between devices  142 us (30%)
  starting transfers between devices  54.7 us (11%)
  local copies, waits for them, and re-layouts  34.2 us (7%)
  other arithmetic  16 us (3%)
  between operations  15.6 us (3%)
    pallas_call x8, Pallas kernels, streamed(): return kernel(table, *operands, *after)  151 us
    ppermute x56, waiting for transfers between devices, trade(): lax.ppermute(values, axis, [(i, i ^ 1 << bit) for i in range(lax.axis_siz...  142 us
    ppermute x56, starting transfers between devices, trade(): lax.ppermute(values, axis, [(i, i ^ 1 << bit) for i in range(lax.axis_siz...  54.7 us
    pallas_call x18, Pallas kernels, run(): made = kernel(*args, *after)  45.9 us
    unnamed x112, local copies, waits for them, and re-layouts  14.3 us
    pallas_call x12, Pallas kernels, moved(): pl.pallas_call(body, in_specs=[ANYWHERE] * (count + waits), out_specs=[AN...  10.2 us
  transfers between devices with their start and end apart: 57, of which 21 were waited for; matrix products, arithmetic and copies ran while one was open for 8% of the time, Pallas kernels for 31%

profile of v3, /device:TPU:0, one launch (start us, length us, event | category | flops | bytes accessed | tf_op | source)
XLA Modules:
  0.0 472.6 jit_solution(9826906151831042541)
XLA Ops:
  12.5 4.1 collective-permute-start.1
  18.7 13.6 %collective-permute-done.1.refs_1_ = bf16[112,768]{1,0:T(8,128)(2,1)S(1)} collective-permute-done((bf16[112,768]{1,0:T(8,128)(2,1)S(1)}, bf16[112,768]{1,0:T(8,128)(2,1)S(1)}, u32[]{:S(2)}, u32[]{:S(2)}) %collective-permute-start.1) | collective-permute-done | bytes 172064 | tf_op jit(solution)/shard_map/ppermute | solution.py:646
  36.2 11.2 %collective-permute-done.2.refs_1_ = bf16[224,768]{1,0:T(8,128)(2,1)S(1)} collective-permute-done((bf16[224,768]{1,0:T(8,128)(2,1)S(1)}, bf16[224,768]{1,0:T(8,128)(2,1)S(1)}, u32[]{:S(2)}, u32[]{:S(2)}) %collective-permute-start.2) | collective-permute-done | bytes 344096 | tf_op jit(solution)/shard_map/ppermute | solution.py:646
  53.8 24.1 %collective-permute-done.3.refs_1_ = bf16[448,768]{1,0:T(8,128)(2,1)S(1)} collective-permute-done((bf16[448,768]{1,0:T(8,128)(2,1)S(1)}, bf16[448,768]{1,0:T(8,128)(2,1)S(1)}, u32[]{:S(2)}, u32[]{:S(2)}) %collective-permute-start.3) | collective-permute-done | bytes 688160 | tf_op jit(solution)/shard_map/ppermute | solution.py:646
  80.8 7.5 %collective-permute-done.7.refs_3_ = bf16[224,768]{1,0:T(8,128)(2,1)S(1)} collective-permute-done((bf16[224,768]{1,0:T(8,128)(2,1)S(1)}, bf16[224,768]{1,0:T(8,128)(2,1)S(1)}, u32[]{:S(2)}, u32[]{:S(2)}) %collective-permute-start.7) | collective-permute-done | bytes 344096 | tf_op jit(solution)/shard_map/ppermute | solution.py:646
  100.4 10.9 %collective-permute-done.12.refs_1_ = bf16[96,768]{1,0:T(8,128)(2,1)S(1)} collective-permute-done((bf16[96,768]{1,0:T(8,128)(2,1)S(1)}, bf16[96,768]{1,0:T(8,128)(2,1)S(1)}, u32[]{:S(2)}, u32[]{:S(2)}) %collective-permute-start.12) | collective-permute-done | bytes 147488 | tf_op jit(solution)/shard_map/ppermute | solution.py:646
  117.2 17.6 %attend.2 = (bf16[4,512,576]{2,1,0:T(8,128)(2,1)}, bf16[12,512,512]{2,1,0:T(8,128)(2,1)}, bf16[4,192,512]{2,1,0:T(8,128)(2,1)}, f32[512,768]{1,0:T(8,128)}, f32[512,1]{1,0:T(8,128)}, /*index=5*/f32[8,128]{1,0:T(8,128)}) custom-call(s32[12]{0:T(128)} %pad_add_fusion.refs_0_, bf16[512,768]{1,0:T(8,128)(2,1)} %copy-done.3, s32[512,1]{1,0:T(8,128)} %copy.72.refs_2_, ...), custom_call_target="tpu_custom_call" | custom-call | flops 4312500224 | tf_op jit(solution)/shard_map/attend/pallas_call | solution.py:254
  141.1 16.2 %collective-permute-done.15.refs_3_ = bf16[192,768]{1,0:T(8,128)(2,1)S(1)} collective-permute-done((bf16[192,768]{1,0:T(8,128)(2,1)S(1)}, bf16[192,768]{1,0:T(8,128)(2,1)S(1)}, u32[]{:S(2)}, u32[]{:S(2)}) %collective-permute-start.15) | collective-permute-done | bytes 294944 | tf_op jit(solution)/shard_map/ppermute | solution.py:646
  162.7 4.2 collective-permute-done.22.refs_3_
  174.8 13.9 %forward.2 = (bf16[512,768]{1,0:T(8,128)(2,1)}, bf16[4,512,768]{2,1,0:T(8,128)(2,1)}, bf16[4,512,768]{2,1,0:T(8,128)(2,1)}, f32[512,768]{1,0:T(8,128)}, f32[512,...) custom-call(s32[12]{0:T(128)} %pad_add_fusion.refs_0_, f32[512,768]{1,0:T(8,128)} %get-tuple-element.166.refs_1_.refs_16_, ...), custom_call_target="tpu_custom_call" | custom-call | flops 4312500224 | tf_op jit(solution)/shard_map/forward/pallas_call | solution.py:254
  188.7 18.0 %attend.3 = (bf16[4,512,576]{2,1,0:T(8,128)(2,1)}, bf16[12,512,512]{2,1,0:T(8,128)(2,1)}, bf16[4,192,512]{2,1,0:T(8,128)(2,1)}, f32[512,768]{1,0:T(8,128)}, f32[512,1]{1,0:T(8,128)}, /*index=5*/f32[8,128]{1,0:T(8,128)}) custom-call(s32[12]{0:T(128)} %pad_add_fusion.refs_0_, f32[512,768]{1,0:T(8,128)} %get-tuple-element.184.refs_1_, s32[512,1]{1,0:T(8,128)} %copy.72.refs_2_, ...), custom_call_target="tpu_custom_call" | custom-call | flops 4312500224 | tf_op jit(solution)/shard_map/attend/pallas_call | solution.py:254
  206.7 15.3 %forward.3 = (bf16[512,768]{1,0:T(8,128)(2,1)}, bf16[4,512,768]{2,1,0:T(8,128)(2,1)}, bf16[4,512,768]{2,1,0:T(8,128)(2,1)}, f32[512,768]{1,0:T(8,128)}, f32[512,...) custom-call(s32[12]{0:T(128)} %pad_add_fusion.refs_0_, f32[512,768]{1,0:T(8,128)} %get-tuple-element.186.refs_1_.refs_10_, ...), custom_call_target="tpu_custom_call" | custom-call | flops 4312500224 | tf_op jit(solution)/shard_map/forward/pallas_call | solution.py:254
  222.0 19.8 %forward_back.2 = (bf16[2,768,1536]{2,1,0:T(8,128)(2,1)}, bf16[2,768,1536]{2,1,0:T(8,128)(2,1)}, f32[512,768]{1,0:T(8,128)}, f32[3,768]{1,0:T(4,128)}, f32[3,768...) custom-call(s32[12]{0:T(128)} %pad_add_fusion.refs_0_, bf16[512,768]{1,0:T(8,128)(2,1)} %copy-done.4, ...), custom_call_target="tpu_custom_call" | custom-call | flops 43700000391168 | tf_op jit(solution)/shard_map/forward_back/pallas_call | solution.py:254
  242.5 7.6 %collective-permute-done.26 = bf16[2,768,1536]{2,1,0:T(8,128)(2,1)} collective-permute-done((bf16[2,768,1536]{2,1,0:T(8,128)(2,1)}, bf16[2,768,1536]{2,1,0:T(8,128)(2,1)}, u32[]{:S(2)}, u32[]{:S(2)}) %collective-permute-start.26) | collective-permute-done | bytes 4718624 | tf_op jit(solution)/shard_map/ppermute | solution.py:646
  253.1 5.7 %merge_core.4 = (bf16[2,192,1536]{2,1,0:T(8,128)(2,1)}, bf16[2,192,1536]{2,1,0:T(8,128)(2,1)S(1)}, bf16[2,192,1536]{2,1,0:T(8,128)(2,1)}, bf16[2,192,1536]{2,1,0:T(8,128)(2,1)S(1)}, f32[8,128]{1,0:T(8,128)S(1)}) custom-call(bf16[2,2,2,192,1536]{4,3,2,1,0:T(8,128)(2,1)S(1)} %bitcast.139, bf16[2,2,2,192,1536]{4,3,2,1,0:T(8,128)(2,1)} %bitcast.41.refs_1_, ...), custom_call_target="tpu_custom_call" | custom-call | flops 4600000151552 | tf_op jit(solution)/shard_map/merge_core/pallas_call | solution.py:604
  262.6 23.8 %attend_back.2 = (bf16[2,896,768]{2,1,0:T(8,128)(2,1)}, bf16[2,896,768]{2,1,0:T(8,128)(2,1)}, f32[512,768]{1,0:T(8,128)}, f32[8,128]{1,0:T(8,128)}) custom-call(s32[12]{0:T(128)} %pad_add_fusion.refs_0_, f32[512,768]{1,0:T(8,128)} %get-tuple-element.184.refs_1_, f32[512,768]{1,0:T(8,128)} %get-tuple-element.195.refs_2_, ...), custom_call_target="tpu_custom_call" | custom-call | flops 50599999569920 | tf_op jit(solution)/shard_map/attend_back/pallas_call | solution.py:254
  295.8 4.0 merge_core.5
  301.8 19.3 %forward_back.3 = (bf16[2,768,1536]{2,1,0:T(8,128)(2,1)}, bf16[2,768,1536]{2,1,0:T(8,128)(2,1)}, f32[512,768]{1,0:T(8,128)}, f32[3,768]{1,0:T(4,128)}, f32[3,768...) custom-call(s32[12]{0:T(128)} %pad_add_fusion.refs_0_, f32[512,768]{1,0:T(8,128)} %get-tuple-element.206.refs_1_, ...), custom_call_target="tpu_custom_call" | custom-call | flops 43700000391168 | tf_op jit(solution)/shard_map/forward_back/pallas_call | solution.py:254
  330.5 5.9 %merge_core.6 = (bf16[2,192,1536]{2,1,0:T(8,128)(2,1)}, bf16[2,192,1536]{2,1,0:T(8,128)(2,1)S(1)}, bf16[2,192,1536]{2,1,0:T(8,128)(2,1)}, bf16[2,192,1536]{2,1,0:T(8,128)(2,1)S(1)}, f32[8,128]{1,0:T(8,128)S(1)}) custom-call(bf16[2,2,2,192,1536]{4,3,2,1,0:T(8,128)(2,1)S(1)} %bitcast.138, bf16[2,2,2,192,1536]{4,3,2,1,0:T(8,128)(2,1)} %bitcast.45.refs_1_, ...), custom_call_target="tpu_custom_call" | custom-call | flops 4600000151552 | tf_op jit(solution)/shard_map/merge_core/pallas_call | solution.py:604
  338.6 23.4 %attend_back.3 = (bf16[2,896,768]{2,1,0:T(8,128)(2,1)}, bf16[2,896,768]{2,1,0:T(8,128)(2,1)}, f32[512,768]{1,0:T(8,128)}, f32[8,128]{1,0:T(8,128)}) custom-call(s32[12]{0:T(128)} %pad_add_fusion.refs_0_, bf16[512,768]{1,0:T(8,128)(2,1)} %copy-done.3, f32[512,768]{1,0:T(8,128)} %get-tuple-element.245.refs_2_, ...), custom_call_target="tpu_custom_call" | custom-call | flops 50599999569920 | tf_op jit(solution)/shard_map/attend_back/pallas_call | solution.py:254
  367.4 4.3 collective-permute-start.55
  386.1 19.9 %collective-permute-done.43.refs_1_ = bf16[2,224,768]{2,1,0:T(8,128)(2,1)S(1)} collective-permute-done((bf16[2,224,768]{2,1,0:T(8,128)(2,1)S(1)}, bf16[2,224,768]{2,1,0:T(8,128)(2,1)S(1)}, u32[]{:S(2)}, u32[]{:S(2)}) %collective-permute-start.43) | collective-permute-done | bytes 688160 | tf_op jit(solution)/shard_map/ppermute | solution.py:646
  421.5 12.7 %collective-permute-done.46.refs_1_ = bf16[192,1536]{1,0:T(8,128)(2,1)} collective-permute-done((bf16[192,1536]{1,0:T(8,128)(2,1)}, bf16[192,1536]{1,0:T(8,128)(2,1)}, u32[]{:S(2)}, u32[]{:S(2)}) %collective-permute-start.46) | collective-permute-done | bytes 589856 | tf_op jit(solution)/shard_map/ppermute | solution.py:646
  447.6 5.9 %collective-permute-done.52 = bf16[112,768]{1,0:T(8,128)(2,1)S(1)} collective-permute-done((bf16[112,768]{1,0:T(8,128)(2,1)S(1)}, bf16[112,768]{1,0:T(8,128)(2,1)S(1)}, u32[]{:S(2)}, u32[]{:S(2)}) %collective-permute-start.52) | collective-permute-done | bytes 172064 | tf_op jit(solution)/shard_map/ppermute | solution.py:646
  (342 shorter events, 148.1 us)
Async XLA Ops:
  7.2 181.5 %all-gather.2.cloned.1.call-start = ((), (), s32[]{:S(2)}) async-start(), calls=%async_computation | async-start | bytes 14598144 | tf_op jit(solution)/shard_map/all_gather | solution.py:811
  18.1 33.9 %collective-permute-start = (bf16[256,768]{1,0:T(8,128)(2,1)}, bf16[256,768]{1,0:T(8,128)(2,1)S(1)}, u32[]{:S(2)}, u32[]{:S(2)}) collective-permute-start(bf16[256,768]{1,0:T(8,128)(2,1)} %dynamic-slice_bitcast_fusion.1), channel_id=1, source_target_pairs={{0,1},{1,0},{2,3},{3,2},{4,5},{5,4},{6,7},{7,6},{8,9},{9,8},{10,11... | collective-permute-start | bytes 1179656 | tf_op jit(solution)/shard_map/ppermute | solution.py:646
  18.6 34.6 %collective-permute-start.5 = (bf16[96,768]{1,0:T(8,128)(2,1)S(1)}, bf16[96,768]{1,0:T(8,128)(2,1)S(1)}, u32[]{:S(2)}, u32[]{:S(2)}) collective-permute-start(bf16[96,768]{1,0:T(8,128)(2,1)S(1)} %get-tuple-element.349.refs_0_), channel_id=1, source_target_pairs={{0,16},{4,20},{8,24},{12,28},{16,0},{20,4},{24,8},{28,12},{1,17},{... | collective-permute-start | bytes 442376 | tf_op jit(solution)/shard_map/ppermute | solution.py:646
  48.0 29.9 %collective-permute-start.3 = (bf16[448,768]{1,0:T(8,128)(2,1)S(1)}, bf16[448,768]{1,0:T(8,128)(2,1)S(1)}, u32[]{:S(2)}, u32[]{:S(2)}) collective-permute-start(bf16[448,768]{1,0:T(8,128)(2,1)S(1)} %get-tuple-element.154.refs_0_), channel_id=1, source_target_pairs={{0,4},{4,0},{8,12},{12,8},{16,20},{20,16},{24,28},{28,24},{1,5},{5... | collective-permute-start | bytes 2064392 | tf_op jit(solution)/shard_map/ppermute | solution.py:646
  49.6 28.3 %collective-permute-start.4 = (bf16[448,768]{1,0:T(8,128)(2,1)S(1)}, bf16[448,768]{1,0:T(8,128)(2,1)S(1)}, u32[]{:S(2)}, u32[]{:S(2)}) collective-permute-start(bf16[448,768]{1,0:T(8,128)(2,1)S(1)} %get-tuple-element.154.refs_0_), channel_id=1, source_target_pairs={{0,2},{1,3},{2,0},{3,1},{4,6},{5,7},{6,4},{7,5},{8,10},{9,11},{10,... | collective-permute-start | bytes 2064392 | tf_op jit(solution)/shard_map/ppermute | solution.py:646
  53.7 26.8 %collective-permute-start.9 = (bf16[192,768]{1,0:T(8,128)(2,1)S(1)}, bf16[192,768]{1,0:T(8,128)(2,1)S(1)}, u32[]{:S(2)}, u32[]{:S(2)}) collective-permute-start(bf16[192,768]{1,0:T(8,128)(2,1)S(1)} %get-tuple-element.159.refs_0_), channel_id=1, source_target_pairs={{0,8},{4,12},{8,0},{12,4},{16,24},{20,28},{24,16},{28,20},{1,9},{5... | collective-permute-start | bytes 884744 | tf_op jit(solution)/shard_map/ppermute | solution.py:646
  96.6 38.2 %collective-permute-start.13 = (bf16[384,768]{1,0:T(8,128)(2,1)S(1)}, bf16[384,768]{1,0:T(8,128)(2,1)S(1)}, u32[]{:S(2)}, u32[]{:S(2)}) collective-permute-start(bf16[384,768]{1,0:T(8,128)(2,1)S(1)} %get-tuple-element.167.refs_0_), channel_id=1, source_target_pairs={{0,4},{4,0},{8,12},{12,8},{16,20},{20,16},{24,28},{28,24},{1,5},{5... | collective-permute-start | bytes 1769480 | tf_op jit(solution)/shard_map/ppermute | solution.py:646
  98.2 36.6 %collective-permute-start.14 = (bf16[384,768]{1,0:T(8,128)(2,1)S(1)}, bf16[384,768]{1,0:T(8,128)(2,1)S(1)}, u32[]{:S(2)}, u32[]{:S(2)}) collective-permute-start(bf16[384,768]{1,0:T(8,128)(2,1)S(1)} %get-tuple-element.167.refs_0_), channel_id=1, source_target_pairs={{0,2},{1,3},{2,0},{3,1},{4,6},{5,7},{6,4},{7,5},{8,10},{9,11},{10,... | collective-permute-start | bytes 1769480 | tf_op jit(solution)/shard_map/ppermute | solution.py:646
  259.5 28.3 %collective-permute-start.28 = (bf16[2,192,1536]{2,1,0:T(8,128)(2,1)}, bf16[2,192,1536]{2,1,0:T(8,128)(2,1)}, u32[]{:S(2)}, u32[]{:S(2)}) collective-permute-start(bf16[2,192,1536]{2,1,0:T(8,128)(2,1)} %get-tuple-element.216), channel_id=1, source_target_pairs={{0,2},{1,3},{2,0},{3,1},{4,6},{5,7},{6,4},{7,5},{8,10},{9,11},{10,... | collective-permute-start | bytes 3538952 | tf_op jit(solution)/shard_map/ppermute | solution.py:646
  261.1 28.0 %collective-permute-start.29 = (bf16[2,192,1536]{2,1,0:T(8,128)(2,1)}, bf16[2,192,1536]{2,1,0:T(8,128)(2,1)}, u32[]{:S(2)}, u32[]{:S(2)}) collective-permute-start(bf16[2,192,1536]{2,1,0:T(8,128)(2,1)} %get-tuple-element.218), channel_id=1, source_target_pairs={{0,4},{4,0},{8,12},{12,8},{16,20},{20,16},{24,28},{28,24},{1,5},{5... | collective-permute-start | bytes 3538952 | tf_op jit(solution)/shard_map/ppermute | solution.py:646
  293.7 27.4 %collective-permute-start.33 = (bf16[192,1536]{1,0:T(8,128)(2,1)}, bf16[192,1536]{1,0:T(8,128)(2,1)}, u32[]{:S(2)}, u32[]{:S(2)}) collective-permute-start(bf16[192,1536]{1,0:T(8,128)(2,1)} %get-tuple-element.229), channel_id=1, source_target_pairs={{0,4},{4,0},{8,12},{12,8},{16,20},{20,16},{24,28},{28,24},{1,5},{5... | collective-permute-start | bytes 1769480 | tf_op jit(solution)/shard_map/ppermute | solution.py:646
  295.2 26.0 %collective-permute-start.34 = (bf16[192,1536]{1,0:T(8,128)(2,1)}, bf16[192,1536]{1,0:T(8,128)(2,1)}, u32[]{:S(2)}, u32[]{:S(2)}) collective-permute-start(bf16[192,1536]{1,0:T(8,128)(2,1)} %get-tuple-element.231), channel_id=1, source_target_pairs={{0,2},{1,3},{2,0},{3,1},{4,6},{5,7},{6,4},{7,5},{8,10},{9,11},{10,... | collective-permute-start | bytes 1769480 | tf_op jit(solution)/shard_map/ppermute | solution.py:646
  299.7 26.4 %collective-permute-start.31 = (bf16[2,224,768]{2,1,0:T(8,128)(2,1)}, bf16[2,224,768]{2,1,0:T(8,128)(2,1)}, u32[]{:S(2)}, u32[]{:S(2)}) collective-permute-start(bf16[2,224,768]{2,1,0:T(8,128)(2,1)} %get-tuple-element.225), channel_id=1, source_target_pairs={{0,2},{1,3},{2,0},{3,1},{4,6},{5,7},{6,4},{7,5},{8,10},{9,11},{10,... | collective-permute-start | bytes 2064392 | tf_op jit(solution)/shard_map/ppermute | solution.py:646
  301.2 25.0 %collective-permute-start.32 = (bf16[2,224,768]{2,1,0:T(8,128)(2,1)}, bf16[2,224,768]{2,1,0:T(8,128)(2,1)}, u32[]{:S(2)}, u32[]{:S(2)}) collective-permute-start(bf16[2,224,768]{2,1,0:T(8,128)(2,1)} %get-tuple-element.227), channel_id=1, source_target_pairs={{0,4},{4,0},{8,12},{12,8},{16,20},{20,16},{24,28},{28,24},{1,5},{5... | collective-permute-start | bytes 2064392 | tf_op jit(solution)/shard_map/ppermute | solution.py:646
  324.9 37.2 %collective-permute-start.39 = (bf16[192,1536]{1,0:T(8,128)(2,1)}, bf16[192,1536]{1,0:T(8,128)(2,1)}, u32[]{:S(2)}, u32[]{:S(2)}) collective-permute-start(bf16[192,1536]{1,0:T(8,128)(2,1)} %get-tuple-element.244), channel_id=1, source_target_pairs={{0,8},{4,12},{8,0},{12,4},{16,24},{20,28},{24,16},{28,20},{1,9},{5... | collective-permute-start | bytes 1769480 | tf_op jit(solution)/shard_map/ppermute | solution.py:646
  328.6 36.2 %collective-permute-start.37 = (bf16[224,768]{1,0:T(8,128)(2,1)}, bf16[224,768]{1,0:T(8,128)(2,1)}, u32[]{:S(2)}, u32[]{:S(2)}) collective-permute-start(bf16[224,768]{1,0:T(8,128)(2,1)} %get-tuple-element.240), channel_id=1, source_target_pairs={{0,4},{4,0},{8,12},{12,8},{16,20},{20,16},{24,28},{28,24},{1,5},{5... | collective-permute-start | bytes 1032200 | tf_op jit(solution)/shard_map/ppermute | solution.py:646
  330.0 34.8 %collective-permute-start.38 = (bf16[224,768]{1,0:T(8,128)(2,1)}, bf16[224,768]{1,0:T(8,128)(2,1)}, u32[]{:S(2)}, u32[]{:S(2)}) collective-permute-start(bf16[224,768]{1,0:T(8,128)(2,1)} %get-tuple-element.242), channel_id=1, source_target_pairs={{0,2},{1,3},{2,0},{3,1},{4,6},{5,7},{6,4},{7,5},{8,10},{9,11},{10,... | collective-permute-start | bytes 1032200 | tf_op jit(solution)/shard_map/ppermute | solution.py:646
  336.5 35.3 %collective-permute-start.35 = (bf16[2,192,1536]{2,1,0:T(8,128)(2,1)}, bf16[2,192,1536]{2,1,0:T(8,128)(2,1)}, u32[]{:S(2)}, u32[]{:S(2)}) collective-permute-start(bf16[2,192,1536]{2,1,0:T(8,128)(2,1)} %get-tuple-element.236), channel_id=1, source_target_pairs={{0,2},{1,3},{2,0},{3,1},{4,6},{5,7},{6,4},{7,5},{8,10},{9,11},{10,... | collective-permute-start | bytes 3538952 | tf_op jit(solution)/shard_map/ppermute | solution.py:646
  338.0 33.7 %collective-permute-start.36 = (bf16[2,192,1536]{2,1,0:T(8,128)(2,1)}, bf16[2,192,1536]{2,1,0:T(8,128)(2,1)}, u32[]{:S(2)}, u32[]{:S(2)}) collective-permute-start(bf16[2,192,1536]{2,1,0:T(8,128)(2,1)} %get-tuple-element.238), channel_id=1, source_target_pairs={{0,4},{4,0},{8,12},{12,8},{16,20},{20,16},{24,28},{28,24},{1,5},{5... | collective-permute-start | bytes 3538952 | tf_op jit(solution)/shard_map/ppermute | solution.py:646
  366.7 52.5 %collective-permute-start.47 = (bf16[224,768]{1,0:T(8,128)(2,1)}, bf16[224,768]{1,0:T(8,128)(2,1)}, u32[]{:S(2)}, u32[]{:S(2)}) collective-permute-start(bf16[224,768]{1,0:T(8,128)(2,1)} %get-tuple-element.274), channel_id=1, source_target_pairs={{0,8},{4,12},{8,0},{12,4},{16,24},{20,28},{24,16},{28,20},{1,9},{5... | collective-permute-start | bytes 1032200 | tf_op jit(solution)/shard_map/ppermute | solution.py:646
  374.8 33.6 %collective-permute-start.40 = (bf16[192,1536]{1,0:T(8,128)(2,1)}, bf16[192,1536]{1,0:T(8,128)(2,1)}, u32[]{:S(2)}, u32[]{:S(2)}) collective-permute-start(bf16[192,1536]{1,0:T(8,128)(2,1)} %get-tuple-element.257), channel_id=1, source_target_pairs={{0,4},{4,0},{8,12},{12,8},{16,20},{20,16},{24,28},{28,24},{1,5},{5... | collective-permute-start | bytes 1769480 | tf_op jit(solution)/shard_map/ppermute | solution.py:646
  376.2 32.3 %collective-permute-start.41 = (bf16[192,1536]{1,0:T(8,128)(2,1)}, bf16[192,1536]{1,0:T(8,128)(2,1)}, u32[]{:S(2)}, u32[]{:S(2)}) collective-permute-start(bf16[192,1536]{1,0:T(8,128)(2,1)} %get-tuple-element.259), channel_id=1, source_target_pairs={{0,2},{1,3},{2,0},{3,1},{4,6},{5,7},{6,4},{7,5},{8,10},{9,11},{10,... | collective-permute-start | bytes 1769480 | tf_op jit(solution)/shard_map/ppermute | solution.py:646
  379.8 26.2 %collective-permute-start.43 = (bf16[2,224,768]{2,1,0:T(8,128)(2,1)S(1)}, bf16[2,224,768]{2,1,0:T(8,128)(2,1)S(1)}, u32[]{:S(2)}, u32[]{:S(2)}) collective-permute-start(bf16[2,224,768]{2,1,0:T(8,128)(2,1)S(1)} %get-tuple-element.264), channel_id=1, source_target_pairs={{0,2},{1,3},{2,0},{3,1},{4,6},{5,7},{6,4},{7,5},{8,10},{9,11},{10,... | collective-permute-start | bytes 2064392 | tf_op jit(solution)/shard_map/ppermute | solution.py:646
  414.0 30.9 %collective-permute-start.45 = (f32[256,768]{1,0:T(8,128)}, f32[256,768]{1,0:T(8,128)}, u32[]{:S(2)}, u32[]{:S(2)}) collective-permute-start(f32[256,768]{1,0:T(8,128)} %constant_dynamic-slice_fusion.3), channel_id=1, source_target_pairs={{0,1},{1,0},{2,3},{3,2},{4,5},{5,4},{6,7},{7,6},{8,9},{9,8},{10,11... | collective-permute-start | bytes 2359304 | tf_op jit(solution)/shard_map/ppermute | solution.py:646
  (86 other events, 833.7 us)
Sparse Core Ops, SparseCore 0:
  11.6 136.9 all-gather.1

commit v4 on v3

--- a/solution.py
+++ b/solution.py
@@ -14,7 +14,7 @@
 BF16 = jnp.bfloat16
 STREAM_BYTES = 60 * 1024 * 1024
 MERGE_BYTES = 32 * 1024 * 1024
-FORWARD_SCALE, BACKWARD_SCALE = 0.25, 2000
+FORWARD_SCALE, BACKWARD_SCALE = 0.5, 100
 
 
 def lasting(microseconds, scale):
@@ -262,7 +262,6 @@
     for inlet in (doc_col, doc_row, vec, q_bias, v_bias, x):
         inlet.start()
     weights.start(0)
-    weights.start(1)
     for inlet in (doc_col, doc_row, vec, q_bias, v_bias, x):
         inlet.wait()
     low_ref[...] = x.held[...].astype(BF16)
@@ -270,8 +269,8 @@
     same_doc = doc_col.held[...] == doc_row.held[...]
     for step in range(steps):
         weights.wait(step)
-        if step + 2 < steps:
-            weights.start(step + 2)
+        if step + 1 < steps:
+            weights.start(step + 1)
         projected = dot_nn(low_ref[...], weights.held[step, :, : 3 * width])
         queries = (projected[:, :width] + q_bias.held[step]).astype(BF16) * jnp.asarray(0.125, BF16)
         key_rows = projected[:, width : 2 * width].astype(BF16)
@@ -331,9 +330,8 @@
     steps = bias.held.shape[0]
     for inlet in (vec, vec_two, bias, normal):
         inlet.start()
-    for step in range(2):
-        first.start(step)
-        second.start(step)
+    first.start(0)
+    second.start(0)
     for inlet in (vec, vec_two, bias, normal):
         inlet.wait()
     rows = normal.held[...] * vec.held[1:2] + vec.held[2:3]
@@ -344,9 +342,9 @@
     for step in range(steps):
         first.wait(step)
         second.wait(step)
-        if step + 2 < steps:
-            first.start(step + 2)
-            second.start(step + 2)
+        if step + 1 < steps:
+            first.start(step + 1)
+            second.start(step + 1)
         hidden = dot_nn(low_ref[...], first.held[step]) + bias.held[step]
         below = 0.5 + 0.5 * lax.erf(hidden * ROOT_HALF)
         value = (hidden * below).astype(BF16)
@@ -402,7 +400,6 @@
 
     bring(0)
     low.start()
-    bring(1)
     upstream, normal_value = up.held[...].astype(F32), normal_two.held[...]
     grad = norm_back(upstream, normal_value, scale_two.held[...], vec_two.held[1:2])
     low_two_ref[...] = grad.astype(BF16)
@@ -414,9 +411,9 @@
             inlet.wait(step)
         if step == 0:
             low.wait()
-        if step + 2 < steps:
-            bring(step + 2)
-        elif step + 2 == steps:
+        if step + 1 < steps:
+            bring(step + 1)
+        if step + 2 == steps:
             for inlet in (scale, vec, normal):
                 inlet.start()
         grads.held[step, :, width:] = dot_tn(low_two_ref[...], active.held[step]).astype(BF16)
@@ -483,7 +480,6 @@
     grad_one.start()
     bring(0)
     x.start()
-    bring(1)
     for inlet in (unit_sums, sums_one, sums_two):
         inlet.start()
     grad_one.wait()
@@ -501,8 +497,8 @@
         if step == 0:
             x.wait()
             x_low_ref[...] = x.held[...].astype(BF16)
-        if step + 2 < steps:
-            bring(step + 2)
+        if step + 1 < steps:
+            bring(step + 1)
         block = qkv.held[step]
         queries, key_rows = block[:, :width], block[:, width : 2 * width]
         value_rows = block[:, 2 * width :]
@@ -981,11 +977,6 @@
         )
         shards += [in_weight[layer], down_turned[layer]]
 
-    weights = {}
-    for layer in GATHERED:
-        for kind, group in enumerate(gather_common(shards[3 * layer : 3 * layer + 3], places, from_common)):
-            weights[3 * layer + kind] = group
-
     doc_ids = segment_ids[core, tensor_at // 2]
     current = dot_nn(to_sequence(tokens, core), place).astype(BF16)
     upstream = dot_nn(to_sequence(cotangent, core), place).astype(BF16)
@@ -1002,7 +993,7 @@
     filled = -(-piece // 16) * 16
     shards[0] = joined(padded(shards[0], filled), padded(extra, EXTRA))
 
-    coming = {at: gather_group(shard, places) for at, shard in enumerate(shards) if at not in weights}
+    coming = {at: gather_group(shard, places) for at, shard in enumerate(shards) if at // 3 not in GATHERED}
     for group in coming.values():
         next(group)
     steps = len(dp_bits(parts)) - 1
@@ -1012,6 +1003,14 @@
         nonlocal last
         last = (coming[index].send(tuple(last) + tuple(after)),)
         return next(coming[index])
+
+    for _ in range(steps):
+        turn(0)
+    weights = {}
+    for layer in GATHERED:
+        own = [gated(shard, last[0]) for shard in shards[3 * layer : 3 * layer + 3]]
+        for kind, group in enumerate(gather_common(own, places, from_common)):
+            weights[3 * layer + kind] = group
 
     ready = (current, upstream)
     saved = []
@@ -1019,7 +1018,7 @@
         at = 3 * layer
         entered = current
         if at in coming:
-            for _ in range(steps):
+            for _ in range(steps if at else 0):
                 turn(at)
             for _ in range(steps - 1):
                 turn(at + 1)
@@ -1115,11 +1114,11 @@
         launch((layer, 0), grads)
         push(*flights)
     first, second, third, final = list(flights)
-    push(first, final, third)
+    push(first, second, final, third)
+    grad_tokens = from_sequence(reorder(upstream, place, last), core)
+    push(final, second, third)
     output = from_sequence(reorder(current, place, last), core)
-    push(final, second, third)
-    grad_tokens = from_sequence(reorder(upstream, place, last), core)
-    push(final, second, third, final)
+    push(final)
     while flights:
         push(*list(flights))
     tops = jnp.stack([owned[layer, 0][-EXTRA:] for layer in range(layers)])

time: 478 us -> 466 us (0.975)
  waiting for transfers between devices: 142 us -> 123 us
    ppermute x56, waiting for transfers between devices: 142 us -> 123 us  [trade(): lax.ppermute(values, axis, [(i, i ^ 1 << bit) for i in range(lax.axis_siz...]
    unnamed x112 -> x114, local copies, waits for them, and re-layouts: 14.3 us -> 14 us
  transfers between devices with their start and end apart: 57 -> 57, of which waited for: 21 -> 22; matrix products, arithmetic and copies ran while one was open for 8% -> 8% of each run, Pallas kernels for 31% -> 32%
where the time goes in v4:
time: 466 us; the launch traced here: 461 us
  Pallas kernels  208 us (45%)
  waiting for transfers between devices  123 us (26%)
  starting transfers between devices  58.7 us (13%)
  local copies, waits for them, and re-layouts  34 us (7%)
  other arithmetic  19.5 us (4%)
  between operations  15.4 us (3%)
    pallas_call x8, Pallas kernels, streamed(): return kernel(table, *operands, *after)  147 us
    ppermute x56, waiting for transfers between devices, trade(): lax.ppermute(values, axis, [(i, i ^ 1 << bit) for i in range(lax.axis_siz...  123 us
    ppermute x56, starting transfers between devices, trade(): lax.ppermute(values, axis, [(i, i ^ 1 << bit) for i in range(lax.axis_siz...  58.7 us
    pallas_call x18, Pallas kernels, run(): made = kernel(*args, *after)  48.3 us
    unnamed x114, local copies, waits for them, and re-layouts  14 us
    pallas_call x12, Pallas kernels, moved(): pl.pallas_call(body, in_specs=[ANYWHERE] * (count + waits), out_specs=[AN...  11.8 us
  transfers between devices with their start and end apart: 57, of which 22 were waited for; matrix products, arithmetic and copies ran while one was open for 8% of the time, Pallas kernels for 32%

profile of v4, /device:TPU:0, one launch (start us, length us, event | category | flops | bytes accessed | tf_op | source)
XLA Modules:
  0.0 460.7 jit_solution(10749546527853813)
XLA Ops:
  12.4 4.1 collective-permute-start.1
  16.5 8.1 %collective-permute-done.1.refs_1_ = bf16[112,768]{1,0:T(8,128)(2,1)S(1)} collective-permute-done((bf16[112,768]{1,0:T(8,128)(2,1)S(1)}, bf16[112,768]{1,0:T(8,128)(2,1)S(1)}, u32[]{:S(2)}, u32[]{:S(2)}) %collective-permute-start.1) | collective-permute-done | bytes 172064 | tf_op jit(solution)/shard_map/ppermute | solution.py:642
  25.9 8.5 %collective-permute-done.2.refs_1_ = bf16[224,768]{1,0:T(8,128)(2,1)S(1)} collective-permute-done((bf16[224,768]{1,0:T(8,128)(2,1)S(1)}, bf16[224,768]{1,0:T(8,128)(2,1)S(1)}, u32[]{:S(2)}, u32[]{:S(2)}) %collective-permute-start.2) | collective-permute-done | bytes 344096 | tf_op jit(solution)/shard_map/ppermute | solution.py:642
  50.5 10.9 %collective-permute-done.5.refs_1_ = bf16[96,768]{1,0:T(8,128)(2,1)S(1)} collective-permute-done((bf16[96,768]{1,0:T(8,128)(2,1)S(1)}, bf16[96,768]{1,0:T(8,128)(2,1)S(1)}, u32[]{:S(2)}, u32[]{:S(2)}) %collective-permute-start.5) | collective-permute-done | bytes 147488 | tf_op jit(solution)/shard_map/ppermute | solution.py:642
  66.8 5.7 %collective-permute-done.9.refs_1_ = bf16[192,768]{1,0:T(8,128)(2,1)S(1)} collective-permute-done((bf16[192,768]{1,0:T(8,128)(2,1)S(1)}, bf16[192,768]{1,0:T(8,128)(2,1)S(1)}, u32[]{:S(2)}, u32[]{:S(2)}) %collective-permute-start.9) | collective-permute-done | bytes 294944 | tf_op jit(solution)/shard_map/ppermute | solution.py:642
  77.6 7.1 %collective-permute-start.12 = (bf16[96,768]{1,0:T(8,128)(2,1)S(1)}, bf16[96,768]{1,0:T(8,128)(2,1)}, u32[]{:S(2)}, u32[]{:S(2)}) collective-permute-start(bf16[96,768]{1,0:T(8,128)(2,1)S(1)} %get-tuple-element.355.refs_0_), channel_id=1, source_target_pairs={{0,16},{4,20},{8,24},{12,28},{16,0},{20,4},{24,8},{28,12},{1,17},{... | collective-permute-start | bytes 442376 | tf_op jit(solution)/shard_map/ppermute | solution.py:642
  89.5 9.5 %collective-permute-done.12.refs_1_ = bf16[96,768]{1,0:T(8,128)(2,1)} collective-permute-done((bf16[96,768]{1,0:T(8,128)(2,1)S(1)}, bf16[96,768]{1,0:T(8,128)(2,1)}, u32[]{:S(2)}, u32[]{:S(2)}) %collective-permute-start.12) | collective-permute-done | bytes 147488 | tf_op jit(solution)/shard_map/ppermute | solution.py:642
  105.6 17.6 %attend.2 = (bf16[4,512,576]{2,1,0:T(8,128)(2,1)}, bf16[12,512,512]{2,1,0:T(8,128)(2,1)}, bf16[4,192,512]{2,1,0:T(8,128)(2,1)}, f32[512,768]{1,0:T(8,128)}, f32[512,1]{1,0:T(8,128)}, /*index=5*/f32[8,128]{1,0:T(8,128)}) custom-call(s32[12]{0:T(128)} %pad_add_fusion.refs_0_, bf16[512,768]{1,0:T(8,128)(2,1)} %copy-done.16, s32[512,1]{1,0:T(8,128)} %copy.72.refs_2_, ...), custom_call_target="tpu_custom_call" | custom-call | flops 8625000448 | tf_op jit(solution)/shard_map/attend/pallas_call | solution.py:254
  130.4 21.4 %collective-permute-done.15.refs_3_ = bf16[192,768]{1,0:T(8,128)(2,1)S(1)} collective-permute-done((bf16[192,768]{1,0:T(8,128)(2,1)S(1)}, bf16[192,768]{1,0:T(8,128)(2,1)S(1)}, u32[]{:S(2)}, u32[]{:S(2)}) %collective-permute-start.15) | collective-permute-done | bytes 294944 | tf_op jit(solution)/shard_map/ppermute | solution.py:642
  156.7 6.2 %collective-permute-done.22.refs_3_ = bf16[192,768]{1,0:T(8,128)(2,1)S(1)} collective-permute-done((bf16[192,768]{1,0:T(8,128)(2,1)S(1)}, bf16[192,768]{1,0:T(8,128)(2,1)S(1)}, u32[]{:S(2)}, u32[]{:S(2)}) %collective-permute-start.22) | collective-permute-done | bytes 294944 | tf_op jit(solution)/shard_map/ppermute | solution.py:642
  171.6 13.5 %forward.2 = (bf16[512,768]{1,0:T(8,128)(2,1)}, bf16[4,512,768]{2,1,0:T(8,128)(2,1)}, bf16[4,512,768]{2,1,0:T(8,128)(2,1)}, f32[512,768]{1,0:T(8,128)}, f32[512,...) custom-call(s32[12]{0:T(128)} %pad_add_fusion.refs_0_, f32[512,768]{1,0:T(8,128)} %get-tuple-element.166.refs_1_.refs_16_, ...), custom_call_target="tpu_custom_call" | custom-call | flops 8625000448 | tf_op jit(solution)/shard_map/forward/pallas_call | solution.py:254
  185.2 17.7 %attend.3 = (bf16[4,512,576]{2,1,0:T(8,128)(2,1)}, bf16[12,512,512]{2,1,0:T(8,128)(2,1)}, bf16[4,192,512]{2,1,0:T(8,128)(2,1)}, f32[512,768]{1,0:T(8,128)}, f32[512,1]{1,0:T(8,128)}, /*index=5*/f32[8,128]{1,0:T(8,128)}) custom-call(s32[12]{0:T(128)} %pad_add_fusion.refs_0_, f32[512,768]{1,0:T(8,128)} %get-tuple-element.184.refs_1_, s32[512,1]{1,0:T(8,128)} %copy.72.refs_2_, ...), custom_call_target="tpu_custom_call" | custom-call | flops 8625000448 | tf_op jit(solution)/shard_map/attend/pallas_call | solution.py:254
  202.8 14.6 %forward.3 = (bf16[512,768]{1,0:T(8,128)(2,1)}, bf16[4,512,768]{2,1,0:T(8,128)(2,1)}, bf16[4,512,768]{2,1,0:T(8,128)(2,1)}, f32[512,768]{1,0:T(8,128)}, f32[512,...) custom-call(s32[12]{0:T(128)} %pad_add_fusion.refs_0_, f32[512,768]{1,0:T(8,128)} %get-tuple-element.186.refs_1_.refs_10_, ...), custom_call_target="tpu_custom_call" | custom-call | flops 8625000448 | tf_op jit(solution)/shard_map/forward/pallas_call | solution.py:254
  217.5 19.1 %forward_back.2 = (bf16[2,768,1536]{2,1,0:T(8,128)(2,1)}, bf16[2,768,1536]{2,1,0:T(8,128)(2,1)}, f32[512,768]{1,0:T(8,128)}, f32[3,768]{1,0:T(4,128)}, f32[3,768...) custom-call(s32[12]{0:T(128)} %pad_add_fusion.refs_0_, bf16[512,768]{1,0:T(8,128)(2,1)} %copy-done.17, ...), custom_call_target="tpu_custom_call" | custom-call | flops 2184999993344 | tf_op jit(solution)/shard_map/forward_back/pallas_call | solution.py:254
  237.4 7.7 %collective-permute-done.26 = bf16[2,768,1536]{2,1,0:T(8,128)(2,1)} collective-permute-done((bf16[2,768,1536]{2,1,0:T(8,128)(2,1)}, bf16[2,768,1536]{2,1,0:T(8,128)(2,1)}, u32[]{:S(2)}, u32[]{:S(2)}) %collective-permute-start.26) | collective-permute-done | bytes 4718624 | tf_op jit(solution)/shard_map/ppermute | solution.py:642
  248.2 5.7 %merge_core.4 = (bf16[2,192,1536]{2,1,0:T(8,128)(2,1)}, bf16[2,192,1536]{2,1,0:T(8,128)(2,1)S(1)}, bf16[2,192,1536]{2,1,0:T(8,128)(2,1)}, bf16[2,192,1536]{2,1,0:T(8,128)(2,1)S(1)}, f32[8,128]{1,0:T(8,128)S(1)}) custom-call(bf16[2,2,2,192,1536]{4,3,2,1,0:T(8,128)(2,1)S(1)} %bitcast.142, bf16[2,2,2,192,1536]{4,3,2,1,0:T(8,128)(2,1)} %bitcast.42.refs_1_, ...), custom_call_target="tpu_custom_call" | custom-call | flops 230000001024 | tf_op jit(solution)/shard_map/merge_core/pallas_call | solution.py:600
  256.5 23.0 %attend_back.2 = (bf16[2,896,768]{2,1,0:T(8,128)(2,1)}, bf16[2,896,768]{2,1,0:T(8,128)(2,1)}, f32[512,768]{1,0:T(8,128)}, f32[8,128]{1,0:T(8,128)}) custom-call(s32[12]{0:T(128)} %pad_add_fusion.refs_0_, f32[512,768]{1,0:T(8,128)} %get-tuple-element.184.refs_1_, f32[512,768]{1,0:T(8,128)} %get-tuple-element.195.refs_2_, ...), custom_call_target="tpu_custom_call" | custom-call | flops 2529999978496 | tf_op jit(solution)/shard_map/attend_back/pallas_call | solution.py:254
  289.7 4.0 merge_core.5
  295.7 19.3 %forward_back.3 = (bf16[2,768,1536]{2,1,0:T(8,128)(2,1)}, bf16[2,768,1536]{2,1,0:T(8,128)(2,1)}, f32[512,768]{1,0:T(8,128)}, f32[3,768]{1,0:T(4,128)}, f32[3,768...) custom-call(s32[12]{0:T(128)} %pad_add_fusion.refs_0_, f32[512,768]{1,0:T(8,128)} %get-tuple-element.206.refs_1_, ...), custom_call_target="tpu_custom_call" | custom-call | flops 2184999993344 | tf_op jit(solution)/shard_map/forward_back/pallas_call | solution.py:254
  324.8 5.9 %merge_core.6 = (bf16[2,192,1536]{2,1,0:T(8,128)(2,1)}, bf16[2,192,1536]{2,1,0:T(8,128)(2,1)S(1)}, bf16[2,192,1536]{2,1,0:T(8,128)(2,1)}, bf16[2,192,1536]{2,1,0:T(8,128)(2,1)S(1)}, f32[8,128]{1,0:T(8,128)S(1)}) custom-call(bf16[2,2,2,192,1536]{4,3,2,1,0:T(8,128)(2,1)S(1)} %bitcast.141, bf16[2,2,2,192,1536]{4,3,2,1,0:T(8,128)(2,1)} %bitcast.46.refs_1_, ...), custom_call_target="tpu_custom_call" | custom-call | flops 230000001024 | tf_op jit(solution)/shard_map/merge_core/pallas_call | solution.py:600
  332.8 22.5 %attend_back.3 = (bf16[2,896,768]{2,1,0:T(8,128)(2,1)}, bf16[2,896,768]{2,1,0:T(8,128)(2,1)}, f32[512,768]{1,0:T(8,128)}, f32[8,128]{1,0:T(8,128)}) custom-call(s32[12]{0:T(128)} %pad_add_fusion.refs_0_, bf16[512,768]{1,0:T(8,128)(2,1)} %copy-done.16, f32[512,768]{1,0:T(8,128)} %get-tuple-element.245.refs_2_, ...), custom_call_target="tpu_custom_call" | custom-call | flops 2529999978496 | tf_op jit(solution)/shard_map/attend_back/pallas_call | solution.py:254
  383.4 14.2 %collective-permute-done.43.refs_1_ = bf16[2,224,768]{2,1,0:T(8,128)(2,1)} collective-permute-done((bf16[2,224,768]{2,1,0:T(8,128)(2,1)}, bf16[2,224,768]{2,1,0:T(8,128)(2,1)}, u32[]{:S(2)}, u32[]{:S(2)}) %collective-permute-start.43) | collective-permute-done | bytes 688160 | tf_op jit(solution)/shard_map/ppermute | solution.py:642
  415.9 4.7 %collective-permute-done.46.refs_1_ = bf16[192,1536]{1,0:T(8,128)(2,1)} collective-permute-done((bf16[192,1536]{1,0:T(8,128)(2,1)}, bf16[192,1536]{1,0:T(8,128)(2,1)}, u32[]{:S(2)}, u32[]{:S(2)}) %collective-permute-start.46) | collective-permute-done | bytes 589856 | tf_op jit(solution)/shard_map/ppermute | solution.py:642
  433.0 8.6 %collective-permute-done.52 = bf16[112,768]{1,0:T(8,128)(2,1)S(1)} collective-permute-done((bf16[112,768]{1,0:T(8,128)(2,1)S(1)}, bf16[112,768]{1,0:T(8,128)(2,1)S(1)}, u32[]{:S(2)}, u32[]{:S(2)}) %collective-permute-start.52) | collective-permute-done | bytes 172064 | tf_op jit(solution)/shard_map/ppermute | solution.py:642
  (349 shorter events, 165.6 us)
Async XLA Ops:
  7.2 178.0 %all-gather.2.cloned.1.call-start = ((), (), s32[]{:S(2)}) async-start(), calls=%async_computation | async-start | bytes 14598144 | tf_op jit(solution)/shard_map/all_gather | solution.py:807
  76.9 24.4 %collective-permute-start.10 = (bf16[896,768]{1,0:T(8,128)(2,1)S(1)}, bf16[896,768]{1,0:T(8,128)(2,1)}, u32[]{:S(2)}, u32[]{:S(2)}) collective-permute-start(bf16[896,768]{1,0:T(8,128)(2,1)S(1)} %get-tuple-element.162.refs_9_.refs_8_), channel_id=1, source_target_pairs={{0,1},{1,0},{2,3},{3,2},{4,5},{5,4},{6,7},{7,6},{8,9},{9,8},{10,11... | collective-permute-start | bytes 4128776 | tf_op jit(solution)/shard_map/ppermute | solution.py:642
  77.0 25.2 %collective-permute-start.11 = (bf16[896,768]{1,0:T(8,128)(2,1)S(1)}, bf16[896,768]{1,0:T(8,128)(2,1)}, u32[]{:S(2)}, u32[]{:S(2)}) collective-permute-start(bf16[896,768]{1,0:T(8,128)(2,1)S(1)} %get-tuple-element.163.refs_10_.refs_9_), channel_id=1, source_target_pairs={{0,1},{1,0},{2,3},{3,2},{4,5},{5,4},{6,7},{7,6},{8,9},{9,8},{10,11... | collective-permute-start | bytes 4128776 | tf_op jit(solution)/shard_map/ppermute | solution.py:642
  87.4 35.8 %collective-permute-start.13 = (bf16[384,768]{1,0:T(8,128)(2,1)S(1)}, bf16[384,768]{1,0:T(8,128)(2,1)}, u32[]{:S(2)}, u32[]{:S(2)}) collective-permute-start(bf16[384,768]{1,0:T(8,128)(2,1)S(1)} %get-tuple-element.167.refs_0_), channel_id=1, source_target_pairs={{0,4},{4,0},{8,12},{12,8},{16,20},{20,16},{24,28},{28,24},{1,5},{5... | collective-permute-start | bytes 1769480 | tf_op jit(solution)/shard_map/ppermute | solution.py:642
  89.3 33.9 %collective-permute-start.14 = (bf16[384,768]{1,0:T(8,128)(2,1)S(1)}, bf16[384,768]{1,0:T(8,128)(2,1)}, u32[]{:S(2)}, u32[]{:S(2)}) collective-permute-start(bf16[384,768]{1,0:T(8,128)(2,1)S(1)} %get-tuple-element.167.refs_0_), channel_id=1, source_target_pairs={{0,2},{1,3},{2,0},{3,1},{4,6},{5,7},{6,4},{7,5},{8,10},{9,11},{10,... | collective-permute-start | bytes 1769480 | tf_op jit(solution)/shard_map/ppermute | solution.py:642
  126.3 27.6 %collective-permute-start.20 = (bf16[384,768]{1,0:T(8,128)(2,1)S(1)}, bf16[384,768]{1,0:T(8,128)(2,1)S(1)}, u32[]{:S(2)}, u32[]{:S(2)}) collective-permute-start(bf16[384,768]{1,0:T(8,128)(2,1)S(1)} %get-tuple-element.176.refs_0_), channel_id=1, source_target_pairs={{0,4},{4,0},{8,12},{12,8},{16,20},{20,16},{24,28},{28,24},{1,5},{5... | collective-permute-start | bytes 1769480 | tf_op jit(solution)/shard_map/ppermute | solution.py:642
  128.2 25.6 %collective-permute-start.21 = (bf16[384,768]{1,0:T(8,128)(2,1)S(1)}, bf16[384,768]{1,0:T(8,128)(2,1)S(1)}, u32[]{:S(2)}, u32[]{:S(2)}) collective-permute-start(bf16[384,768]{1,0:T(8,128)(2,1)S(1)} %get-tuple-element.176.refs_0_), channel_id=1, source_target_pairs={{0,2},{1,3},{2,0},{3,1},{4,6},{5,7},{6,4},{7,5},{8,10},{9,11},{10,... | collective-permute-start | bytes 1769480 | tf_op jit(solution)/shard_map/ppermute | solution.py:642
  254.5 28.3 %collective-permute-start.28 = (bf16[2,192,1536]{2,1,0:T(8,128)(2,1)}, bf16[2,192,1536]{2,1,0:T(8,128)(2,1)}, u32[]{:S(2)}, u32[]{:S(2)}) collective-permute-start(bf16[2,192,1536]{2,1,0:T(8,128)(2,1)} %get-tuple-element.216), channel_id=1, source_target_pairs={{0,2},{1,3},{2,0},{3,1},{4,6},{5,7},{6,4},{7,5},{8,10},{9,11},{10,... | collective-permute-start | bytes 3538952 | tf_op jit(solution)/shard_map/ppermute | solution.py:642
  255.0 28.0 %collective-permute-start.29 = (bf16[2,192,1536]{2,1,0:T(8,128)(2,1)}, bf16[2,192,1536]{2,1,0:T(8,128)(2,1)}, u32[]{:S(2)}, u32[]{:S(2)}) collective-permute-start(bf16[2,192,1536]{2,1,0:T(8,128)(2,1)} %get-tuple-element.218), channel_id=1, source_target_pairs={{0,4},{4,0},{8,12},{12,8},{16,20},{20,16},{24,28},{28,24},{1,5},{5... | collective-permute-start | bytes 3538952 | tf_op jit(solution)/shard_map/ppermute | solution.py:642
  287.6 27.4 %collective-permute-start.33 = (bf16[192,1536]{1,0:T(8,128)(2,1)}, bf16[192,1536]{1,0:T(8,128)(2,1)}, u32[]{:S(2)}, u32[]{:S(2)}) collective-permute-start(bf16[192,1536]{1,0:T(8,128)(2,1)} %get-tuple-element.229), channel_id=1, source_target_pairs={{0,4},{4,0},{8,12},{12,8},{16,20},{20,16},{24,28},{28,24},{1,5},{5... | collective-permute-start | bytes 1769480 | tf_op jit(solution)/shard_map/ppermute | solution.py:642
  289.1 26.0 %collective-permute-start.34 = (bf16[192,1536]{1,0:T(8,128)(2,1)}, bf16[192,1536]{1,0:T(8,128)(2,1)}, u32[]{:S(2)}, u32[]{:S(2)}) collective-permute-start(bf16[192,1536]{1,0:T(8,128)(2,1)} %get-tuple-element.231), channel_id=1, source_target_pairs={{0,2},{1,3},{2,0},{3,1},{4,6},{5,7},{6,4},{7,5},{8,10},{9,11},{10,... | collective-permute-start | bytes 1769480 | tf_op jit(solution)/shard_map/ppermute | solution.py:642
  293.7 26.6 %collective-permute-start.31 = (bf16[2,224,768]{2,1,0:T(8,128)(2,1)}, bf16[2,224,768]{2,1,0:T(8,128)(2,1)}, u32[]{:S(2)}, u32[]{:S(2)}) collective-permute-start(bf16[2,224,768]{2,1,0:T(8,128)(2,1)} %get-tuple-element.225), channel_id=1, source_target_pairs={{0,2},{1,3},{2,0},{3,1},{4,6},{5,7},{6,4},{7,5},{8,10},{9,11},{10,... | collective-permute-start | bytes 2064392 | tf_op jit(solution)/shard_map/ppermute | solution.py:642
  295.1 25.2 %collective-permute-start.32 = (bf16[2,224,768]{2,1,0:T(8,128)(2,1)}, bf16[2,224,768]{2,1,0:T(8,128)(2,1)}, u32[]{:S(2)}, u32[]{:S(2)}) collective-permute-start(bf16[2,224,768]{2,1,0:T(8,128)(2,1)} %get-tuple-element.227), channel_id=1, source_target_pairs={{0,4},{4,0},{8,12},{12,8},{16,20},{20,16},{24,28},{28,24},{1,5},{5... | collective-permute-start | bytes 2064392 | tf_op jit(solution)/shard_map/ppermute | solution.py:642
  318.8 36.6 %collective-permute-start.39 = (bf16[192,1536]{1,0:T(8,128)(2,1)}, bf16[192,1536]{1,0:T(8,128)(2,1)}, u32[]{:S(2)}, u32[]{:S(2)}) collective-permute-start(bf16[192,1536]{1,0:T(8,128)(2,1)} %get-tuple-element.244), channel_id=1, source_target_pairs={{0,8},{4,12},{8,0},{12,4},{16,24},{20,28},{24,16},{28,20},{1,9},{5... | collective-permute-start | bytes 1769480 | tf_op jit(solution)/shard_map/ppermute | solution.py:642
  322.7 35.4 %collective-permute-start.37 = (bf16[224,768]{1,0:T(8,128)(2,1)}, bf16[224,768]{1,0:T(8,128)(2,1)}, u32[]{:S(2)}, u32[]{:S(2)}) collective-permute-start(bf16[224,768]{1,0:T(8,128)(2,1)} %get-tuple-element.240), channel_id=1, source_target_pairs={{0,4},{4,0},{8,12},{12,8},{16,20},{20,16},{24,28},{28,24},{1,5},{5... | collective-permute-start | bytes 1032200 | tf_op jit(solution)/shard_map/ppermute | solution.py:642
  324.2 33.9 %collective-permute-start.38 = (bf16[224,768]{1,0:T(8,128)(2,1)}, bf16[224,768]{1,0:T(8,128)(2,1)}, u32[]{:S(2)}, u32[]{:S(2)}) collective-permute-start(bf16[224,768]{1,0:T(8,128)(2,1)} %get-tuple-element.242), channel_id=1, source_target_pairs={{0,2},{1,3},{2,0},{3,1},{4,6},{5,7},{6,4},{7,5},{8,10},{9,11},{10,... | collective-permute-start | bytes 1032200 | tf_op jit(solution)/shard_map/ppermute | solution.py:642
  330.7 32.2 %collective-permute-start.35 = (bf16[2,192,1536]{2,1,0:T(8,128)(2,1)}, bf16[2,192,1536]{2,1,0:T(8,128)(2,1)}, u32[]{:S(2)}, u32[]{:S(2)}) collective-permute-start(bf16[2,192,1536]{2,1,0:T(8,128)(2,1)} %get-tuple-element.236), channel_id=1, source_target_pairs={{0,2},{1,3},{2,0},{3,1},{4,6},{5,7},{6,4},{7,5},{8,10},{9,11},{10,... | collective-permute-start | bytes 3538952 | tf_op jit(solution)/shard_map/ppermute | solution.py:642
  332.3 30.7 %collective-permute-start.36 = (bf16[2,192,1536]{2,1,0:T(8,128)(2,1)}, bf16[2,192,1536]{2,1,0:T(8,128)(2,1)}, u32[]{:S(2)}, u32[]{:S(2)}) collective-permute-start(bf16[2,192,1536]{2,1,0:T(8,128)(2,1)} %get-tuple-element.238), channel_id=1, source_target_pairs={{0,4},{4,0},{8,12},{12,8},{16,20},{20,16},{24,28},{28,24},{1,5},{5... | collective-permute-start | bytes 3538952 | tf_op jit(solution)/shard_map/ppermute | solution.py:642
  366.0 35.6 %collective-permute-start.40 = (bf16[192,1536]{1,0:T(8,128)(2,1)}, bf16[192,1536]{1,0:T(8,128)(2,1)}, u32[]{:S(2)}, u32[]{:S(2)}) collective-permute-start(bf16[192,1536]{1,0:T(8,128)(2,1)} %get-tuple-element.257), channel_id=1, source_target_pairs={{0,4},{4,0},{8,12},{12,8},{16,20},{20,16},{24,28},{28,24},{1,5},{5... | collective-permute-start | bytes 1769480 | tf_op jit(solution)/shard_map/ppermute | solution.py:642
  367.6 34.1 %collective-permute-start.41 = (bf16[192,1536]{1,0:T(8,128)(2,1)}, bf16[192,1536]{1,0:T(8,128)(2,1)}, u32[]{:S(2)}, u32[]{:S(2)}) collective-permute-start(bf16[192,1536]{1,0:T(8,128)(2,1)} %get-tuple-element.259), channel_id=1, source_target_pairs={{0,2},{1,3},{2,0},{3,1},{4,6},{5,7},{6,4},{7,5},{8,10},{9,11},{10,... | collective-permute-start | bytes 1769480 | tf_op jit(solution)/shard_map/ppermute | solution.py:642
  372.0 25.5 %collective-permute-start.43 = (bf16[2,224,768]{2,1,0:T(8,128)(2,1)}, bf16[2,224,768]{2,1,0:T(8,128)(2,1)}, u32[]{:S(2)}, u32[]{:S(2)}) collective-permute-start(bf16[2,224,768]{2,1,0:T(8,128)(2,1)} %get-tuple-element.264), channel_id=1, source_target_pairs={{0,2},{1,3},{2,0},{3,1},{4,6},{5,7},{6,4},{7,5},{8,10},{9,11},{10,... | collective-permute-start | bytes 2064392 | tf_op jit(solution)/shard_map/ppermute | solution.py:642
  380.8 32.1 %collective-permute-start.53 = (bf16[112,768]{1,0:T(8,128)(2,1)}, bf16[112,768]{1,0:T(8,128)(2,1)}, u32[]{:S(2)}, u32[]{:S(2)}) collective-permute-start(bf16[112,768]{1,0:T(8,128)(2,1)} %get-tuple-element.288), channel_id=1, source_target_pairs={{0,16},{4,20},{8,24},{12,28},{16,0},{20,4},{24,8},{28,12},{1,17},{... | collective-permute-start | bytes 516104 | tf_op jit(solution)/shard_map/ppermute | solution.py:642
  422.5 25.0 %collective-permute-start.54 = (bf16[96,1536]{1,0:T(8,128)(2,1)}, bf16[96,1536]{1,0:T(8,128)(2,1)}, u32[]{:S(2)}, u32[]{:S(2)}) collective-permute-start(bf16[96,1536]{1,0:T(8,128)(2,1)} %get-tuple-element.290), channel_id=1, source_target_pairs={{0,16},{4,20},{8,24},{12,28},{16,0},{20,4},{24,8},{28,12},{1,17},{... | collective-permute-start | bytes 884744 | tf_op jit(solution)/shard_map/ppermute | solution.py:642
  425.6 25.5 %collective-permute-start.49 = (f32[256,768]{1,0:T(8,128)}, f32[256,768]{1,0:T(8,128)}, u32[]{:S(2)}, u32[]{:S(2)}) collective-permute-start(f32[256,768]{1,0:T(8,128)} %constant_dynamic-slice_fusion.3), channel_id=1, source_target_pairs={{0,1},{1,0},{2,3},{3,2},{4,5},{5,4},{6,7},{7,6},{8,9},{9,8},{10,11... | collective-permute-start | bytes 2359304 | tf_op jit(solution)/shard_map/ppermute | solution.py:642
  (87 other events, 745.9 us)
Sparse Core Ops, SparseCore 0:
  38.7 115.1 all-gather.1
